TPU v7x, 512 devices: a whole 4x8x8 slice. The times are simulated.
512 devices in a mesh: gx: 16 (over y, core), gy: 8 (over x, z_hi), view: 4 (over z_lo).
Axes of the slice: x: 4, y: 8, z: 8 (z_hi: 2, z_lo: 4; z = z_hi * 4 + z_lo), core: 2. Of those that a mesh axis runs over, the one named last changes fastest.
Arguments:
- estimate: float32 [512, 512, 128], P('gx', 'gy'), may hold values from 0.5 to 2
- views_data: bfloat16 [4, 512, 512, 128], P('view', 'gx', 'gy'), may hold values from 0.19921875 to 3
- spread_x: float32 [4, 33], P('view'), may hold values from 0.05 to 1
- spread_y: float32 [4, 33], P('view'), may hold values from 0.05 to 1
- spread_z: float32 [4, 33], P('view'), may hold values from 0.05 to 1
Outputs:
- deconvolved: float32 [512, 512, 128], P(('gx', 'view'), 'gy')
All inputs are finite; a program needn't handle non-finite values.
Results may differ from a plain program's by a relative error of at most 0.0003.
Values sent between devices are 32-bit elements; how exact they have to be, the bound alone decides.
No kernel may reach another device: no remote copies, remote signals or barrier semaphores. Data moves between devices by JAX's collectives and lax.ppermute only.
A program may use at most 64 MiB of HBM per device.

v0:
```python
import jax
import jax.numpy as jnp
from jax import lax
from jax.sharding import PartitionSpec as P

ITERS = 2


def extended(shard, sides, width):
    for axis, dim in sides:
        size, length = (lax.axis_size(axis), shard.shape[dim])
        up = [(i, (i + 1) % size) for i in range(size - 1)]
        down = [(j, i) for i, j in up]
        last = lax.slice_in_dim(shard, length - width, length, axis=dim)
        leading = lax.slice_in_dim(shard, 0, width, axis=dim)
        before = lax.ppermute(last, axis, up)
        after = lax.ppermute(leading, axis, down)
        shard = jnp.concatenate([before, shard, after], axis=dim)
    return shard


def band_matrix(weights, length, adjoint):
    taps_total = weights.shape[0]
    half_width = (taps_total - 1) // 2
    shape_pair = (length, length + 2 * half_width)
    out_index = lax.broadcasted_iota(jnp.int32, shape_pair, 0)
    in_index = lax.broadcasted_iota(jnp.int32, shape_pair, 1)
    if adjoint:
        offset = in_index - out_index
    else:
        offset = out_index - in_index + 2 * half_width
    matrix = jnp.zeros(shape_pair, jnp.float32)
    for tap_number in range(taps_total):
        matrix = matrix + jnp.where(offset == tap_number, weights[tap_number], 0.0)
    return matrix


def along_rows(matrix, volume):
    return jnp.einsum("im,myz->iyz", matrix, volume, precision=lax.Precision.HIGHEST)


def along_columns(matrix, volume):
    return jnp.einsum("jm,imz->ijz", matrix, volume, precision=lax.Precision.HIGHEST)


def along_depth(matrix, volume, half_width):
    padded = jnp.pad(volume, ((0, 0), (0, 0), (half_width, half_width)))
    pieces = jnp.einsum("xym,zm->xyz", padded, matrix, precision=lax.Precision.HIGHEST)
    return pieces


def body(estimate, views_data, spread_x, spread_y, spread_z):
    tile_x, tile_y, depth_cells = estimate.shape
    half_width = (spread_x.shape[1] - 1) // 2
    views_total = views_data.shape[0] * lax.axis_size("view")
    block_cells = 128
    kernel_x = spread_x[0] / jnp.sum(spread_x[0])
    kernel_y = spread_y[0] / jnp.sum(spread_y[0])
    kernel_z = spread_z[0] / jnp.sum(spread_z[0])
    forward_x = band_matrix(kernel_x, tile_x, False)
    forward_y = band_matrix(kernel_y, tile_y, False)
    forward_z = band_matrix(kernel_z, block_cells, False)
    adjoint_x = band_matrix(kernel_x, tile_x, True)
    adjoint_y = band_matrix(kernel_y, tile_y, True)
    adjoint_z = band_matrix(kernel_z, block_cells, True)
    measured = views_data[0].astype(jnp.float32)
    share_rows = tile_x // lax.axis_size("view")
    first_row = lax.axis_index("view") * share_rows
    for step_number in range(ITERS):
        last_step = step_number + 1 == ITERS
        padded = extended(estimate, (("gx", 0), ("gy", 1)), half_width)
        along_y = along_columns(forward_y, along_rows(forward_x, padded))
        blurred = along_depth(forward_z, along_y, half_width)
        ratios = measured / blurred
        ratio_padded = extended(ratios, (("gx", 0), ("gy", 1)), half_width)
        back_y = along_columns(adjoint_y, along_rows(adjoint_x, ratio_padded))
        back_field = along_depth(adjoint_z, back_y, half_width)
        log_terms = jnp.log(back_field)
        total_logs = lax.psum(log_terms, "view")
        estimate = estimate * jnp.exp(total_logs / views_total)
        if last_step:
            estimate = lax.dynamic_slice_in_dim(estimate, first_row, share_rows, 0)
    return estimate


def solution(mesh):
    in_specs = (
        P("gx", "gy", None),
        P("view", "gx", "gy", None),
        P("view", None),
        P("view", None),
        P("view", None),
    )
    out_specs = P(("gx", "view"), "gy", None)
    return jax.shard_map(body, mesh=mesh, in_specs=in_specs, out_specs=out_specs, check_vma=False)
```

profile of v0, /device:TPU:1, one launch (start us, length us, event | category | flops | bytes accessed | tf_op | source)
XLA Modules:
  0.0 705.0 jit_solution(8336264688812745479)
XLA Ops:
  26.7 7.1 %collective-permute-start.2 = (f32[64,16,128]{2,1,0:T(8,128)S(1)}, f32[64,16,128]{2,1,0:T(8,128)S(1)}, u32[]{:S(2)}, u32[]{:S(2)}) collective-permute-start(f32[64,16,128]{2,1,0:T(8,128)S(1)} %get-tuple-element.11), channel_id=1, source_target_pairs={{0,4},{4,8},{8,12},{12,16},{16,20},{20,24},{24,28},{1,5},{5,9},{9,... | collective-permute-start | bytes 1572872 | tf_op jit(solution)/shard_map/ppermute | solution.py:16
  44.1 22.7 %collective-permute-done.3 = f32[64,16,128]{2,1,0:T(8,128)S(1)} collective-permute-done((f32[64,16,128]{2,1,0:T(8,128)S(1)}, f32[64,16,128]{2,1,0:T(8,128)S(1)}, u32[]{:S(2)}, u32[]{:S(2)}) %collective-permute-start.3) | collective-permute-done | bytes 524320 | tf_op jit(solution)/shard_map/ppermute | solution.py:17
  67.1 23.8 %fusion.6 = f32[32,96,128]{2,0,1:T(8,128)S(1)} fusion(f32[64,96,128]{2,1,0:T(8,128)S(1)} %pad_maximum_fusion, f32[]{:T(128)} %bitcast.32, f32[]{:T(128)} %bitcast.31, f32[]{:T(128)} %bitcast.30, f32[]{:T(128)} %bitcast.29, f32[]{:T(128)} %bitcast.28, f32[]{:T(128)} %bitcast.27, f32[]{:T(128)} %bitcast.26, f32[]{:T(128)} %bitcast.25, f32[]{:T(128)} %bitcast.24, ...), kind=kOutput, calls=%fused_computation.10 | convolution fusion | flops 302194688 | bytes 4718724 | tf_op jit(solution)/shard_map/im,myz->iyz/dot_general | solution.py:39
  90.9 22.5 %fusion.36 = f32[32,64,128]{2,1,0:T(8,128)S(1)} fusion(f32[32,96,128]{2,0,1:T(8,128)S(1)} %fusion.6, f32[]{:T(128)} %bitcast.68, f32[]{:T(128)} %bitcast.67, f32[]{:T(128)} %bitcast.66, f32[]{:T(128)} %bitcast.65, f32[]{:T(128)} %bitcast.64, f32[]{:T(128)} %bitcast.63, f32[]{:T(128)} %bitcast.62, f32[]{:T(128)} %bitcast.61, f32[]{:T(128)} %bitcast.60, ...), kind=kOutput, calls=%fused_computation.32 | convolution fusion | flops 302604288 | bytes 2621572 | tf_op jit(solution)/shard_map/jm,imz->ijz/dot_general | solution.py:43
  113.4 22.9 %fusion.24 = f32[32,64,128]{2,1,0:T(8,128)S(1)} fusion(f32[32,64,128]{2,1,0:T(8,128)S(1)} %fusion.36, bf16[1,32,64,128]{3,2,1,0:T(8,128)(2,1)S(1)} %copy-done.1, f32[]{:T(128)} %bitcast.103, f32[]{:T(128)} %bitcast.102, f32[]{:T(128)} %bitcast.101, f32[]{:T(128)} %bitcast.100, f32[]{:T(128)} %bitcast.99, f32[]{:T(128)} %bitcast.98, f32[]{:T(128)} %bitcast.97, ...), kind=kOutput, calls=%fused_computation.28 | convolution fusion | flops 505888768 | bytes 2621572 | tf_op jit(solution)/shard_map/xym,zm->xyz/dot_general | solution.py:48
  152.5 19.3 %collective-permute-start.6 = (f32[64,16,128]{2,1,0:T(8,128)S(1)}, f32[64,16,128]{2,1,0:T(8,128)S(1)}, u32[]{:S(2)}, u32[]{:S(2)}) collective-permute-start(f32[64,16,128]{2,1,0:T(8,128)S(1)} %get-tuple-element.9), channel_id=1, source_target_pairs={{0,4},{4,8},{8,12},{12,16},{16,20},{20,24},{24,28},{1,5},{5,9},{9,... | collective-permute-start | bytes 1572872 | tf_op jit(solution)/shard_map/ppermute | solution.py:16
  179.1 21.6 %collective-permute-done.7 = f32[64,16,128]{2,1,0:T(8,128)S(1)} collective-permute-done((f32[64,16,128]{2,1,0:T(8,128)S(1)}, f32[64,16,128]{2,1,0:T(8,128)S(1)}, u32[]{:S(2)}, u32[]{:S(2)}) %collective-permute-start.7) | collective-permute-done | bytes 524320 | tf_op jit(solution)/shard_map/ppermute | solution.py:17
  201.0 23.8 %fusion.4 = f32[32,96,128]{2,0,1:T(8,128)S(1)} fusion(f32[64,96,128]{2,1,0:T(8,128)S(1)} %pad_maximum_fusion.1, f32[]{:T(128)} %bitcast.32, f32[]{:T(128)} %bitcast.31, f32[]{:T(128)} %bitcast.30, f32[]{:T(128)} %bitcast.29, f32[]{:T(128)} %bitcast.28, f32[]{:T(128)} %bitcast.27, f32[]{:T(128)} %bitcast.26, f32[]{:T(128)} %bitcast.25, f32[]{:T(128)} %bitcast.24, ...), kind=kOutput, calls=%fused_computation.8 | convolution fusion | flops 302192640 | bytes 4718724 | tf_op jit(solution)/shard_map/im,myz->iyz/dot_general | solution.py:39
  224.8 22.4 %fusion.39 = f32[32,64,128]{2,1,0:T(8,128)S(1)} fusion(f32[32,96,128]{2,0,1:T(8,128)S(1)} %fusion.4, f32[]{:T(128)} %bitcast.68, f32[]{:T(128)} %bitcast.67, f32[]{:T(128)} %bitcast.66, f32[]{:T(128)} %bitcast.65, f32[]{:T(128)} %bitcast.64, f32[]{:T(128)} %bitcast.63, f32[]{:T(128)} %bitcast.62, f32[]{:T(128)} %bitcast.61, f32[]{:T(128)} %bitcast.60, ...), kind=kOutput, calls=%fused_computation.33 | convolution fusion | flops 302598144 | bytes 2621572 | tf_op jit(solution)/shard_map/jm,imz->ijz/dot_general | solution.py:43
  247.2 23.7 %fusion.27 = f32[32,64,128]{2,1,0:T(8,128)} fusion(f32[32,64,128]{2,1,0:T(8,128)S(1)} %fusion.39, f32[]{:T(128)} %bitcast.103, f32[]{:T(128)} %bitcast.102, f32[]{:T(128)} %bitcast.101, f32[]{:T(128)} %bitcast.100, f32[]{:T(128)} %bitcast.99, f32[]{:T(128)} %bitcast.98, f32[]{:T(128)} %bitcast.97, f32[]{:T(128)} %bitcast.96, f32[]{:T(128)} %bitcast.95, ...), kind=kOutput, calls=%fused_computation.29 | convolution fusion | flops 505344000 | bytes 2097284 | tf_op jit(solution)/shard_map/xym,zm->xyz/dot_general | solution.py:48
  271.0 84.7 %all-reduce.7.cloned.1.call-done = f32[32,64,128]{2,1,0:T(8,128)} async-done(((f32[32,64,128]{2,1,0:T(8,128)}), f32[32,64,128]{2,1,0:T(8,128)}) %all-reduce.7.cloned.1.call-update) | async-done | bytes 1048592 | tf_op jit(solution)/shard_map/psum | solution.py:79
  378.5 16.8 %collective-permute-done.10 = f32[64,16,128]{2,1,0:T(8,128)S(1)} collective-permute-done((f32[64,16,128]{2,1,0:T(8,128)S(1)}, f32[64,16,128]{2,1,0:T(8,128)S(1)}, u32[]{:S(2)}, u32[]{:S(2)}) %collective-permute-start.10) | collective-permute-done | bytes 524320 | tf_op jit(solution)/shard_map/ppermute | solution.py:16
  395.4 13.2 %collective-permute-done.11 = f32[64,16,128]{2,1,0:T(8,128)S(1)} collective-permute-done((f32[64,16,128]{2,1,0:T(8,128)S(1)}, f32[64,16,128]{2,1,0:T(8,128)S(1)}, u32[]{:S(2)}, u32[]{:S(2)}) %collective-permute-start.11) | collective-permute-done | bytes 524320 | tf_op jit(solution)/shard_map/ppermute | solution.py:17
  408.9 23.8 %fusion.2 = f32[32,96,128]{2,0,1:T(8,128)S(1)} fusion(f32[64,96,128]{2,1,0:T(8,128)S(1)} %pad_maximum_fusion.2, f32[]{:T(128)} %bitcast.32, f32[]{:T(128)} %bitcast.31, f32[]{:T(128)} %bitcast.30, f32[]{:T(128)} %bitcast.29, f32[]{:T(128)} %bitcast.28, f32[]{:T(128)} %bitcast.27, f32[]{:T(128)} %bitcast.26, f32[]{:T(128)} %bitcast.25, f32[]{:T(128)} %bitcast.24, ...), kind=kOutput, calls=%fused_computation.6 | convolution fusion | flops 302194688 | bytes 4718724 | tf_op jit(solution)/shard_map/im,myz->iyz/dot_general | solution.py:39
  432.7 22.5 %fusion.42 = f32[32,64,128]{2,1,0:T(8,128)S(1)} fusion(f32[32,96,128]{2,0,1:T(8,128)S(1)} %fusion.2, f32[]{:T(128)} %bitcast.68, f32[]{:T(128)} %bitcast.67, f32[]{:T(128)} %bitcast.66, f32[]{:T(128)} %bitcast.65, f32[]{:T(128)} %bitcast.64, f32[]{:T(128)} %bitcast.63, f32[]{:T(128)} %bitcast.62, f32[]{:T(128)} %bitcast.61, f32[]{:T(128)} %bitcast.60, ...), kind=kOutput, calls=%fused_computation.34 | convolution fusion | flops 302604288 | bytes 2621572 | tf_op jit(solution)/shard_map/jm,imz->ijz/dot_general | solution.py:43
  455.1 22.9 %fusion.30 = f32[32,64,128]{2,1,0:T(8,128)S(1)} fusion(f32[32,64,128]{2,1,0:T(8,128)S(1)} %fusion.42, bf16[1,32,64,128]{3,2,1,0:T(8,128)(2,1)S(1)} %copy-done.1, f32[]{:T(128)} %bitcast.103, f32[]{:T(128)} %bitcast.102, f32[]{:T(128)} %bitcast.101, f32[]{:T(128)} %bitcast.100, f32[]{:T(128)} %bitcast.99, f32[]{:T(128)} %bitcast.98, f32[]{:T(128)} %bitcast.97, ...), kind=kOutput, calls=%fused_computation.30 | convolution fusion | flops 505888768 | bytes 2621572 | tf_op jit(solution)/shard_map/xym,zm->xyz/dot_general | solution.py:48
  478.1 8.4 %collective-permute-start.12 = (f32[16,64,128]{2,1,0:T(8,128)S(1)}, f32[16,64,128]{2,1,0:T(8,128)S(1)}, u32[]{:S(2)}, u32[]{:S(2)}) collective-permute-start(f32[16,64,128]{2,1,0:T(8,128)S(1)} %get-tuple-element.13), channel_id=1, source_target_pairs={{0,32},{32,64},{64,96},{96,128},{128,160},{160,192},{192,224},{224... | collective-permute-start | bytes 1572872 | tf_op jit(solution)/shard_map/ppermute | solution.py:16
  497.1 16.4 %collective-permute-start.14 = (f32[64,16,128]{2,1,0:T(8,128)S(1)}, f32[64,16,128]{2,1,0:T(8,128)S(1)}, u32[]{:S(2)}, u32[]{:S(2)}) collective-permute-start(f32[64,16,128]{2,1,0:T(8,128)S(1)} %get-tuple-element.5), channel_id=1, source_target_pairs={{0,4},{4,8},{8,12},{12,16},{16,20},{20,24},{24,28},{1,5},{5,9},{9,... | collective-permute-start | bytes 1572872 | tf_op jit(solution)/shard_map/ppermute | solution.py:16
  515.2 14.1 %collective-permute-done.14 = f32[64,16,128]{2,1,0:T(8,128)S(1)} collective-permute-done((f32[64,16,128]{2,1,0:T(8,128)S(1)}, f32[64,16,128]{2,1,0:T(8,128)S(1)}, u32[]{:S(2)}, u32[]{:S(2)}) %collective-permute-start.14) | collective-permute-done | bytes 524320 | tf_op jit(solution)/shard_map/ppermute | solution.py:16
  529.2 12.4 %collective-permute-done.15 = f32[64,16,128]{2,1,0:T(8,128)S(1)} collective-permute-done((f32[64,16,128]{2,1,0:T(8,128)S(1)}, f32[64,16,128]{2,1,0:T(8,128)S(1)}, u32[]{:S(2)}, u32[]{:S(2)}) %collective-permute-start.15) | collective-permute-done | bytes 524320 | tf_op jit(solution)/shard_map/ppermute | solution.py:17
  541.9 23.8 %fusion = f32[32,96,128]{2,0,1:T(8,128)S(1)} fusion(f32[64,96,128]{2,1,0:T(8,128)S(1)} %pad_maximum_fusion.3, f32[]{:T(128)} %bitcast.32, f32[]{:T(128)} %bitcast.31, f32[]{:T(128)} %bitcast.30, f32[]{:T(128)} %bitcast.29, f32[]{:T(128)} %bitcast.28, f32[]{:T(128)} %bitcast.27, f32[]{:T(128)} %bitcast.26, f32[]{:T(128)} %bitcast.25, f32[]{:T(128)} %bitcast.24, ...), kind=kOutput, calls=%fused_computation.4 | convolution fusion | flops 302192640 | bytes 4718724 | tf_op jit(solution)/shard_map/im,myz->iyz/dot_general | solution.py:39
  565.7 22.4 %fusion.45 = f32[32,64,128]{2,1,0:T(8,128)S(1)} fusion(f32[32,96,128]{2,0,1:T(8,128)S(1)} %fusion, f32[]{:T(128)} %bitcast.68, f32[]{:T(128)} %bitcast.67, f32[]{:T(128)} %bitcast.66, f32[]{:T(128)} %bitcast.65, f32[]{:T(128)} %bitcast.64, f32[]{:T(128)} %bitcast.63, f32[]{:T(128)} %bitcast.62, f32[]{:T(128)} %bitcast.61, f32[]{:T(128)} %bitcast.60, ...), kind=kOutput, calls=%fused_computation.35 | convolution fusion | flops 302598144 | bytes 2621572 | tf_op jit(solution)/shard_map/jm,imz->ijz/dot_general | solution.py:43
  588.1 23.8 %fusion.33 = f32[32,64,128]{2,1,0:T(8,128)} fusion(f32[32,64,128]{2,1,0:T(8,128)S(1)} %fusion.45, f32[]{:T(128)} %bitcast.103, f32[]{:T(128)} %bitcast.102, f32[]{:T(128)} %bitcast.101, f32[]{:T(128)} %bitcast.100, f32[]{:T(128)} %bitcast.99, f32[]{:T(128)} %bitcast.98, f32[]{:T(128)} %bitcast.97, f32[]{:T(128)} %bitcast.96, f32[]{:T(128)} %bitcast.95, ...), kind=kOutput, calls=%fused_computation.31 | convolution fusion | flops 505344000 | bytes 2097284 | tf_op jit(solution)/shard_map/xym,zm->xyz/dot_general | solution.py:48
  611.9 84.1 %all-reduce.9.cloned.1.call-done = f32[32,64,128]{2,1,0:T(8,128)} async-done(((f32[32,64,128]{2,1,0:T(8,128)}), f32[32,64,128]{2,1,0:T(8,128)}) %all-reduce.9.cloned.1.call-update) | async-done | bytes 1048592 | tf_op jit(solution)/shard_map/psum | solution.py:79
  (59 shorter events, 91.7 us)
Async XLA Ops:
  6.5 20.0 %copy-start = (f32[32,64,128]{2,1,0:T(8,128)S(1)}, f32[32,64,128]{2,1,0:T(8,128)}, u32[]{:S(2)}) copy-start(f32[32,64,128]{2,1,0:T(8,128)} %param.5) | copy-start | bytes 3145732
  6.5 349.2 %all-reduce.7.cloned.1.call-start = ((), (), s32[]{:S(2)}) async-start(), calls=%async_computation | async-start | bytes 2097152 | tf_op jit(solution)/shard_map/psum | solution.py:79
  7.9 18.5 %collective-permute-start = (f32[16,64,128]{2,1,0:T(8,128)S(1)}, f32[16,64,128]{2,1,0:T(8,128)S(1)}, u32[]{:S(2)}, u32[]{:S(2)}) collective-permute-start(f32[16,64,128]{2,1,0:T(8,128)S(1)} %get-tuple-element.20), channel_id=1, source_target_pairs={{0,32},{32,64},{64,96},{96,128},{128,160},{160,192},{192,224},{224... | collective-permute-start | bytes 1572872 | tf_op jit(solution)/shard_map/ppermute | solution.py:16
  12.5 14.1 %collective-permute-start.1 = (f32[16,64,128]{2,1,0:T(8,128)S(1)}, f32[16,64,128]{2,1,0:T(8,128)S(1)}, u32[]{:S(2)}, u32[]{:S(2)}) collective-permute-start(f32[16,64,128]{2,1,0:T(8,128)S(1)} %get-tuple-element.19), channel_id=1, source_target_pairs={{32,0},{64,32},{96,64},{128,96},{160,128},{192,160},{224,192},{256... | collective-permute-start | bytes 1572872 | tf_op jit(solution)/shard_map/ppermute | solution.py:17
  26.7 17.4 %collective-permute-start.2 = (f32[64,16,128]{2,1,0:T(8,128)S(1)}, f32[64,16,128]{2,1,0:T(8,128)S(1)}, u32[]{:S(2)}, u32[]{:S(2)}) collective-permute-start(f32[64,16,128]{2,1,0:T(8,128)S(1)} %get-tuple-element.11), channel_id=1, source_target_pairs={{0,4},{4,8},{8,12},{12,16},{16,20},{20,24},{24,28},{1,5},{5,9},{9,... | collective-permute-start | bytes 1572872 | tf_op jit(solution)/shard_map/ppermute | solution.py:16
  33.8 33.0 %collective-permute-start.3 = (f32[64,16,128]{2,1,0:T(8,128)S(1)}, f32[64,16,128]{2,1,0:T(8,128)S(1)}, u32[]{:S(2)}, u32[]{:S(2)}) collective-permute-start(f32[64,16,128]{2,1,0:T(8,128)S(1)} %get-tuple-element.12), channel_id=1, source_target_pairs={{4,0},{8,4},{12,8},{16,12},{20,16},{24,20},{28,24},{5,1},{9,5},{13... | collective-permute-start | bytes 1572872 | tf_op jit(solution)/shard_map/ppermute | solution.py:17
  67.1 46.3 %copy-start.1 = (bf16[1,32,64,128]{3,2,1,0:T(8,128)(2,1)S(1)}, bf16[1,32,64,128]{3,2,1,0:T(8,128)(2,1)}, u32[]{:S(2)}) copy-start(bf16[1,32,64,128]{3,2,1,0:T(8,128)(2,1)} %param.6) | copy-start | bytes 1572868
  136.4 11.7 %collective-permute-start.4 = (f32[16,64,128]{2,1,0:T(8,128)S(1)}, f32[16,64,128]{2,1,0:T(8,128)S(1)}, u32[]{:S(2)}, u32[]{:S(2)}) collective-permute-start(f32[16,64,128]{2,1,0:T(8,128)S(1)} %get-tuple-element.17), channel_id=1, source_target_pairs={{0,32},{32,64},{64,96},{96,128},{128,160},{160,192},{192,224},{224... | collective-permute-start | bytes 1572872 | tf_op jit(solution)/shard_map/ppermute | solution.py:16
  141.9 10.5 %collective-permute-start.5 = (f32[16,64,128]{2,1,0:T(8,128)S(1)}, f32[16,64,128]{2,1,0:T(8,128)S(1)}, u32[]{:S(2)}, u32[]{:S(2)}) collective-permute-start(f32[16,64,128]{2,1,0:T(8,128)S(1)} %get-tuple-element.18), channel_id=1, source_target_pairs={{32,0},{64,32},{96,64},{128,96},{160,128},{192,160},{224,192},{256... | collective-permute-start | bytes 1572872 | tf_op jit(solution)/shard_map/ppermute | solution.py:17
  152.5 26.6 %collective-permute-start.6 = (f32[64,16,128]{2,1,0:T(8,128)S(1)}, f32[64,16,128]{2,1,0:T(8,128)S(1)}, u32[]{:S(2)}, u32[]{:S(2)}) collective-permute-start(f32[64,16,128]{2,1,0:T(8,128)S(1)} %get-tuple-element.9), channel_id=1, source_target_pairs={{0,4},{4,8},{8,12},{12,16},{16,20},{20,24},{24,28},{1,5},{5,9},{9,... | collective-permute-start | bytes 1572872 | tf_op jit(solution)/shard_map/ppermute | solution.py:16
  171.8 28.9 %collective-permute-start.7 = (f32[64,16,128]{2,1,0:T(8,128)S(1)}, f32[64,16,128]{2,1,0:T(8,128)S(1)}, u32[]{:S(2)}, u32[]{:S(2)}) collective-permute-start(f32[64,16,128]{2,1,0:T(8,128)S(1)} %get-tuple-element.10), channel_id=1, source_target_pairs={{4,0},{8,4},{12,8},{16,12},{20,16},{24,20},{28,24},{5,1},{9,5},{13... | collective-permute-start | bytes 1572872 | tf_op jit(solution)/shard_map/ppermute | solution.py:17
  271.0 425.0 %all-reduce.9.cloned.1.call-start = ((), (), s32[]{:S(2)}) async-start(), calls=%async_computation.1 | async-start | bytes 2097152 | tf_op jit(solution)/shard_map/psum | solution.py:79
  357.3 10.0 %collective-permute-start.8 = (f32[16,64,128]{2,1,0:T(8,128)S(1)}, f32[16,64,128]{2,1,0:T(8,128)S(1)}, u32[]{:S(2)}, u32[]{:S(2)}) collective-permute-start(f32[16,64,128]{2,1,0:T(8,128)S(1)} %get-tuple-element.15), channel_id=1, source_target_pairs={{0,32},{32,64},{64,96},{96,128},{128,160},{160,192},{192,224},{224... | collective-permute-start | bytes 1572872 | tf_op jit(solution)/shard_map/ppermute | solution.py:16
  361.2 10.5 %collective-permute-start.9 = (f32[16,64,128]{2,1,0:T(8,128)S(1)}, f32[16,64,128]{2,1,0:T(8,128)S(1)}, u32[]{:S(2)}, u32[]{:S(2)}) collective-permute-start(f32[16,64,128]{2,1,0:T(8,128)S(1)} %get-tuple-element.16), channel_id=1, source_target_pairs={{32,0},{64,32},{96,64},{128,96},{160,128},{192,160},{224,192},{256... | collective-permute-start | bytes 1572872 | tf_op jit(solution)/shard_map/ppermute | solution.py:17
  371.8 23.6 %collective-permute-start.10 = (f32[64,16,128]{2,1,0:T(8,128)S(1)}, f32[64,16,128]{2,1,0:T(8,128)S(1)}, u32[]{:S(2)}, u32[]{:S(2)}) collective-permute-start(f32[64,16,128]{2,1,0:T(8,128)S(1)} %get-tuple-element.7), channel_id=1, source_target_pairs={{0,4},{4,8},{8,12},{12,16},{16,20},{20,24},{24,28},{1,5},{5,9},{9,... | collective-permute-start | bytes 1572872 | tf_op jit(solution)/shard_map/ppermute | solution.py:16
  377.0 31.5 %collective-permute-start.11 = (f32[64,16,128]{2,1,0:T(8,128)S(1)}, f32[64,16,128]{2,1,0:T(8,128)S(1)}, u32[]{:S(2)}, u32[]{:S(2)}) collective-permute-start(f32[64,16,128]{2,1,0:T(8,128)S(1)} %get-tuple-element.8), channel_id=1, source_target_pairs={{4,0},{8,4},{12,8},{16,12},{20,16},{24,20},{28,24},{5,1},{9,5},{13... | collective-permute-start | bytes 1572872 | tf_op jit(solution)/shard_map/ppermute | solution.py:17
  478.1 14.6 %collective-permute-start.12 = (f32[16,64,128]{2,1,0:T(8,128)S(1)}, f32[16,64,128]{2,1,0:T(8,128)S(1)}, u32[]{:S(2)}, u32[]{:S(2)}) collective-permute-start(f32[16,64,128]{2,1,0:T(8,128)S(1)} %get-tuple-element.13), channel_id=1, source_target_pairs={{0,32},{32,64},{64,96},{96,128},{128,160},{160,192},{192,224},{224... | collective-permute-start | bytes 1572872 | tf_op jit(solution)/shard_map/ppermute | solution.py:16
  486.6 10.5 %collective-permute-start.13 = (f32[16,64,128]{2,1,0:T(8,128)S(1)}, f32[16,64,128]{2,1,0:T(8,128)S(1)}, u32[]{:S(2)}, u32[]{:S(2)}) collective-permute-start(f32[16,64,128]{2,1,0:T(8,128)S(1)} %get-tuple-element.14), channel_id=1, source_target_pairs={{32,0},{64,32},{96,64},{128,96},{160,128},{192,160},{224,192},{256... | collective-permute-start | bytes 1572872 | tf_op jit(solution)/shard_map/ppermute | solution.py:17
  497.1 32.1 %collective-permute-start.14 = (f32[64,16,128]{2,1,0:T(8,128)S(1)}, f32[64,16,128]{2,1,0:T(8,128)S(1)}, u32[]{:S(2)}, u32[]{:S(2)}) collective-permute-start(f32[64,16,128]{2,1,0:T(8,128)S(1)} %get-tuple-element.5), channel_id=1, source_target_pairs={{0,4},{4,8},{8,12},{12,16},{16,20},{20,24},{24,28},{1,5},{5,9},{9,... | collective-permute-start | bytes 1572872 | tf_op jit(solution)/shard_map/ppermute | solution.py:16
  513.6 28.0 %collective-permute-start.15 = (f32[64,16,128]{2,1,0:T(8,128)S(1)}, f32[64,16,128]{2,1,0:T(8,128)S(1)}, u32[]{:S(2)}, u32[]{:S(2)}) collective-permute-start(f32[64,16,128]{2,1,0:T(8,128)S(1)} %get-tuple-element.6), channel_id=1, source_target_pairs={{4,0},{8,4},{12,8},{16,12},{20,16},{24,20},{28,24},{5,1},{9,5},{13... | collective-permute-start | bytes 1572872 | tf_op jit(solution)/shard_map/ppermute | solution.py:17
Sparse Core Ops, SparseCore 0:
  271.1 84.6 all-reduce.6
  612.0 83.9 all-reduce.8
where the time goes:
time: 717 us; the launch traced here: 705 us
  waiting for transfers between devices  307 us (43%)
  matrix products  278 us (39%)
  starting transfers between devices  87.7 us (12%)
  between operations  14.2 us (2%)
  other arithmetic  12.2 us (2%)
    psum x2, waiting for transfers between devices, body(): total_logs = lax.psum(log_terms, 'view')  169 us
    dot_general x4, matrix products, along_rows(): jnp.einsum('im,myz->iyz', matrix, volume, precision=lax.Precision.HIGHEST)  95.1 us
    dot_general x4, matrix products, along_depth(): jnp.einsum('xym,zm->xyz', padded, matrix, precision=lax.Precision.HIGHEST)  93.3 us
    dot_general x4, matrix products, along_columns(): jnp.einsum('jm,imz->ijz', matrix, volume, precision=lax.Precision.HIGHEST)  89.7 us
    ppermute x8, waiting for transfers between devices, extended(): after = lax.ppermute(leading, axis, down)  83.1 us
    ppermute x8, starting transfers between devices, extended(): before = lax.ppermute(last, axis, up)  70.6 us
    ppermute x8, waiting for transfers between devices, extended(): before = lax.ppermute(last, axis, up)  54.6 us
    ppermute x8, starting transfers between devices, extended(): after = lax.ppermute(leading, axis, down)  17.1 us
  transfers between devices with their start and end apart: 18, of which 16 were waited for; matrix products, arithmetic and copies ran while one was open for 2% of the time, Pallas kernels for 0%

commit v1 on v0

v1 whole, which is shorter than its diff:
```python
import functools

import jax
import jax.numpy as jnp
from jax import lax
from jax.experimental import pallas as pl
from jax.experimental.pallas import tpu as pltpu
from jax.sharding import PartitionSpec as P

ITERS = 2
TAPS = 33
HALF = 16
LANES = 128
VMEM = pl.BlockSpec(memory_space=pltpu.VMEM)
SMEM = pl.BlockSpec(memory_space=pltpu.SMEM)


def call(kernel, outs, scratch, *args):
    specs = [SMEM if a.dtype == jnp.int32 else VMEM for a in args]
    return pl.pallas_call(
        kernel,
        out_shape=[jax.ShapeDtypeStruct(s, d) for s, d in outs],
        in_specs=specs,
        out_specs=[VMEM] * len(outs),
        scratch_shapes=scratch,
        compiler_params=pltpu.CompilerParams(vmem_limit_bytes=24 * 2**20),
    )(*args)


def split(value):
    high = value.astype(jnp.bfloat16)
    low = (value - high.astype(jnp.float32)).astype(jnp.bfloat16)
    return high, low


def prepare_kernel(sx_ref, sy_ref, sz_ref, kx_ref, ky_ref, forward_ref, adjoint_ref):
    for source, target in ((sx_ref, kx_ref), (sy_ref, ky_ref)):
        taps = source[...] / jnp.sum(source[...], axis=1, keepdims=True)
        for t in range(TAPS):
            target[t] = jnp.broadcast_to(taps[:, t : t + 1], (8, LANES))
    taps = sz_ref[...] / jnp.sum(sz_ref[...], axis=1, keepdims=True)
    row = lax.broadcasted_iota(jnp.int32, (LANES, LANES), 0)
    column = lax.broadcasted_iota(jnp.int32, (LANES, LANES), 1)
    for target, offset in ((forward_ref, column - row + HALF), (adjoint_ref, row - column + HALF)):
        band = jnp.zeros((LANES, LANES), jnp.float32)
        for t in range(TAPS):
            band = jnp.where(offset == t, jnp.broadcast_to(taps[:, t : t + 1], (LANES, LANES)), band)
        high, low = split(band)
        for k in (0, LANES):
            target[k : k + LANES, :LANES] = high
            target[k : k + LANES, LANES:] = low


def blur_y_row(ext_ref, row, taps_ref, adjoint):
    length = ext_ref.shape[1] - 2 * HALF
    groups = length // 8
    total = None
    for rho in range(8):
        reach = 5 if rho == 0 else 4
        window = ext_ref[row, pl.ds(rho, length + 8 * (reach - 1)), :]
        window = window.reshape(groups + reach - 1, 8, LANES)
        for m in range(reach):
            s = rho + 8 * m
            t = s if adjoint else TAPS - 1 - s
            term = window[m : m + groups] * taps_ref[t]
            total = term if total is None else total + term
    return total.reshape(length, LANES)


def blur_x_block(ext_ref, columns, taps_ref, adjoint, store):
    length = ext_ref.shape[0] - 2 * HALF
    block = 16
    taps = [taps_ref[t] for t in range(TAPS)]
    for first in range(0, length, block):
        totals = [None] * block
        for m in range(block + 2 * HALF):
            value = ext_ref[first + m, columns, :]
            for i in range(block):
                s = m - i
                if 0 <= s < TAPS:
                    t = s if adjoint else TAPS - 1 - s
                    term = value * taps[t]
                    totals[i] = term if totals[i] is None else totals[i] + term
        for i in range(block):
            store(first + i, totals[i])


def blur_z(value, matrix_ref):
    high, low = split(value)
    both = jnp.concatenate([high, low], axis=1)
    product = jnp.dot(both, matrix_ref[...], preferred_element_type=jnp.float32)
    return product[:, :LANES] + product[:, LANES:]


def forward_y_kernel(v_ref, *refs):
    quarters, (before_ref, after_ref, taps_ref, low_ref, high_ref, ext_ref) = refs[:-6], refs[-6:]
    rows, width = before_ref.shape[0], low_ref.shape[1]
    ext_ref[:, :HALF, :] = before_ref[...]
    ext_ref[:, HALF + width :, :] = after_ref[...]
    if len(quarters) == 1:
        ext_ref[:, HALF : HALF + width, :] = quarters[0][...]
    else:
        share = rows // len(quarters)
        for d, quarter in enumerate(quarters):
            place = lax.rem(v_ref[0] + len(quarters) - d, len(quarters)) * share
            ext_ref[pl.ds(place, share), HALF : HALF + width, :] = quarter[...]

    half = rows // 2

    @pl.loop(0, half)
    def _(i):
        low_ref[i] = blur_y_row(ext_ref, i, taps_ref, False)

    @pl.loop(0, half)
    def _(i):
        high_ref[i] = blur_y_row(ext_ref, half + i, taps_ref, False)


def fill_x(ext_ref, before_ref, low_ref, high_ref, after_ref):
    half = low_ref.shape[0]
    ext_ref[:HALF] = before_ref[...]
    ext_ref[HALF : HALF + half] = low_ref[...]
    ext_ref[HALF + half : HALF + 2 * half] = high_ref[...]
    ext_ref[HALF + 2 * half :] = after_ref[...]


def ratio_kernel(before_ref, low_ref, high_ref, after_ref, data_ref, taps_ref, matrix_ref, out_low_ref, out_high_ref, ext_ref, mid_ref):
    fill_x(ext_ref, before_ref, low_ref, high_ref, after_ref)
    rows, width = mid_ref.shape[:2]

    @pl.loop(0, width // 8)
    def _(j):
        columns = pl.ds(pl.multiple_of(j * 8, 8), 8)

        def store(i, value):
            mid_ref[i, columns, :] = value

        blur_x_block(ext_ref, columns, taps_ref, False, store)

    step = 4
    for out_ref, first in ((out_low_ref, 0), (out_high_ref, rows // 2)):

        @pl.loop(0, rows // 2 // step)
        def _(c):
            value = mid_ref[pl.ds(first + c * step, step)].reshape(step * width, LANES)
            blurred = blur_z(value, matrix_ref).reshape(step, width, LANES)
            data = data_ref[pl.ds(first + c * step, step)].astype(jnp.float32)
            out_ref[pl.ds(c * step, step)] = data / blurred


def adjoint_x_kernel(before_ref, low_ref, high_ref, after_ref, taps_ref, out_ref, left_ref, right_ref, ext_ref):
    fill_x(ext_ref, before_ref, low_ref, high_ref, after_ref)
    width = out_ref.shape[1]

    @pl.loop(0, width // 8)
    def _(j):
        columns = pl.ds(pl.multiple_of(j * 8, 8), 8)

        def store(i, value):
            out_ref[i, columns, :] = value

        blur_x_block(ext_ref, columns, taps_ref, True, store)

    left_ref[...] = out_ref[:, :HALF, :]
    right_ref[...] = out_ref[:, width - HALF :, :]


def logs_kernel(v_ref, before_ref, own_ref, after_ref, taps_ref, matrix_ref, *refs):
    outs, (ext_ref, mid_ref) = refs[:-2], refs[-2:]
    rows, width = own_ref.shape[:2]
    ext_ref[:, :HALF, :] = before_ref[...]
    ext_ref[:, HALF : HALF + width, :] = own_ref[...]
    ext_ref[:, HALF + width :, :] = after_ref[...]
    share = rows // len(outs)
    for d, out_ref in enumerate(outs):
        first = lax.rem(v_ref[0] + d, len(outs)) * share

        @pl.loop(0, share)
        def _(i):
            mid_ref[i] = blur_y_row(ext_ref, first + i, taps_ref, True)

        step = 4

        @pl.loop(0, share // step)
        def _(c):
            value = mid_ref[pl.ds(c * step, step)].reshape(step * width, LANES)
            back = blur_z(value, matrix_ref).reshape(step, width, LANES)
            out_ref[pl.ds(c * step, step)] = jnp.log(back)


def shifted(size, by):
    return [(i, i + by) for i in range(size) if 0 <= i + by < size]


def exchange(last, first, axis):
    size = lax.axis_size(axis)
    return lax.ppermute(last, axis, shifted(size, 1)), lax.ppermute(first, axis, shifted(size, -1))


def rotated(value, by):
    size = lax.axis_size("view")
    return lax.ppermute(value, "view", [(i, (i + by) % size) for i in range(size)])


def body(estimate, views_data, spread_x, spread_y, spread_z):
    rows, width, depth = estimate.shape
    views = lax.axis_size("view")
    share = rows // views
    v = lax.axis_index("view")
    v_word = v.astype(jnp.int32).reshape(1)
    data = views_data[0]
    f32 = jnp.float32
    taps_shape = ((TAPS, 8, LANES), f32)
    matrix_shape = ((2 * LANES, 2 * LANES), jnp.bfloat16)
    taps_x, taps_y, forward_z, adjoint_z = call(
        prepare_kernel, [taps_shape, taps_shape, matrix_shape, matrix_shape], [], spread_x, spread_y, spread_z
    )
    half_shape = ((rows // 2, width, depth), f32)
    edge_shape = ((rows, HALF, depth), f32)
    ext_x = pltpu.VMEM((rows + 2 * HALF, width, depth), f32)
    ext_y = pltpu.VMEM((rows, width + 2 * HALF, depth), f32)
    own = lax.dynamic_slice_in_dim(estimate, v * share, share, 0)
    pieces = [estimate]
    edges = (estimate[:, width - HALF :], estimate[:, :HALF])
    for step_number in range(ITERS):
        before, after = exchange(*edges, "gy")
        low, high = call(forward_y_kernel, [half_shape] * 2, [ext_y], v_word, *pieces, before, after, taps_y)
        before, after = exchange(high, low, "gx")
        low, high = call(
            ratio_kernel, [half_shape] * 2, [ext_x, pltpu.VMEM((rows, width, depth), f32)],
            before, low, high, after, data, taps_x, forward_z,
        )
        before, after = exchange(high, low, "gx")
        mid, left, right = call(
            adjoint_x_kernel, [((rows, width, depth), f32), edge_shape, edge_shape], [ext_x],
            before, low, high, after, taps_x,
        )
        before, after = exchange(right, left, "gy")
        terms = call(
            logs_kernel, [((share, width, depth), f32)] * views, [ext_y, pltpu.VMEM((share, width, depth), f32)],
            v_word, before, mid, after, taps_y, adjoint_z,
        )
        total = terms[0]
        for d in range(1, views):
            total = total + rotated(terms[d], d)
        own = own * jnp.exp(total / views)
        if step_number + 1 < ITERS:
            pieces = [own] + [rotated(own, d) for d in range(1, views)]
            whole = jnp.zeros((rows, width, depth), f32)
            for d, piece in enumerate(pieces):
                whole = lax.dynamic_update_slice_in_dim(whole, piece, lax.rem(v + views - d, views) * share, 0)
            edges = (whole[:, width - HALF :], whole[:, :HALF])
    return own


def solution(mesh):
    in_specs = (
        P("gx", "gy", None),
        P("view", "gx", "gy", None),
        P("view", None),
        P("view", None),
        P("view", None),
    )
    out_specs = P(("gx", "view"), "gy", None)
    return jax.shard_map(body, mesh=mesh, in_specs=in_specs, out_specs=out_specs, check_vma=False)
```

time: 717 us -> 296 us (0.41)
  the two profiles are of different devices: /device:TPU:1 before, /device:TPU:115 now
where the time goes in v1:
time: 296 us; the launch traced here: 295 us
  waiting for transfers between devices  163 us (55%)
  starting transfers between devices  92.3 us (31%)
  Pallas kernels  32.7 us (11%)
  local copies, waits for them, and re-layouts  5.18 us (2%)
    ppermute x8, waiting for transfers between devices, exchange(): lax.ppermute(last, axis, shifted(size, 1))  68 us
    ppermute x9, waiting for transfers between devices, rotated(): lax.ppermute(value, 'view', [(i, (i + by) % size) for i in range(size)])  54.4 us
    ppermute x8, waiting for transfers between devices, exchange(): lax.ppermute(first, axis, shifted(size, -1))  40.5 us
    ppermute x8, starting transfers between devices, exchange(): lax.ppermute(first, axis, shifted(size, -1))  36.9 us
    pallas_call x9, Pallas kernels, call(): pl.pallas_call(kernel, out_shape=[jax.ShapeDtypeStruct(s, d) for s, d in...  32.7 us
    ppermute x9, starting transfers between devices, rotated(): lax.ppermute(value, 'view', [(i, (i + by) % size) for i in range(size)])  31 us
    ppermute x8, starting transfers between devices, exchange(): lax.ppermute(last, axis, shifted(size, 1))  24.4 us
  transfers between devices with their start and end apart: 25, of which 23 were waited for; matrix products, arithmetic and copies ran while one was open for 0% of the time, Pallas kernels for 0%

profile of v1, /device:TPU:115, one launch (start us, length us, event | category | flops | bytes accessed | tf_op | source)
XLA Modules:
  0.0 295.5 jit_solution(18306187644564591917)
XLA Ops:
  1.2 9.7 %collective-permute-start.1 = (f32[32,16,128]{2,1,0:T(8,128)S(1)}, f32[32,16,128]{2,1,0:T(8,128)S(1)}, u32[]{:S(2)}, u32[]{:S(2)}) collective-permute-start(f32[32,16,128]{2,1,0:T(8,128)S(1)} %get-tuple-element.61), channel_id=1, source_target_pairs={{4,0},{8,4},{12,8},{16,12},{20,16},{24,20},{28,24},{5,1},{9,5},{13... | collective-permute-start | bytes 786440 | tf_op jit(solution)/shard_map/ppermute | solution.py:197
  14.5 8.4 %collective-permute-done.1.refs_2_ = f32[32,16,128]{2,1,0:T(8,128)S(1)} collective-permute-done((f32[32,16,128]{2,1,0:T(8,128)S(1)}, f32[32,16,128]{2,1,0:T(8,128)S(1)}, u32[]{:S(2)}, u32[]{:S(2)}) %collective-permute-start.1) | collective-permute-done | bytes 262176 | tf_op jit(solution)/shard_map/ppermute | solution.py:197
  22.9 10.8 %collective-permute-done.refs_1_ = f32[32,16,128]{2,1,0:T(8,128)S(1)} collective-permute-done((f32[32,16,128]{2,1,0:T(8,128)S(1)}, f32[32,16,128]{2,1,0:T(8,128)S(1)}, u32[]{:S(2)}, u32[]{:S(2)}) %collective-permute-start) | collective-permute-done | bytes 262176 | tf_op jit(solution)/shard_map/ppermute | solution.py:197
  46.8 4.4 %collective-permute-done.3.after_ref = f32[16,64,128]{2,1,0:T(8,128)S(1)} collective-permute-done((f32[16,64,128]{2,1,0:T(8,128)S(1)}, f32[16,64,128]{2,1,0:T(8,128)S(1)}, u32[]{:S(2)}, u32[]{:S(2)}) %collective-permute-start.3) | collective-permute-done | bytes 524320 | tf_op jit(solution)/shard_map/ppermute | solution.py:197
  51.2 4.3 %shard_map.57 = (f32[16,64,128]{2,1,0:T(8,128)S(1)}, f32[16,64,128]{2,1,0:T(8,128)S(1)}) custom-call(f32[16,64,128]{2,1,0:T(8,128)S(1)} %collective-permute-done.2.before_ref, f32[16,64,128]{2,1,0:T(8,128)S(1)} %get-tuple-element.33.low_ref, f32[16,64,128]{2,1,0:T(8,128)S(1)} %get-tuple-element.32.high_ref, ...), custom_call_target="tpu_custom_call" | custom-call | tf_op jit(solution)/shard_map/pallas_call | solution.py:20
  63.6 4.4 %collective-permute-done.5.after_ref = f32[16,64,128]{2,1,0:T(8,128)S(1)} collective-permute-done((f32[16,64,128]{2,1,0:T(8,128)S(1)}, f32[16,64,128]{2,1,0:T(8,128)S(1)}, u32[]{:S(2)}, u32[]{:S(2)}) %collective-permute-start.5) | collective-permute-done | bytes 524320 | tf_op jit(solution)/shard_map/ppermute | solution.py:197
  70.7 6.7 %collective-permute-start.6 = (f32[32,16,128]{2,1,0:T(8,128)S(1)}, f32[32,16,128]{2,1,0:T(8,128)S(1)}, u32[]{:S(2)}, u32[]{:S(2)}) collective-permute-start(f32[32,16,128]{2,1,0:T(8,128)S(1)} %get-tuple-element.38), channel_id=1, source_target_pairs={{0,4},{4,8},{8,12},{12,16},{16,20},{20,24},{24,28},{1,5},{5,9},{9,... | collective-permute-start | bytes 786440 | tf_op jit(solution)/shard_map/ppermute | solution.py:197
  80.8 13.9 %collective-permute-done.6.before_ref = f32[32,16,128]{2,1,0:T(8,128)S(1)} collective-permute-done((f32[32,16,128]{2,1,0:T(8,128)S(1)}, f32[32,16,128]{2,1,0:T(8,128)S(1)}, u32[]{:S(2)}, u32[]{:S(2)}) %collective-permute-start.6) | collective-permute-done | bytes 262176 | tf_op jit(solution)/shard_map/ppermute | solution.py:197
  94.8 7.5 %collective-permute-done.7.after_ref = f32[32,16,128]{2,1,0:T(8,128)S(1)} collective-permute-done((f32[32,16,128]{2,1,0:T(8,128)S(1)}, f32[32,16,128]{2,1,0:T(8,128)S(1)}, u32[]{:S(2)}, u32[]{:S(2)}) %collective-permute-start.7) | collective-permute-done | bytes 262176 | tf_op jit(solution)/shard_map/ppermute | solution.py:197
  102.3 5.3 %shard_map.59 = (f32[8,64,128]{2,1,0:T(8,128)S(1)}, f32[8,64,128]{2,1,0:T(8,128)S(1)}, f32[8,64,128]{2,1,0:T(8,128)S(1)}, f32[8,64,128]{2,1,0:T(8,128)S(1)}) custom-call(s32[1]{0:T(128)} %bitcast.v_ref, f32[32,16,128]{2,1,0:T(8,128)S(1)} %collective-permute-done.6.before_ref, f32[32,64,128]{2,1,0:T(8,128)S(1)} %get-tuple-element.39.own_ref, ...), custom_call_target="tpu_custom_call" | custom-call | tf_op jit(solution)/shard_map/pallas_call | solution.py:20
  116.9 15.0 %collective-permute-done.9 = f32[8,64,128]{2,1,0:T(8,128)} collective-permute-done((f32[8,64,128]{2,1,0:T(8,128)S(1)}, f32[8,64,128]{2,1,0:T(8,128)}, u32[]{:S(2)}, u32[]{:S(2)}) %collective-permute-start.9) | collective-permute-done | bytes 262176 | tf_op jit(solution)/shard_map/ppermute | solution.py:202
  145.4 14.3 %collective-permute-done.12.refs_2_ = f32[8,64,128]{2,1,0:T(8,128)S(1)} collective-permute-done((f32[8,64,128]{2,1,0:T(8,128)S(1)}, f32[8,64,128]{2,1,0:T(8,128)S(1)}, u32[]{:S(2)}, u32[]{:S(2)}) %collective-permute-start.12) | collective-permute-done | bytes 262176 | tf_op jit(solution)/shard_map/ppermute | solution.py:202
  163.8 8.0 %collective-permute-start.15 = (f32[32,16,128]{2,1,0:T(8,128)S(1)}, f32[32,16,128]{2,1,0:T(8,128)S(1)}, u32[]{:S(2)}, u32[]{:S(2)}) collective-permute-start(f32[32,16,128]{2,1,0:T(8,128)S(1)} %get-tuple-element.59), channel_id=1, source_target_pairs={{4,0},{8,4},{12,8},{16,12},{20,16},{24,20},{28,24},{5,1},{9,5},{13... | collective-permute-start | bytes 786440 | tf_op jit(solution)/shard_map/ppermute | solution.py:197
  173.7 7.0 %collective-permute-done.15.refs_5_ = f32[32,16,128]{2,1,0:T(8,128)S(1)} collective-permute-done((f32[32,16,128]{2,1,0:T(8,128)S(1)}, f32[32,16,128]{2,1,0:T(8,128)S(1)}, u32[]{:S(2)}, u32[]{:S(2)}) %collective-permute-start.15) | collective-permute-done | bytes 262176 | tf_op jit(solution)/shard_map/ppermute | solution.py:197
  180.6 14.1 %collective-permute-done.14.refs_4_ = f32[32,16,128]{2,1,0:T(8,128)S(1)} collective-permute-done((f32[32,16,128]{2,1,0:T(8,128)S(1)}, f32[32,16,128]{2,1,0:T(8,128)S(1)}, u32[]{:S(2)}, u32[]{:S(2)}) %collective-permute-start.14) | collective-permute-done | bytes 262176 | tf_op jit(solution)/shard_map/ppermute | solution.py:197
  206.3 4.4 %collective-permute-done.17.after_ref = f32[16,64,128]{2,1,0:T(8,128)S(1)} collective-permute-done((f32[16,64,128]{2,1,0:T(8,128)S(1)}, f32[16,64,128]{2,1,0:T(8,128)S(1)}, u32[]{:S(2)}, u32[]{:S(2)}) %collective-permute-start.17) | collective-permute-done | bytes 524320 | tf_op jit(solution)/shard_map/ppermute | solution.py:197
  223.0 4.4 %collective-permute-done.19.after_ref = f32[16,64,128]{2,1,0:T(8,128)S(1)} collective-permute-done((f32[16,64,128]{2,1,0:T(8,128)S(1)}, f32[16,64,128]{2,1,0:T(8,128)S(1)}, u32[]{:S(2)}, u32[]{:S(2)}) %collective-permute-start.19) | collective-permute-done | bytes 524320 | tf_op jit(solution)/shard_map/ppermute | solution.py:197
  230.2 4.6 %collective-permute-start.20 = (f32[32,16,128]{2,1,0:T(8,128)S(1)}, f32[32,16,128]{2,1,0:T(8,128)S(1)}, u32[]{:S(2)}, u32[]{:S(2)}) collective-permute-start(f32[32,16,128]{2,1,0:T(8,128)S(1)} %get-tuple-element.50), channel_id=1, source_target_pairs={{0,4},{4,8},{8,12},{12,16},{16,20},{20,24},{24,28},{1,5},{5,9},{9,... | collective-permute-start | bytes 786440 | tf_op jit(solution)/shard_map/ppermute | solution.py:197
  234.8 5.5 %collective-permute-start.21 = (f32[32,16,128]{2,1,0:T(8,128)S(1)}, f32[32,16,128]{2,1,0:T(8,128)S(1)}, u32[]{:S(2)}, u32[]{:S(2)}) collective-permute-start(f32[32,16,128]{2,1,0:T(8,128)S(1)} %get-tuple-element.52), channel_id=1, source_target_pairs={{4,0},{8,4},{12,8},{16,12},{20,16},{24,20},{28,24},{5,1},{9,5},{13... | collective-permute-start | bytes 786440 | tf_op jit(solution)/shard_map/ppermute | solution.py:197
  240.3 15.2 %collective-permute-done.20.before_ref = f32[32,16,128]{2,1,0:T(8,128)S(1)} collective-permute-done((f32[32,16,128]{2,1,0:T(8,128)S(1)}, f32[32,16,128]{2,1,0:T(8,128)S(1)}, u32[]{:S(2)}, u32[]{:S(2)}) %collective-permute-start.20) | collective-permute-done | bytes 262176 | tf_op jit(solution)/shard_map/ppermute | solution.py:197
  255.5 5.3 %shard_map.63 = (f32[8,64,128]{2,1,0:T(8,128)S(1)}, f32[8,64,128]{2,1,0:T(8,128)S(1)}, f32[8,64,128]{2,1,0:T(8,128)S(1)}, f32[8,64,128]{2,1,0:T(8,128)S(1)}) custom-call(s32[1]{0:T(128)} %bitcast.v_ref, f32[32,16,128]{2,1,0:T(8,128)S(1)} %collective-permute-done.20.before_ref, f32[32,64,128]{2,1,0:T(8,128)S(1)} %get-tuple-element.51.own_ref, ...), custom_call_target="tpu_custom_call" | custom-call | tf_op jit(solution)/shard_map/pallas_call | solution.py:20
  264.2 8.7 %collective-permute-start.23 = (f32[8,64,128]{2,1,0:T(8,128)S(1)}, f32[8,64,128]{2,1,0:T(8,128)S(1)}, u32[]{:S(2)}, u32[]{:S(2)}) collective-permute-start(f32[8,64,128]{2,1,0:T(8,128)S(1)} %get-tuple-element.55), channel_id=1, source_target_pairs={{0,2},{1,3},{2,0},{3,1},{4,6},{5,7},{6,4},{7,5},{8,10},{9,11},{10,... | collective-permute-start | bytes 786440 | tf_op jit(solution)/shard_map/ppermute | solution.py:202
  276.3 13.0 %collective-permute-done.23 = f32[8,64,128]{2,1,0:T(8,128)S(1)} collective-permute-done((f32[8,64,128]{2,1,0:T(8,128)S(1)}, f32[8,64,128]{2,1,0:T(8,128)S(1)}, u32[]{:S(2)}, u32[]{:S(2)}) %collective-permute-start.23) | collective-permute-done | bytes 262176 | tf_op jit(solution)/shard_map/ppermute | solution.py:202
  289.3 5.3 %collective-permute-done.24 = f32[8,64,128]{2,1,0:T(8,128)S(1)} collective-permute-done((f32[8,64,128]{2,1,0:T(8,128)S(1)}, f32[8,64,128]{2,1,0:T(8,128)S(1)}, u32[]{:S(2)}, u32[]{:S(2)}) %collective-permute-start.24) | collective-permute-done | bytes 262176 | tf_op jit(solution)/shard_map/ppermute | solution.py:202
  (55 shorter events, 95.1 us)
Async XLA Ops:
  1.2 21.7 %collective-permute-start.1 = (f32[32,16,128]{2,1,0:T(8,128)S(1)}, f32[32,16,128]{2,1,0:T(8,128)S(1)}, u32[]{:S(2)}, u32[]{:S(2)}) collective-permute-start(f32[32,16,128]{2,1,0:T(8,128)S(1)} %get-tuple-element.61), channel_id=1, source_target_pairs={{4,0},{8,4},{12,8},{16,12},{20,16},{24,20},{28,24},{5,1},{9,5},{13... | collective-permute-start | bytes 786440 | tf_op jit(solution)/shard_map/ppermute | solution.py:197
  10.9 22.9 %collective-permute-start = (f32[32,16,128]{2,1,0:T(8,128)S(1)}, f32[32,16,128]{2,1,0:T(8,128)S(1)}, u32[]{:S(2)}, u32[]{:S(2)}) collective-permute-start(f32[32,16,128]{2,1,0:T(8,128)S(1)} %get-tuple-element.62), channel_id=1, source_target_pairs={{0,4},{4,8},{8,12},{12,16},{16,20},{20,24},{24,28},{1,5},{5,9},{9,... | collective-permute-start | bytes 786440 | tf_op jit(solution)/shard_map/ppermute | solution.py:197
  37.3 9.5 %collective-permute-start.2 = (f32[16,64,128]{2,1,0:T(8,128)S(1)}, f32[16,64,128]{2,1,0:T(8,128)S(1)}, u32[]{:S(2)}, u32[]{:S(2)}) collective-permute-start(f32[16,64,128]{2,1,0:T(8,128)S(1)} %get-tuple-element.32.high_ref), channel_id=1, source_target_pairs={{0,32},{32,64},{64,96},{96,128},{128,160},{160,192},{192,224},{224... | collective-permute-start | bytes 1572872 | tf_op jit(solution)/shard_map/ppermute | solution.py:197
  40.7 10.5 %collective-permute-start.3 = (f32[16,64,128]{2,1,0:T(8,128)S(1)}, f32[16,64,128]{2,1,0:T(8,128)S(1)}, u32[]{:S(2)}, u32[]{:S(2)}) collective-permute-start(f32[16,64,128]{2,1,0:T(8,128)S(1)} %get-tuple-element.33.low_ref), channel_id=1, source_target_pairs={{32,0},{64,32},{96,64},{128,96},{160,128},{192,160},{224,192},{256... | collective-permute-start | bytes 1572872 | tf_op jit(solution)/shard_map/ppermute | solution.py:197
  55.5 8.0 %collective-permute-start.4 = (f32[16,64,128]{2,1,0:T(8,128)S(1)}, f32[16,64,128]{2,1,0:T(8,128)S(1)}, u32[]{:S(2)}, u32[]{:S(2)}) collective-permute-start(f32[16,64,128]{2,1,0:T(8,128)S(1)} %get-tuple-element.36.high_ref), channel_id=1, source_target_pairs={{0,32},{32,64},{64,96},{96,128},{128,160},{160,192},{192,224},{224... | collective-permute-start | bytes 1572872 | tf_op jit(solution)/shard_map/ppermute | solution.py:197
  57.5 10.5 %collective-permute-start.5 = (f32[16,64,128]{2,1,0:T(8,128)S(1)}, f32[16,64,128]{2,1,0:T(8,128)S(1)}, u32[]{:S(2)}, u32[]{:S(2)}) collective-permute-start(f32[16,64,128]{2,1,0:T(8,128)S(1)} %get-tuple-element.37.low_ref), channel_id=1, source_target_pairs={{32,0},{64,32},{96,64},{128,96},{160,128},{192,160},{224,192},{256... | collective-permute-start | bytes 1572872 | tf_op jit(solution)/shard_map/ppermute | solution.py:197
  70.7 24.0 %collective-permute-start.6 = (f32[32,16,128]{2,1,0:T(8,128)S(1)}, f32[32,16,128]{2,1,0:T(8,128)S(1)}, u32[]{:S(2)}, u32[]{:S(2)}) collective-permute-start(f32[32,16,128]{2,1,0:T(8,128)S(1)} %get-tuple-element.38), channel_id=1, source_target_pairs={{0,4},{4,8},{8,12},{12,16},{16,20},{20,24},{24,28},{1,5},{5,9},{9,... | collective-permute-start | bytes 786440 | tf_op jit(solution)/shard_map/ppermute | solution.py:197
  77.4 24.8 %collective-permute-start.7 = (f32[32,16,128]{2,1,0:T(8,128)S(1)}, f32[32,16,128]{2,1,0:T(8,128)S(1)}, u32[]{:S(2)}, u32[]{:S(2)}) collective-permute-start(f32[32,16,128]{2,1,0:T(8,128)S(1)} %get-tuple-element.40), channel_id=1, source_target_pairs={{4,0},{8,4},{12,8},{16,12},{20,16},{24,20},{28,24},{5,1},{9,5},{13... | collective-permute-start | bytes 786440 | tf_op jit(solution)/shard_map/ppermute | solution.py:197
  107.6 9.4 %collective-permute-start.8 = (f32[8,64,128]{2,1,0:T(8,128)S(1)}, f32[8,64,128]{2,1,0:T(8,128)S(1)}, u32[]{:S(2)}, u32[]{:S(2)}) collective-permute-start(f32[8,64,128]{2,1,0:T(8,128)S(1)} %get-tuple-element.43), channel_id=1, source_target_pairs={{0,1},{1,2},{2,3},{3,0},{4,5},{5,6},{6,7},{7,4},{8,9},{9,10},{10,1... | collective-permute-start | bytes 786440 | tf_op jit(solution)/shard_map/ppermute | solution.py:202
  109.9 22.0 %collective-permute-start.9 = (f32[8,64,128]{2,1,0:T(8,128)S(1)}, f32[8,64,128]{2,1,0:T(8,128)}, u32[]{:S(2)}, u32[]{:S(2)}) collective-permute-start(f32[8,64,128]{2,1,0:T(8,128)S(1)} %get-tuple-element.44), channel_id=1, source_target_pairs={{0,2},{1,3},{2,0},{3,1},{4,6},{5,7},{6,4},{7,5},{8,10},{9,11},{10,... | collective-permute-start | bytes 786440 | tf_op jit(solution)/shard_map/ppermute | solution.py:202
  112.4 21.8 %collective-permute-start.10 = (f32[8,64,128]{2,1,0:T(8,128)S(1)}, f32[8,64,128]{2,1,0:T(8,128)}, u32[]{:S(2)}, u32[]{:S(2)}) collective-permute-start(f32[8,64,128]{2,1,0:T(8,128)S(1)} %get-tuple-element.45), channel_id=1, source_target_pairs={{0,3},{1,0},{2,1},{3,2},{4,7},{5,4},{6,5},{7,6},{8,11},{9,8},{10,9... | collective-permute-start | bytes 786440 | tf_op jit(solution)/shard_map/ppermute | solution.py:202
  135.5 9.3 %collective-permute-start.11 = (f32[8,64,128]{2,1,0:T(8,128)S(1)}, f32[8,64,128]{2,1,0:T(8,128)S(1)}, u32[]{:S(2)}, u32[]{:S(2)}) collective-permute-start(f32[8,64,128]{2,1,0:T(8,128)S(1)} %get-tuple-element.58.refs_0_), channel_id=1, source_target_pairs={{0,1},{1,2},{2,3},{3,0},{4,5},{5,6},{6,7},{7,4},{8,9},{9,10},{10,1... | collective-permute-start | bytes 786440 | tf_op jit(solution)/shard_map/ppermute | solution.py:202
  137.4 22.3 %collective-permute-start.12 = (f32[8,64,128]{2,1,0:T(8,128)S(1)}, f32[8,64,128]{2,1,0:T(8,128)S(1)}, u32[]{:S(2)}, u32[]{:S(2)}) collective-permute-start(f32[8,64,128]{2,1,0:T(8,128)S(1)} %get-tuple-element.58.refs_0_), channel_id=1, source_target_pairs={{0,2},{1,3},{2,0},{3,1},{4,6},{5,7},{6,4},{7,5},{8,10},{9,11},{10,... | collective-permute-start | bytes 786440 | tf_op jit(solution)/shard_map/ppermute | solution.py:202
  140.2 21.7 %collective-permute-start.13 = (f32[8,64,128]{2,1,0:T(8,128)S(1)}, f32[8,64,128]{2,1,0:T(8,128)S(1)}, u32[]{:S(2)}, u32[]{:S(2)}) collective-permute-start(f32[8,64,128]{2,1,0:T(8,128)S(1)} %get-tuple-element.58.refs_0_), channel_id=1, source_target_pairs={{0,3},{1,0},{2,1},{3,2},{4,7},{5,4},{6,5},{7,6},{8,11},{9,8},{10,9... | collective-permute-start | bytes 786440 | tf_op jit(solution)/shard_map/ppermute | solution.py:202
  163.8 16.9 %collective-permute-start.15 = (f32[32,16,128]{2,1,0:T(8,128)S(1)}, f32[32,16,128]{2,1,0:T(8,128)S(1)}, u32[]{:S(2)}, u32[]{:S(2)}) collective-permute-start(f32[32,16,128]{2,1,0:T(8,128)S(1)} %get-tuple-element.59), channel_id=1, source_target_pairs={{4,0},{8,4},{12,8},{16,12},{20,16},{24,20},{28,24},{5,1},{9,5},{13... | collective-permute-start | bytes 786440 | tf_op jit(solution)/shard_map/ppermute | solution.py:197
  171.7 23.0 %collective-permute-start.14 = (f32[32,16,128]{2,1,0:T(8,128)S(1)}, f32[32,16,128]{2,1,0:T(8,128)S(1)}, u32[]{:S(2)}, u32[]{:S(2)}) collective-permute-start(f32[32,16,128]{2,1,0:T(8,128)S(1)} %get-tuple-element.60), channel_id=1, source_target_pairs={{0,4},{4,8},{8,12},{12,16},{16,20},{20,24},{24,28},{1,5},{5,9},{9,... | collective-permute-start | bytes 786440 | tf_op jit(solution)/shard_map/ppermute | solution.py:197
  200.2 10.5 %collective-permute-start.17 = (f32[16,64,128]{2,1,0:T(8,128)S(1)}, f32[16,64,128]{2,1,0:T(8,128)S(1)}, u32[]{:S(2)}, u32[]{:S(2)}) collective-permute-start(f32[16,64,128]{2,1,0:T(8,128)S(1)} %get-tuple-element.47.low_ref), channel_id=1, source_target_pairs={{32,0},{64,32},{96,64},{128,96},{160,128},{192,160},{224,192},{256... | collective-permute-start | bytes 1572872 | tf_op jit(solution)/shard_map/ppermute | solution.py:197
  215.0 8.0 %collective-permute-start.18 = (f32[16,64,128]{2,1,0:T(8,128)S(1)}, f32[16,64,128]{2,1,0:T(8,128)S(1)}, u32[]{:S(2)}, u32[]{:S(2)}) collective-permute-start(f32[16,64,128]{2,1,0:T(8,128)S(1)} %get-tuple-element.48.high_ref), channel_id=1, source_target_pairs={{0,32},{32,64},{64,96},{96,128},{128,160},{160,192},{192,224},{224... | collective-permute-start | bytes 1572872 | tf_op jit(solution)/shard_map/ppermute | solution.py:197
  216.9 10.5 %collective-permute-start.19 = (f32[16,64,128]{2,1,0:T(8,128)S(1)}, f32[16,64,128]{2,1,0:T(8,128)S(1)}, u32[]{:S(2)}, u32[]{:S(2)}) collective-permute-start(f32[16,64,128]{2,1,0:T(8,128)S(1)} %get-tuple-element.49.low_ref), channel_id=1, source_target_pairs={{32,0},{64,32},{96,64},{128,96},{160,128},{192,160},{224,192},{256... | collective-permute-start | bytes 1572872 | tf_op jit(solution)/shard_map/ppermute | solution.py:197
  230.2 25.3 %collective-permute-start.20 = (f32[32,16,128]{2,1,0:T(8,128)S(1)}, f32[32,16,128]{2,1,0:T(8,128)S(1)}, u32[]{:S(2)}, u32[]{:S(2)}) collective-permute-start(f32[32,16,128]{2,1,0:T(8,128)S(1)} %get-tuple-element.50), channel_id=1, source_target_pairs={{0,4},{4,8},{8,12},{12,16},{16,20},{20,24},{24,28},{1,5},{5,9},{9,... | collective-permute-start | bytes 786440 | tf_op jit(solution)/shard_map/ppermute | solution.py:197
  234.8 20.7 %collective-permute-start.21 = (f32[32,16,128]{2,1,0:T(8,128)S(1)}, f32[32,16,128]{2,1,0:T(8,128)S(1)}, u32[]{:S(2)}, u32[]{:S(2)}) collective-permute-start(f32[32,16,128]{2,1,0:T(8,128)S(1)} %get-tuple-element.52), channel_id=1, source_target_pairs={{4,0},{8,4},{12,8},{16,12},{20,16},{24,20},{28,24},{5,1},{9,5},{13... | collective-permute-start | bytes 786440 | tf_op jit(solution)/shard_map/ppermute | solution.py:197
  260.7 15.6 %collective-permute-start.22 = (f32[8,64,128]{2,1,0:T(8,128)S(1)}, f32[8,64,128]{2,1,0:T(8,128)S(1)}, u32[]{:S(2)}, u32[]{:S(2)}) collective-permute-start(f32[8,64,128]{2,1,0:T(8,128)S(1)} %get-tuple-element.54), channel_id=1, source_target_pairs={{0,1},{1,2},{2,3},{3,0},{4,5},{5,6},{6,7},{7,4},{8,9},{9,10},{10,1... | collective-permute-start | bytes 786440 | tf_op jit(solution)/shard_map/ppermute | solution.py:202
  264.2 25.1 %collective-permute-start.23 = (f32[8,64,128]{2,1,0:T(8,128)S(1)}, f32[8,64,128]{2,1,0:T(8,128)S(1)}, u32[]{:S(2)}, u32[]{:S(2)}) collective-permute-start(f32[8,64,128]{2,1,0:T(8,128)S(1)} %get-tuple-element.55), channel_id=1, source_target_pairs={{0,2},{1,3},{2,0},{3,1},{4,6},{5,7},{6,4},{7,5},{8,10},{9,11},{10,... | collective-permute-start | bytes 786440 | tf_op jit(solution)/shard_map/ppermute | solution.py:202
  272.9 21.7 %collective-permute-start.24 = (f32[8,64,128]{2,1,0:T(8,128)S(1)}, f32[8,64,128]{2,1,0:T(8,128)S(1)}, u32[]{:S(2)}, u32[]{:S(2)}) collective-permute-start(f32[8,64,128]{2,1,0:T(8,128)S(1)} %get-tuple-element.56), channel_id=1, source_target_pairs={{0,3},{1,0},{2,1},{3,2},{4,7},{5,4},{6,5},{7,6},{8,11},{9,8},{10,9... | collective-permute-start | bytes 786440 | tf_op jit(solution)/shard_map/ppermute | solution.py:202
  (7 other events, 63.2 us)

commit v2 on v0

v2 whole, which is shorter than its diff:
```python
import jax
import jax.numpy as jnp
from jax import lax
from jax.experimental import pallas as pl
from jax.experimental.pallas import tpu as pltpu
from jax.sharding import PartitionSpec as P

ITERS = 2
TAPS = 33
HALF = 16
LANES = 128
VMEM = pl.BlockSpec(memory_space=pltpu.VMEM)
SMEM = pl.BlockSpec(memory_space=pltpu.SMEM)


def call(kernel, outs, scratch, *args):
    specs = [SMEM if a.dtype == jnp.int32 else VMEM for a in args]
    return pl.pallas_call(
        kernel,
        out_shape=[jax.ShapeDtypeStruct(s, d) for s, d in outs],
        in_specs=specs,
        out_specs=[VMEM] * len(outs),
        scratch_shapes=scratch,
        compiler_params=pltpu.CompilerParams(vmem_limit_bytes=24 * 2**20),
    )(*args)


def split(value):
    high = value.astype(jnp.bfloat16)
    low = (value - high.astype(jnp.float32)).astype(jnp.bfloat16)
    return high, low


def source(v_ref, d, views):
    return lax.rem(v_ref[0] + views - d, views)


def deal_kernel(v_ref, data_ref, *out_refs):
    views, width = len(out_refs), out_refs[0].shape[1]
    for d, out_ref in enumerate(out_refs):
        first = pl.multiple_of(lax.rem(v_ref[0] + d, views) * width, width)
        out_ref[...] = data_ref[:, pl.ds(first, width), :].astype(jnp.float32)


def prepare_kernel(v_ref, *refs):
    spreads_refs, (taps_x_ref, taps_y_ref, forward_ref, adjoint_ref) = refs[:-4], refs[-4:]
    row = lax.broadcasted_iota(jnp.int32, (LANES, LANES), 0)
    column = lax.broadcasted_iota(jnp.int32, (LANES, LANES), 1)
    for d, spreads_ref in enumerate(spreads_refs):
        view = source(v_ref, d, len(spreads_refs))
        spreads = spreads_ref[:, :TAPS]
        normal = spreads / jnp.sum(spreads, axis=1, keepdims=True)
        for n, target in ((0, taps_x_ref), (1, taps_y_ref)):
            for t in range(TAPS):
                target[view, t] = jnp.broadcast_to(normal[n : n + 1, t : t + 1], (8, LANES))
        for target, offset in ((forward_ref, column - row + HALF), (adjoint_ref, row - column + HALF)):
            band = jnp.zeros((LANES, LANES), jnp.float32)
            for t in range(TAPS):
                tap = jnp.broadcast_to(normal[2:3, t : t + 1], (LANES, LANES))
                band = jnp.where(offset == t, tap, band)
            high, low = split(band)
            for k in (0, LANES):
                target[view, k : k + LANES, :LANES] = high
                target[view, k : k + LANES, LANES:] = low


def blur_y(ext_ref, rows, taps, adjoint):
    width = ext_ref.shape[1] - 2 * HALF
    groups = width // 8
    totals = [None] * len(taps)
    for rho in range(8):
        reach = 5 if rho == 0 else 4
        window = ext_ref[rows, pl.ds(rho, width + 8 * (reach - 1)), :]
        window = window.reshape(window.shape[0], groups + reach - 1, 8, LANES)
        for m in range(reach):
            s = rho + 8 * m
            t = s if adjoint else TAPS - 1 - s
            for n, tap in enumerate(taps):
                term = window[:, m : m + groups] * tap(t)
                totals[n] = term if totals[n] is None else totals[n] + term
    return [total.reshape(total.shape[0], width, LANES) for total in totals]


def blur_x(load, tap, adjoint, length, store):
    block = 16
    taps = [tap(t) for t in range(TAPS)]
    for first in range(0, length, block):
        totals = [None] * block
        for m in range(block + 2 * HALF):
            value = load(first + m)
            for i in range(block):
                s = m - i
                if 0 <= s < TAPS:
                    term = value * taps[s if adjoint else TAPS - 1 - s]
                    totals[i] = term if totals[i] is None else totals[i] + term
        for i in range(block):
            store(first + i, totals[i])


def blur_z(value, matrix):
    rows, width, _ = value.shape
    high, low = split(value.reshape(rows * width, LANES))
    product = jnp.dot(jnp.concatenate([high, low], axis=1), matrix, preferred_element_type=jnp.float32)
    return (product[:, :LANES] + product[:, LANES:]).reshape(rows, width, LANES)


def forward_y_kernel(before_ref, own_ref, after_ref, taps_ref, low_ref, high_ref, ext_ref):
    rows, width = own_ref.shape[:2]
    views, half = low_ref.shape[:2]
    ext_ref[:, :HALF, :] = before_ref[...]
    ext_ref[:, HALF : HALF + width, :] = own_ref[...]
    ext_ref[:, HALF + width :, :] = after_ref[...]
    taps = [lambda t, view=view: taps_ref[view, t] for view in range(views)]
    block = 2
    for out_ref, first in ((low_ref, 0), (high_ref, half)):

        @pl.loop(0, half // block)
        def _(i):
            for view, blurred in enumerate(blur_y(ext_ref, pl.ds(first + i * block, block), taps, False)):
                out_ref[view, pl.ds(i * block, block)] = blurred


def loop_x(refs, taps_ref, adjoint, out_ref):
    views, rows, width, _ = out_ref.shape
    groups = width // 8

    @pl.loop(0, views * groups)
    def _(n):
        view = n // groups
        columns = pl.ds(pl.multiple_of(lax.rem(n, groups) * 8, 8), 8)

        def load(m):
            return refs[m // HALF][view, m % HALF, columns, :]

        def store(i, value):
            out_ref[view, i, columns, :] = value

        blur_x(load, lambda t: taps_ref[view, t], adjoint, rows, store)


def ratio_kernel(v_ref, before_ref, low_ref, high_ref, after_ref, taps_ref, matrix_ref, *refs):
    data_refs, (out_low_ref, out_high_ref, mid_ref) = refs[:-3], refs[-3:]
    loop_x((before_ref, low_ref, high_ref, after_ref), taps_ref, False, mid_ref)
    half = out_low_ref.shape[1]
    for d, data_ref in enumerate(data_refs):
        view = source(v_ref, d, len(data_refs))
        for out_ref, first in ((out_low_ref, 0), (out_high_ref, half)):
            blurred = blur_z(mid_ref[view, pl.ds(first, half)], matrix_ref[view])
            out_ref[view] = data_ref[pl.ds(first, half)] / blurred


def adjoint_x_kernel(before_ref, low_ref, high_ref, after_ref, taps_ref, out_ref):
    loop_x((before_ref, low_ref, high_ref, after_ref), taps_ref, True, out_ref)


def update_kernel(v_ref, before_ref, own_ref, after_ref, taps_ref, matrix_ref, estimate_ref, *refs):
    outs, (ext_ref, mid_ref, total_ref) = refs[:-3], refs[-3:]
    views, rows, width, _ = own_ref.shape
    block = 4

    @pl.loop(0, views)
    def _(view):
        ext_ref[:, :HALF, :] = before_ref[view]
        ext_ref[:, HALF : HALF + width, :] = own_ref[view]
        ext_ref[:, HALF + width :, :] = after_ref[view]

        @pl.loop(0, rows // block)
        def _(i):
            there = pl.ds(i * block, block)
            mid_ref[there] = blur_y(ext_ref, there, [lambda t: taps_ref[view, t]], True)[0]

        for first in range(0, rows, HALF):
            there = pl.ds(first, HALF)
            terms = jnp.log(blur_z(mid_ref[there], matrix_ref[view]))
            total_ref[there] = jnp.where(view == 0, terms, terms + total_ref[there])

    share = rows // len(outs)
    for d, out_ref in enumerate(outs):
        there = pl.ds(lax.rem(v_ref[0] + d, len(outs)) * share, share)
        out_ref[...] = estimate_ref[there] * jnp.exp(total_ref[there] / views)


def collect_kernel(v_ref, *refs):
    pieces, out_ref = refs[:-1], refs[-1]
    width = pieces[0].shape[1]
    for d, piece in enumerate(pieces):
        first = pl.multiple_of(source(v_ref, d, len(pieces)) * width, width)
        out_ref[:, pl.ds(first, width), :] = piece[...]


def shifted(size, by):
    return [(i, i + by) for i in range(size) if 0 <= i + by < size]


def exchange(last, first, axes):
    size = lax.axis_size(axes)
    return lax.ppermute(last, axes, shifted(size, 1)), lax.ppermute(first, axes, shifted(size, -1))


def rotated(pieces):
    size = len(pieces)
    return [pieces[0]] + [
        lax.ppermute(pieces[d], "view", [(i, (i + d) % size) for i in range(size)]) for d in range(1, size)
    ]


def body(estimate, views_data, spread_x, spread_y, spread_z):
    rows, width, depth = estimate.shape
    views = lax.axis_size("view")
    width = width // views
    assert width == HALF and rows == 2 * HALF and depth == LANES
    f32 = jnp.float32
    v = lax.axis_index("view")
    v_word = v.astype(jnp.int32).reshape(1)
    part_shape = ((rows, width, depth), f32)
    all_shape = ((views, rows, width, depth), f32)
    half_shape = ((views, rows // 2, width, depth), f32)
    taps_shape = ((views, TAPS, 8, LANES), f32)
    matrix_shape = ((views, 2 * LANES, 2 * LANES), jnp.bfloat16)
    ext = pltpu.VMEM((rows, width + 2 * HALF, depth), f32)

    own = lax.dynamic_slice_in_dim(estimate, v * width, width, 1)
    spreads = jnp.concatenate([spread_x, spread_y, spread_z, jnp.ones((5, TAPS), f32)])
    spreads = rotated([jnp.pad(spreads, ((0, 0), (0, LANES - TAPS)))] * views)
    data = rotated(call(deal_kernel, [part_shape] * views, [], v_word, views_data[0]))
    taps_x, taps_y, forward_z, adjoint_z = call(
        prepare_kernel, [taps_shape, taps_shape, matrix_shape, matrix_shape], [], v_word, *spreads
    )
    for step_number in range(ITERS):
        before, after = exchange(own, own, ("gy", "view"))
        low, high = call(forward_y_kernel, [half_shape] * 2, [ext], before, own, after, taps_y)
        before, after = exchange(high, low, "gx")
        low, high = call(
            ratio_kernel, [half_shape] * 2, [pltpu.VMEM(*all_shape)],
            v_word, before, low, high, after, taps_x, forward_z, *data,
        )
        before, after = exchange(high, low, "gx")
        mid = call(adjoint_x_kernel, [all_shape], [], before, low, high, after, taps_x)[0]
        before, after = exchange(mid, mid, ("gy", "view"))
        last_step = step_number + 1 == ITERS
        pieces = [((rows // views, width, depth), f32)] * views if last_step else [part_shape]
        own, *others = call(
            update_kernel, pieces, [ext, pltpu.VMEM(*part_shape), pltpu.VMEM(*part_shape)],
            v_word, before, mid, after, taps_y, adjoint_z, own,
        )
    pieces = rotated([own, *others])
    return call(collect_kernel, [((rows // views, width * views, depth), f32)], [], v_word, *pieces)[0]


def solution(mesh):
    in_specs = (
        P("gx", "gy", None),
        P("view", "gx", "gy", None),
        P("view", None),
        P("view", None),
        P("view", None),
    )
    out_specs = P(("gx", "view"), "gy", None)
    return jax.shard_map(body, mesh=mesh, in_specs=in_specs, out_specs=out_specs, check_vma=False)
```

time: 717 us -> 222 us (0.31)
  the two profiles are of different devices: /device:TPU:1 before, /device:TPU:22 now
where the time goes in v2:
time: 222 us; the launch traced here: 221 us
  waiting for transfers between devices  101 us (45%)
  starting transfers between devices  88 us (40%)
  Pallas kernels  29.3 us (13%)
    ppermute x8, waiting for transfers between devices, exchange(): lax.ppermute(first, axes, shifted(size, -1))  51.9 us
    ppermute x8, starting transfers between devices, exchange(): lax.ppermute(first, axes, shifted(size, -1))  39 us
    pallas_call x11, Pallas kernels, call(): pl.pallas_call(kernel, out_shape=[jax.ShapeDtypeStruct(s, d) for s, d in...  29.3 us
    ppermute x8, waiting for transfers between devices, exchange(): lax.ppermute(last, axes, shifted(size, 1))  28.9 us
    ppermute x9, starting transfers between devices, rotated(): lax.ppermute(pieces[d], 'view', [(i, (i + d) % size) for i in range(size)])  26.9 us
    ppermute x8, starting transfers between devices, exchange(): lax.ppermute(last, axes, shifted(size, 1))  22.1 us
    ppermute x9, waiting for transfers between devices, rotated(): lax.ppermute(pieces[d], 'view', [(i, (i + d) % size) for i in range(size)])  20.6 us
  transfers between devices with their start and end apart: 25, of which 18 were waited for; matrix products, arithmetic and copies ran while one was open for 0% of the time, Pallas kernels for 1%

profile of v2, /device:TPU:22, one launch (start us, length us, event | category | flops | bytes accessed | tf_op | source)
XLA Modules:
  0.0 221.0 jit_solution(4962762696061251345)
XLA Ops:
  1.2 11.2 %collective-permute-start.1 = (f32[32,16,128]{2,1,0:T(8,128)S(1)}, f32[32,16,128]{2,1,0:T(8,128)S(1)}, u32[]{:S(2)}, u32[]{:S(2)}) collective-permute-start(f32[32,16,128]{2,1,0:T(8,128)S(1)} %constant_dynamic-slice_fusion.own_ref.estimate_ref), channel_id=1, source_target_pairs={{1,0},{2,1},{3,2},{4,3},{5,4},{6,5},{7,6},{8,7},{9,8},{10,9},{11,1... | collective-permute-start | bytes 786440 | tf_op jit(solution)/shard_map/ppermute | solution.py:197
  19.3 3.7 %collective-permute-start.2 = (f32[8,128]{1,0:T(8,128)S(1)}, f32[8,128]{1,0:T(8,128)S(1)}, u32[]{:S(2)}, u32[]{:S(2)}) collective-permute-start(f32[8,128]{1,0:T(8,128)S(1)} %pad.4.refs_0_), channel_id=1, source_target_pairs={{0,1},{1,2},{2,3},{3,0},{4,5},{5,6},{6,7},{7,4},{8,9},{9,10},{10,1... | collective-permute-start | bytes 12296 | tf_op jit(solution)/shard_map/ppermute | solution.py:203
  34.3 3.6 %collective-permute-start.6 = (f32[4,16,16,128]{3,2,1,0:T(8,128)S(1)}, f32[4,16,16,128]{3,2,1,0:T(8,128)S(1)}, u32[]{:S(2)}, u32[]{:S(2)}) collective-permute-start(f32[4,16,16,128]{3,2,1,0:T(8,128)S(1)} %get-tuple-element.27.low_ref), channel_id=1, source_target_pairs={{32,0},{64,32},{96,64},{128,96},{160,128},{192,160},{224,192},{256... | collective-permute-start | bytes 1572872 | tf_op jit(solution)/shard_map/ppermute | solution.py:197
  40.0 4.5 %collective-permute-start.8 = (f32[32,16,128]{2,1,0:T(8,128)S(1)}, f32[32,16,128]{2,1,0:T(8,128)S(1)}, u32[]{:S(2)}, u32[]{:S(2)}) collective-permute-start(f32[32,16,128]{2,1,0:T(8,128)S(1)} %get-tuple-element.32), channel_id=1, source_target_pairs={{0,2},{1,3},{2,0},{3,1},{4,6},{5,7},{6,4},{7,5},{8,10},{9,11},{10,... | collective-permute-start | bytes 786440 | tf_op jit(solution)/shard_map/ppermute | solution.py:203
  47.6 3.4 %collective-permute-done.7.refs_1_ = f32[32,16,128]{2,1,0:T(8,128)S(1)} collective-permute-done((f32[32,16,128]{2,1,0:T(8,128)S(1)}, f32[32,16,128]{2,1,0:T(8,128)S(1)}, u32[]{:S(2)}, u32[]{:S(2)}) %collective-permute-start.7) | collective-permute-done | bytes 262176 | tf_op jit(solution)/shard_map/ppermute | solution.py:203
  51.0 10.2 %collective-permute-done.8.refs_2_ = f32[32,16,128]{2,1,0:T(8,128)S(1)} collective-permute-done((f32[32,16,128]{2,1,0:T(8,128)S(1)}, f32[32,16,128]{2,1,0:T(8,128)S(1)}, u32[]{:S(2)}, u32[]{:S(2)}) %collective-permute-start.8) | collective-permute-done | bytes 262176 | tf_op jit(solution)/shard_map/ppermute | solution.py:203
  66.2 3.6 %collective-permute-start.11 = (f32[4,16,16,128]{3,2,1,0:T(8,128)S(1)}, f32[4,16,16,128]{3,2,1,0:T(8,128)S(1)}, u32[]{:S(2)}, u32[]{:S(2)}) collective-permute-start(f32[4,16,16,128]{3,2,1,0:T(8,128)S(1)} %get-tuple-element.35.low_ref), channel_id=1, source_target_pairs={{32,0},{64,32},{96,64},{128,96},{160,128},{192,160},{224,192},{256... | collective-permute-start | bytes 1572872 | tf_op jit(solution)/shard_map/ppermute | solution.py:197
  69.9 4.9 %collective-permute-done.10.before_ref = f32[4,16,16,128]{3,2,1,0:T(8,128)S(1)} collective-permute-done((f32[4,16,16,128]{3,2,1,0:T(8,128)S(1)}, f32[4,16,16,128]{3,2,1,0:T(8,128)S(1)}, u32[]{:S(2)}, u32[]{:S(2)}) %collective-permute-start.10) | collective-permute-done | bytes 524320 | tf_op jit(solution)/shard_map/ppermute | solution.py:197
  79.1 11.2 %collective-permute-start.13 = (f32[4,32,16,128]{3,2,1,0:T(8,128)S(1)}, f32[4,32,16,128]{3,2,1,0:T(8,128)S(1)}, u32[]{:S(2)}, u32[]{:S(2)}) collective-permute-start(f32[4,32,16,128]{3,2,1,0:T(8,128)S(1)} %shard_map.59.own_ref), channel_id=1, source_target_pairs={{1,0},{2,1},{3,2},{4,3},{5,4},{6,5},{7,6},{8,7},{9,8},{10,9},{11,1... | collective-permute-start | bytes 3145736 | tf_op jit(solution)/shard_map/ppermute | solution.py:197
  92.3 19.8 %collective-permute-done.13.after_ref = f32[4,32,16,128]{3,2,1,0:T(8,128)S(1)} collective-permute-done((f32[4,32,16,128]{3,2,1,0:T(8,128)S(1)}, f32[4,32,16,128]{3,2,1,0:T(8,128)S(1)}, u32[]{:S(2)}, u32[]{:S(2)}) %collective-permute-start.13) | collective-permute-done | bytes 1048608 | tf_op jit(solution)/shard_map/ppermute | solution.py:197
  112.1 6.8 %collective-permute-done.12.before_ref = f32[4,32,16,128]{3,2,1,0:T(8,128)S(1)} collective-permute-done((f32[4,32,16,128]{3,2,1,0:T(8,128)S(1)}, f32[4,32,16,128]{3,2,1,0:T(8,128)S(1)}, u32[]{:S(2)}, u32[]{:S(2)}) %collective-permute-start.12) | collective-permute-done | bytes 1048608 | tf_op jit(solution)/shard_map/ppermute | solution.py:197
  118.9 4.4 %shard_map.60.own_ref.estimate_ref = f32[32,16,128]{2,1,0:T(8,128)S(1)} custom-call(s32[1]{0:T(128)} %bitcast.v_ref, f32[4,32,16,128]{3,2,1,0:T(8,128)S(1)} %collective-permute-done.12.before_ref, f32[4,32,16,128]{3,2,1,0:T(8,128)S(1)} %shard_map.59.own_ref, f32[4,32,16,128]{3,2,1,0:T(8,128)S(1)} %collective-permute-done.13.after_ref, ...), custom_call_target="tpu_custom_call" | custom-call | tf_op jit(solution)/shard_map/pallas_call | solution.py:18
  125.2 3.9 %collective-permute-start.14 = (f32[32,16,128]{2,1,0:T(8,128)S(1)}, f32[32,16,128]{2,1,0:T(8,128)S(1)}, u32[]{:S(2)}, u32[]{:S(2)}) collective-permute-start(f32[32,16,128]{2,1,0:T(8,128)S(1)} %shard_map.60.own_ref.estimate_ref), channel_id=1, source_target_pairs={{0,1},{1,2},{2,3},{3,4},{4,5},{5,6},{6,7},{7,8},{8,9},{9,10},{10,1... | collective-permute-start | bytes 786440 | tf_op jit(solution)/shard_map/ppermute | solution.py:197
  129.2 4.9 %collective-permute-done.15.after_ref = f32[32,16,128]{2,1,0:T(8,128)S(1)} collective-permute-done((f32[32,16,128]{2,1,0:T(8,128)S(1)}, f32[32,16,128]{2,1,0:T(8,128)S(1)}, u32[]{:S(2)}, u32[]{:S(2)}) %collective-permute-start.15) | collective-permute-done | bytes 262176 | tf_op jit(solution)/shard_map/ppermute | solution.py:197
  134.1 4.0 %collective-permute-done.14.before_ref = f32[32,16,128]{2,1,0:T(8,128)S(1)} collective-permute-done((f32[32,16,128]{2,1,0:T(8,128)S(1)}, f32[32,16,128]{2,1,0:T(8,128)S(1)}, u32[]{:S(2)}, u32[]{:S(2)}) %collective-permute-start.14) | collective-permute-done | bytes 262176 | tf_op jit(solution)/shard_map/ppermute | solution.py:197
  143.2 3.5 %collective-permute-start.17 = (f32[4,16,16,128]{3,2,1,0:T(8,128)S(1)}, f32[4,16,16,128]{3,2,1,0:T(8,128)S(1)}, u32[]{:S(2)}, u32[]{:S(2)}) collective-permute-start(f32[4,16,16,128]{3,2,1,0:T(8,128)S(1)} %get-tuple-element.38.low_ref), channel_id=1, source_target_pairs={{32,0},{64,32},{96,64},{128,96},{160,128},{192,160},{224,192},{256... | collective-permute-start | bytes 1572872 | tf_op jit(solution)/shard_map/ppermute | solution.py:197
  146.7 4.9 %collective-permute-done.16.before_ref = f32[4,16,16,128]{3,2,1,0:T(8,128)S(1)} collective-permute-done((f32[4,16,16,128]{3,2,1,0:T(8,128)S(1)}, f32[4,16,16,128]{3,2,1,0:T(8,128)S(1)}, u32[]{:S(2)}, u32[]{:S(2)}) %collective-permute-start.16) | collective-permute-done | bytes 524320 | tf_op jit(solution)/shard_map/ppermute | solution.py:197
  156.4 4.6 %collective-permute-start.18 = (f32[4,16,16,128]{3,2,1,0:T(8,128)S(1)}, f32[4,16,16,128]{3,2,1,0:T(8,128)S(1)}, u32[]{:S(2)}, u32[]{:S(2)}) collective-permute-start(f32[4,16,16,128]{3,2,1,0:T(8,128)S(1)} %get-tuple-element.39.high_ref), channel_id=1, source_target_pairs={{0,32},{32,64},{64,96},{96,128},{128,160},{160,192},{192,224},{224... | collective-permute-start | bytes 1572872 | tf_op jit(solution)/shard_map/ppermute | solution.py:197
  162.9 4.2 %collective-permute-done.18.before_ref = f32[4,16,16,128]{3,2,1,0:T(8,128)S(1)} collective-permute-done((f32[4,16,16,128]{3,2,1,0:T(8,128)S(1)}, f32[4,16,16,128]{3,2,1,0:T(8,128)S(1)}, u32[]{:S(2)}, u32[]{:S(2)}) %collective-permute-start.18) | collective-permute-done | bytes 524320 | tf_op jit(solution)/shard_map/ppermute | solution.py:197
  174.1 3.9 %collective-permute-start.20 = (f32[4,32,16,128]{3,2,1,0:T(8,128)S(1)}, f32[4,32,16,128]{3,2,1,0:T(8,128)S(1)}, u32[]{:S(2)}, u32[]{:S(2)}) collective-permute-start(f32[4,32,16,128]{3,2,1,0:T(8,128)S(1)} %shard_map.63.own_ref), channel_id=1, source_target_pairs={{0,1},{1,2},{2,3},{3,4},{4,5},{5,6},{6,7},{7,8},{8,9},{9,10},{10,1... | collective-permute-start | bytes 3145736 | tf_op jit(solution)/shard_map/ppermute | solution.py:197
  178.1 21.1 %collective-permute-done.21.after_ref = f32[4,32,16,128]{3,2,1,0:T(8,128)S(1)} collective-permute-done((f32[4,32,16,128]{3,2,1,0:T(8,128)S(1)}, f32[4,32,16,128]{3,2,1,0:T(8,128)S(1)}, u32[]{:S(2)}, u32[]{:S(2)}) %collective-permute-start.21) | collective-permute-done | bytes 1048608 | tf_op jit(solution)/shard_map/ppermute | solution.py:197
  199.2 4.0 %collective-permute-done.20.before_ref = f32[4,32,16,128]{3,2,1,0:T(8,128)S(1)} collective-permute-done((f32[4,32,16,128]{3,2,1,0:T(8,128)S(1)}, f32[4,32,16,128]{3,2,1,0:T(8,128)S(1)}, u32[]{:S(2)}, u32[]{:S(2)}) %collective-permute-start.20) | collective-permute-done | bytes 1048608 | tf_op jit(solution)/shard_map/ppermute | solution.py:197
  203.2 4.4 %shard_map.64 = (f32[8,16,128]{2,1,0:T(8,128)S(1)}, f32[8,16,128]{2,1,0:T(8,128)S(1)}, f32[8,16,128]{2,1,0:T(8,128)S(1)}, f32[8,16,128]{2,1,0:T(8,128)S(1)}) custom-call(s32[1]{0:T(128)} %bitcast.v_ref, f32[4,32,16,128]{3,2,1,0:T(8,128)S(1)} %collective-permute-done.20.before_ref, f32[4,32,16,128]{3,2,1,0:T(8,128)S(1)} %shard_map.63.own_ref, ...), custom_call_target="tpu_custom_call" | custom-call | tf_op jit(solution)/shard_map/pallas_call | solution.py:18
  211.7 5.5 %collective-permute-start.24 = (f32[8,16,128]{2,1,0:T(8,128)S(1)}, f32[8,16,128]{2,1,0:T(8,128)S(1)}, u32[]{:S(2)}, u32[]{:S(2)}) collective-permute-start(f32[8,16,128]{2,1,0:T(8,128)S(1)} %get-tuple-element.44), channel_id=1, source_target_pairs={{0,3},{1,0},{2,1},{3,2},{4,7},{5,4},{6,5},{7,6},{8,11},{9,8},{10,9... | collective-permute-start | bytes 196616 | tf_op jit(solution)/shard_map/ppermute | solution.py:203
  (52 shorter events, 64.2 us)
Async XLA Ops:
  1.2 28.0 %collective-permute-start.1 = (f32[32,16,128]{2,1,0:T(8,128)S(1)}, f32[32,16,128]{2,1,0:T(8,128)S(1)}, u32[]{:S(2)}, u32[]{:S(2)}) collective-permute-start(f32[32,16,128]{2,1,0:T(8,128)S(1)} %constant_dynamic-slice_fusion.own_ref.estimate_ref), channel_id=1, source_target_pairs={{1,0},{2,1},{3,2},{4,3},{5,4},{6,5},{7,6},{8,7},{9,8},{10,9},{11,1... | collective-permute-start | bytes 786440 | tf_op jit(solution)/shard_map/ppermute | solution.py:197
  12.5 16.8 %collective-permute-start = (f32[32,16,128]{2,1,0:T(8,128)S(1)}, f32[32,16,128]{2,1,0:T(8,128)S(1)}, u32[]{:S(2)}, u32[]{:S(2)}) collective-permute-start(f32[32,16,128]{2,1,0:T(8,128)S(1)} %constant_dynamic-slice_fusion.own_ref.estimate_ref), channel_id=1, source_target_pairs={{0,1},{1,2},{2,3},{3,4},{4,5},{5,6},{6,7},{7,8},{8,9},{9,10},{10,1... | collective-permute-start | bytes 786440 | tf_op jit(solution)/shard_map/ppermute | solution.py:197
  15.2 7.8 %collective-permute-start.4 = (f32[8,128]{1,0:T(8,128)S(1)}, f32[8,128]{1,0:T(8,128)S(1)}, u32[]{:S(2)}, u32[]{:S(2)}) collective-permute-start(f32[8,128]{1,0:T(8,128)S(1)} %pad.4.refs_0_), channel_id=1, source_target_pairs={{0,3},{1,0},{2,1},{3,2},{4,7},{5,4},{6,5},{7,6},{8,11},{9,8},{10,9... | collective-permute-start | bytes 12296 | tf_op jit(solution)/shard_map/ppermute | solution.py:203
  19.3 7.6 %collective-permute-start.2 = (f32[8,128]{1,0:T(8,128)S(1)}, f32[8,128]{1,0:T(8,128)S(1)}, u32[]{:S(2)}, u32[]{:S(2)}) collective-permute-start(f32[8,128]{1,0:T(8,128)S(1)} %pad.4.refs_0_), channel_id=1, source_target_pairs={{0,1},{1,2},{2,3},{3,0},{4,5},{5,6},{6,7},{7,4},{8,9},{9,10},{10,1... | collective-permute-start | bytes 12296 | tf_op jit(solution)/shard_map/ppermute | solution.py:203
  32.4 28.9 %collective-permute-start.5 = (f32[4,16,16,128]{3,2,1,0:T(8,128)S(1)}, f32[4,16,16,128]{3,2,1,0:T(8,128)S(1)}, u32[]{:S(2)}, u32[]{:S(2)}) collective-permute-start(f32[4,16,16,128]{3,2,1,0:T(8,128)S(1)} %get-tuple-element.26.high_ref), channel_id=1, source_target_pairs={{0,32},{32,64},{64,96},{96,128},{128,160},{160,192},{192,224},{224... | collective-permute-start | bytes 1572872 | tf_op jit(solution)/shard_map/ppermute | solution.py:197
  34.3 26.9 %collective-permute-start.6 = (f32[4,16,16,128]{3,2,1,0:T(8,128)S(1)}, f32[4,16,16,128]{3,2,1,0:T(8,128)S(1)}, u32[]{:S(2)}, u32[]{:S(2)}) collective-permute-start(f32[4,16,16,128]{3,2,1,0:T(8,128)S(1)} %get-tuple-element.27.low_ref), channel_id=1, source_target_pairs={{32,0},{64,32},{96,64},{128,96},{160,128},{192,160},{224,192},{256... | collective-permute-start | bytes 1572872 | tf_op jit(solution)/shard_map/ppermute | solution.py:197
  38.0 13.0 %collective-permute-start.7 = (f32[32,16,128]{2,1,0:T(8,128)S(1)}, f32[32,16,128]{2,1,0:T(8,128)S(1)}, u32[]{:S(2)}, u32[]{:S(2)}) collective-permute-start(f32[32,16,128]{2,1,0:T(8,128)S(1)} %get-tuple-element.31), channel_id=1, source_target_pairs={{0,1},{1,2},{2,3},{3,0},{4,5},{5,6},{6,7},{7,4},{8,9},{9,10},{10,1... | collective-permute-start | bytes 786440 | tf_op jit(solution)/shard_map/ppermute | solution.py:203
  40.0 21.3 %collective-permute-start.8 = (f32[32,16,128]{2,1,0:T(8,128)S(1)}, f32[32,16,128]{2,1,0:T(8,128)S(1)}, u32[]{:S(2)}, u32[]{:S(2)}) collective-permute-start(f32[32,16,128]{2,1,0:T(8,128)S(1)} %get-tuple-element.32), channel_id=1, source_target_pairs={{0,2},{1,3},{2,0},{3,1},{4,6},{5,7},{6,4},{7,5},{8,10},{9,11},{10,... | collective-permute-start | bytes 786440 | tf_op jit(solution)/shard_map/ppermute | solution.py:203
  44.4 16.8 %collective-permute-start.9 = (f32[32,16,128]{2,1,0:T(8,128)S(1)}, f32[32,16,128]{2,1,0:T(8,128)S(1)}, u32[]{:S(2)}, u32[]{:S(2)}) collective-permute-start(f32[32,16,128]{2,1,0:T(8,128)S(1)} %get-tuple-element.33), channel_id=1, source_target_pairs={{0,3},{1,0},{2,1},{3,2},{4,7},{5,4},{6,5},{7,6},{8,11},{9,8},{10,9... | collective-permute-start | bytes 786440 | tf_op jit(solution)/shard_map/ppermute | solution.py:203
  64.3 10.5 %collective-permute-start.10 = (f32[4,16,16,128]{3,2,1,0:T(8,128)S(1)}, f32[4,16,16,128]{3,2,1,0:T(8,128)S(1)}, u32[]{:S(2)}, u32[]{:S(2)}) collective-permute-start(f32[4,16,16,128]{3,2,1,0:T(8,128)S(1)} %get-tuple-element.34.high_ref), channel_id=1, source_target_pairs={{0,32},{32,64},{64,96},{96,128},{128,160},{160,192},{192,224},{224... | collective-permute-start | bytes 1572872 | tf_op jit(solution)/shard_map/ppermute | solution.py:197
  66.2 10.3 %collective-permute-start.11 = (f32[4,16,16,128]{3,2,1,0:T(8,128)S(1)}, f32[4,16,16,128]{3,2,1,0:T(8,128)S(1)}, u32[]{:S(2)}, u32[]{:S(2)}) collective-permute-start(f32[4,16,16,128]{3,2,1,0:T(8,128)S(1)} %get-tuple-element.35.low_ref), channel_id=1, source_target_pairs={{32,0},{64,32},{96,64},{128,96},{160,128},{192,160},{224,192},{256... | collective-permute-start | bytes 1572872 | tf_op jit(solution)/shard_map/ppermute | solution.py:197
  79.1 33.0 %collective-permute-start.13 = (f32[4,32,16,128]{3,2,1,0:T(8,128)S(1)}, f32[4,32,16,128]{3,2,1,0:T(8,128)S(1)}, u32[]{:S(2)}, u32[]{:S(2)}) collective-permute-start(f32[4,32,16,128]{3,2,1,0:T(8,128)S(1)} %shard_map.59.own_ref), channel_id=1, source_target_pairs={{1,0},{2,1},{3,2},{4,3},{5,4},{6,5},{7,6},{8,7},{9,8},{10,9},{11,1... | collective-permute-start | bytes 3145736 | tf_op jit(solution)/shard_map/ppermute | solution.py:197
  90.3 28.6 %collective-permute-start.12 = (f32[4,32,16,128]{3,2,1,0:T(8,128)S(1)}, f32[4,32,16,128]{3,2,1,0:T(8,128)S(1)}, u32[]{:S(2)}, u32[]{:S(2)}) collective-permute-start(f32[4,32,16,128]{3,2,1,0:T(8,128)S(1)} %shard_map.59.own_ref), channel_id=1, source_target_pairs={{0,1},{1,2},{2,3},{3,4},{4,5},{5,6},{6,7},{7,8},{8,9},{9,10},{10,1... | collective-permute-start | bytes 3145736 | tf_op jit(solution)/shard_map/ppermute | solution.py:197
  123.3 10.8 %collective-permute-start.15 = (f32[32,16,128]{2,1,0:T(8,128)S(1)}, f32[32,16,128]{2,1,0:T(8,128)S(1)}, u32[]{:S(2)}, u32[]{:S(2)}) collective-permute-start(f32[32,16,128]{2,1,0:T(8,128)S(1)} %shard_map.60.own_ref.estimate_ref), channel_id=1, source_target_pairs={{1,0},{2,1},{3,2},{4,3},{5,4},{6,5},{7,6},{8,7},{9,8},{10,9},{11,1... | collective-permute-start | bytes 786440 | tf_op jit(solution)/shard_map/ppermute | solution.py:197
  125.2 12.9 %collective-permute-start.14 = (f32[32,16,128]{2,1,0:T(8,128)S(1)}, f32[32,16,128]{2,1,0:T(8,128)S(1)}, u32[]{:S(2)}, u32[]{:S(2)}) collective-permute-start(f32[32,16,128]{2,1,0:T(8,128)S(1)} %shard_map.60.own_ref.estimate_ref), channel_id=1, source_target_pairs={{0,1},{1,2},{2,3},{3,4},{4,5},{5,6},{6,7},{7,8},{8,9},{9,10},{10,1... | collective-permute-start | bytes 786440 | tf_op jit(solution)/shard_map/ppermute | solution.py:197
  141.2 10.5 %collective-permute-start.16 = (f32[4,16,16,128]{3,2,1,0:T(8,128)S(1)}, f32[4,16,16,128]{3,2,1,0:T(8,128)S(1)}, u32[]{:S(2)}, u32[]{:S(2)}) collective-permute-start(f32[4,16,16,128]{3,2,1,0:T(8,128)S(1)} %get-tuple-element.37.high_ref), channel_id=1, source_target_pairs={{0,32},{32,64},{64,96},{96,128},{128,160},{160,192},{192,224},{224... | collective-permute-start | bytes 1572872 | tf_op jit(solution)/shard_map/ppermute | solution.py:197
  143.2 10.2 %collective-permute-start.17 = (f32[4,16,16,128]{3,2,1,0:T(8,128)S(1)}, f32[4,16,16,128]{3,2,1,0:T(8,128)S(1)}, u32[]{:S(2)}, u32[]{:S(2)}) collective-permute-start(f32[4,16,16,128]{3,2,1,0:T(8,128)S(1)} %get-tuple-element.38.low_ref), channel_id=1, source_target_pairs={{32,0},{64,32},{96,64},{128,96},{160,128},{192,160},{224,192},{256... | collective-permute-start | bytes 1572872 | tf_op jit(solution)/shard_map/ppermute | solution.py:197
  156.4 10.7 %collective-permute-start.18 = (f32[4,16,16,128]{3,2,1,0:T(8,128)S(1)}, f32[4,16,16,128]{3,2,1,0:T(8,128)S(1)}, u32[]{:S(2)}, u32[]{:S(2)}) collective-permute-start(f32[4,16,16,128]{3,2,1,0:T(8,128)S(1)} %get-tuple-element.39.high_ref), channel_id=1, source_target_pairs={{0,32},{32,64},{64,96},{96,128},{128,160},{160,192},{192,224},{224... | collective-permute-start | bytes 1572872 | tf_op jit(solution)/shard_map/ppermute | solution.py:197
  161.0 8.6 %collective-permute-start.19 = (f32[4,16,16,128]{3,2,1,0:T(8,128)S(1)}, f32[4,16,16,128]{3,2,1,0:T(8,128)S(1)}, u32[]{:S(2)}, u32[]{:S(2)}) collective-permute-start(f32[4,16,16,128]{3,2,1,0:T(8,128)S(1)} %get-tuple-element.40.low_ref), channel_id=1, source_target_pairs={{32,0},{64,32},{96,64},{128,96},{160,128},{192,160},{224,192},{256... | collective-permute-start | bytes 1572872 | tf_op jit(solution)/shard_map/ppermute | solution.py:197
  172.2 27.0 %collective-permute-start.21 = (f32[4,32,16,128]{3,2,1,0:T(8,128)S(1)}, f32[4,32,16,128]{3,2,1,0:T(8,128)S(1)}, u32[]{:S(2)}, u32[]{:S(2)}) collective-permute-start(f32[4,32,16,128]{3,2,1,0:T(8,128)S(1)} %shard_map.63.own_ref), channel_id=1, source_target_pairs={{1,0},{2,1},{3,2},{4,3},{5,4},{6,5},{7,6},{8,7},{9,8},{10,9},{11,1... | collective-permute-start | bytes 3145736 | tf_op jit(solution)/shard_map/ppermute | solution.py:197
  174.1 29.1 %collective-permute-start.20 = (f32[4,32,16,128]{3,2,1,0:T(8,128)S(1)}, f32[4,32,16,128]{3,2,1,0:T(8,128)S(1)}, u32[]{:S(2)}, u32[]{:S(2)}) collective-permute-start(f32[4,32,16,128]{3,2,1,0:T(8,128)S(1)} %shard_map.63.own_ref), channel_id=1, source_target_pairs={{0,1},{1,2},{2,3},{3,4},{4,5},{5,6},{6,7},{7,8},{8,9},{9,10},{10,1... | collective-permute-start | bytes 3145736 | tf_op jit(solution)/shard_map/ppermute | solution.py:197
  207.6 9.6 %collective-permute-start.22 = (f32[8,16,128]{2,1,0:T(8,128)S(1)}, f32[8,16,128]{2,1,0:T(8,128)S(1)}, u32[]{:S(2)}, u32[]{:S(2)}) collective-permute-start(f32[8,16,128]{2,1,0:T(8,128)S(1)} %get-tuple-element.42), channel_id=1, source_target_pairs={{0,1},{1,2},{2,3},{3,0},{4,5},{5,6},{6,7},{7,4},{8,9},{9,10},{10,1... | collective-permute-start | bytes 196616 | tf_op jit(solution)/shard_map/ppermute | solution.py:203
  209.8 9.1 %collective-permute-start.23 = (f32[8,16,128]{2,1,0:T(8,128)S(1)}, f32[8,16,128]{2,1,0:T(8,128)S(1)}, u32[]{:S(2)}, u32[]{:S(2)}) collective-permute-start(f32[8,16,128]{2,1,0:T(8,128)S(1)} %get-tuple-element.43), channel_id=1, source_target_pairs={{0,2},{1,3},{2,0},{3,1},{4,6},{5,7},{6,4},{7,5},{8,10},{9,11},{10,... | collective-permute-start | bytes 196616 | tf_op jit(solution)/shard_map/ppermute | solution.py:203
  211.7 8.6 %collective-permute-start.24 = (f32[8,16,128]{2,1,0:T(8,128)S(1)}, f32[8,16,128]{2,1,0:T(8,128)S(1)}, u32[]{:S(2)}, u32[]{:S(2)}) collective-permute-start(f32[8,16,128]{2,1,0:T(8,128)S(1)} %get-tuple-element.44), channel_id=1, source_target_pairs={{0,3},{1,0},{2,1},{3,2},{4,7},{5,4},{6,5},{7,6},{8,11},{9,8},{10,9... | collective-permute-start | bytes 196616 | tf_op jit(solution)/shard_map/ppermute | solution.py:203
  (6 other events, 18.3 us)

commit v3 on v2

v3 whole, which is shorter than its diff:
```python
import functools

import jax
import jax.numpy as jnp
from jax import lax
from jax.experimental import pallas as pl
from jax.experimental.pallas import tpu as pltpu
from jax.sharding import PartitionSpec as P

ITERS = 2
TAPS = 33
HALF = 16
LANES = 128
VMEM = pl.BlockSpec(memory_space=pltpu.VMEM)
SMEM = pl.BlockSpec(memory_space=pltpu.SMEM)


def call(kernel, outs, scratch, *args):
    specs = [SMEM if a.dtype == jnp.int32 else VMEM for a in args]
    return pl.pallas_call(
        kernel,
        out_shape=[jax.ShapeDtypeStruct(s, d) for s, d in outs],
        in_specs=specs,
        out_specs=[VMEM] * len(outs),
        scratch_shapes=scratch,
        compiler_params=pltpu.CompilerParams(vmem_limit_bytes=24 * 2**20),
    )(*args)


def split(value):
    high = value.astype(jnp.bfloat16)
    low = (value - high.astype(jnp.float32)).astype(jnp.bfloat16)
    return high, low


def deal_kernel(data_ref, out_ref):
    views, _, width, _ = out_ref.shape
    for view in range(views):
        out_ref[view] = data_ref[:, view * width : (view + 1) * width, :].astype(jnp.float32)


def prepare_kernel(spreads_ref, taps_x_ref, taps_y_ref, forward_ref, adjoint_ref):
    row = lax.broadcasted_iota(jnp.int32, (LANES, LANES), 0)
    column = lax.broadcasted_iota(jnp.int32, (LANES, LANES), 1)
    for view in range(spreads_ref.shape[0]):
        spreads = spreads_ref[view, :, :TAPS]
        normal = spreads / jnp.sum(spreads, axis=1, keepdims=True)
        for n, target in ((0, taps_x_ref), (1, taps_y_ref)):
            for t in range(TAPS):
                target[view, t] = jnp.broadcast_to(normal[n : n + 1, t : t + 1], (8, LANES))
        for target, offset in ((forward_ref, column - row + HALF), (adjoint_ref, row - column + HALF)):
            band = jnp.zeros((LANES, LANES), jnp.float32)
            for t in range(TAPS):
                tap = jnp.broadcast_to(normal[2:3, t : t + 1], (LANES, LANES))
                band = jnp.where(offset == t, tap, band)
            high, low = split(band)
            for k in (0, LANES):
                target[view, k : k + LANES, :LANES] = high
                target[view, k : k + LANES, LANES:] = low


def blur_y(ext_ref, rows, taps, adjoint):
    width = ext_ref.shape[1] - 2 * HALF
    groups = width // 8
    totals = [None] * len(taps)
    for rho in range(8):
        reach = 5 if rho == 0 else 4
        window = ext_ref[rows, pl.ds(rho, width + 8 * (reach - 1)), :]
        window = window.reshape(window.shape[0], groups + reach - 1, 8, LANES)
        for m in range(reach):
            s = rho + 8 * m
            t = s if adjoint else TAPS - 1 - s
            for n, tap in enumerate(taps):
                term = window[:, m : m + groups] * tap(t)
                totals[n] = term if totals[n] is None else totals[n] + term
    return [total.reshape(total.shape[0], width, LANES) for total in totals]


def blur_x(load, tap, adjoint, length, store):
    block = 16
    taps = [tap(t) for t in range(TAPS)]
    for first in range(0, length, block):
        totals = [None] * block
        for m in range(block + 2 * HALF):
            value = load(first + m)
            for i in range(block):
                s = m - i
                if 0 <= s < TAPS:
                    term = value * taps[s if adjoint else TAPS - 1 - s]
                    totals[i] = term if totals[i] is None else totals[i] + term
        for i in range(block):
            store(first + i, totals[i])


def blur_z(value, matrix):
    rows, width, _ = value.shape
    high, low = split(value.reshape(rows * width, LANES))
    product = jnp.dot(jnp.concatenate([high, low], axis=1), matrix, preferred_element_type=jnp.float32)
    return (product[:, :LANES] + product[:, LANES:]).reshape(rows, width, LANES)


def forward_y(ext_ref, taps_ref, out_ref):
    views, rows = out_ref.shape[:2]
    taps = [lambda t, view=view: taps_ref[view, t] for view in range(views)]
    block = 2

    @pl.loop(0, rows // block)
    def _(i):
        there = pl.ds(i * block, block)
        for view, blurred in enumerate(blur_y(ext_ref, there, taps, False)):
            out_ref[view, there] = blurred


def forward_y_kernel(before_ref, own_ref, after_ref, taps_ref, out_ref, ext_ref):
    width = own_ref.shape[1]
    ext_ref[:, :HALF, :] = before_ref[...]
    ext_ref[:, HALF : HALF + width, :] = own_ref[...]
    ext_ref[:, HALF + width :, :] = after_ref[...]
    forward_y(ext_ref, taps_ref, out_ref)


def first_forward_y_kernel(first, v_ref, tile_ref, across_ref, taps_ref, out_ref, ext_ref):
    rows, width = out_ref.shape[1:3]
    views = tile_ref.shape[1] // width
    there = pl.ds(first, rows)
    for n in range(3):
        place = v_ref[0] + n - 1
        inside = jnp.logical_and(place >= 0, place < views)

        @pl.when(inside)
        def _():
            columns = pl.ds(pl.multiple_of(place * width, width), width)
            ext_ref[:, n * width : (n + 1) * width, :] = tile_ref[there, columns, :]

        @pl.when(jnp.logical_not(inside))
        def _():
            ext_ref[:, n * width : (n + 1) * width, :] = across_ref[there]

    forward_y(ext_ref, taps_ref, out_ref)


def loop_x(refs, taps_ref, adjoint, out_ref):
    views, rows, width, _ = out_ref.shape
    groups = width // 8

    @pl.loop(0, views * groups)
    def _(n):
        view = n // groups
        columns = pl.ds(pl.multiple_of(lax.rem(n, groups) * 8, 8), 8)

        def load(m):
            return refs[m // HALF][view, m % HALF, columns, :]

        def store(i, value):
            out_ref[view, i, columns, :] = value

        blur_x(load, lambda t: taps_ref[view, t], adjoint, rows, store)


def ratio_kernel(first, before_ref, own_ref, after_ref, taps_ref, matrix_ref, data_ref, out_ref, mid_ref):
    loop_x((before_ref, own_ref, after_ref), taps_ref, False, mid_ref)
    views, rows = out_ref.shape[:2]
    for view in range(views):
        out_ref[view] = data_ref[view, pl.ds(first, rows)] / blur_z(mid_ref[view], matrix_ref[view])


def adjoint_x_kernel(before_ref, own_ref, after_ref, taps_ref, out_ref):
    loop_x((before_ref, own_ref, after_ref), taps_ref, True, out_ref)


def corrected(before_ref, own_ref, after_ref, taps_ref, matrix_ref, estimate_ref, ext_ref, mid_ref, total_ref):
    views, rows, width, _ = own_ref.shape
    block = 4

    @pl.loop(0, views)
    def _(view):
        ext_ref[:, :HALF, :] = before_ref[view]
        ext_ref[:, HALF : HALF + width, :] = own_ref[view]
        ext_ref[:, HALF + width :, :] = after_ref[view]

        @pl.loop(0, rows // block)
        def _(i):
            there = pl.ds(i * block, block)
            mid_ref[there] = blur_y(ext_ref, there, [lambda t: taps_ref[view, t]], True)[0]

        terms = jnp.log(blur_z(mid_ref[...], matrix_ref[view]))
        total_ref[...] = jnp.where(view == 0, terms, terms + total_ref[...])

    return estimate_ref[...] * jnp.exp(total_ref[...] / views)


def update_kernel(before_ref, own_ref, after_ref, taps_ref, matrix_ref, estimate_ref, out_ref, *scratch):
    out_ref[...] = corrected(before_ref, own_ref, after_ref, taps_ref, matrix_ref, estimate_ref, *scratch)


def collect_kernel(pieces_ref, out_ref):
    views, _, width, _ = pieces_ref.shape
    for view in range(views):
        out_ref[:, view * width : (view + 1) * width, :] = pieces_ref[view]


def shifted(size, by):
    return [(i, i + by) for i in range(size) if 0 <= i + by < size]


def onward(value, axes):
    return lax.ppermute(value, axes, shifted(lax.axis_size(axes), 1))


def back(value, axes):
    return lax.ppermute(value, axes, shifted(lax.axis_size(axes), -1))


def across(value):
    tiles, views = lax.axis_size("gy"), lax.axis_size("view")
    pairs = [(gy * views + views - 1, (gy + 1) * views) for gy in range(tiles - 1)]
    return lax.ppermute(value, ("gy", "view"), pairs + [(b, a) for a, b in pairs])


def exchanged(pieces):
    return lax.all_to_all(pieces, "view", 0, 0, tiled=True)


def body(estimate, views_data, spread_x, spread_y, spread_z):
    rows, width, depth = estimate.shape
    views = lax.axis_size("view")
    width = width // views
    half = rows // 2
    assert width == HALF and half == HALF and depth == LANES
    f32 = jnp.float32
    v = lax.axis_index("view")
    v_word = v.astype(jnp.int32).reshape(1)
    y = ("gy", "view")
    half_shape = ((views, half, width, depth), f32)
    taps_shape = ((views, TAPS, 8, LANES), f32)
    matrix_shape = ((views, 2 * LANES, 2 * LANES), jnp.bfloat16)
    part = ((half, width, depth), f32)
    ext = pltpu.VMEM((half, width + 2 * HALF, depth), f32)

    own = lax.dynamic_slice_in_dim(estimate, v * width, width, 1)
    spreads = jnp.concatenate([spread_x, spread_y, spread_z, jnp.ones((5, TAPS), f32)])
    spreads = exchanged(jnp.broadcast_to(jnp.pad(spreads, ((0, 0), (0, LANES - TAPS))), (views, 8, LANES)))
    beside = across(own)
    data = exchanged(call(deal_kernel, [((views, rows, width, depth), f32)], [], views_data[0])[0])
    taps_x, taps_y, forward_z, adjoint_z = call(
        prepare_kernel, [taps_shape, taps_shape, matrix_shape, matrix_shape], [], spreads
    )
    own = [own[:half], own[half:]]
    for step_number in range(ITERS):
        if step_number == 0:
            blurred = [
                call(functools.partial(first_forward_y_kernel, n * half), [half_shape], [ext], v_word, estimate, beside, taps_y)[0]
                for n in range(2)
            ]
        else:
            edges = [(onward(own[n], y), back(own[n], y)) for n in range(2)]
            blurred = [
                call(forward_y_kernel, [half_shape], [ext], edges[n][0], own[n], edges[n][1], taps_y)[0] for n in range(2)
            ]
        low, high = blurred
        before, after = onward(high, "gx"), back(low, "gx")
        mid = [pltpu.VMEM(*half_shape)]
        ratio_low = call(
            functools.partial(ratio_kernel, 0), [half_shape], mid, before, low, high, taps_x, forward_z, data
        )[0]
        ratio_high = call(
            functools.partial(ratio_kernel, half), [half_shape], mid, low, high, after, taps_x, forward_z, data
        )[0]
        before, after = onward(ratio_high, "gx"), back(ratio_low, "gx")
        high = call(adjoint_x_kernel, [half_shape], [], ratio_low, ratio_high, after, taps_x)[0]
        low = call(adjoint_x_kernel, [half_shape], [], before, ratio_low, ratio_high, taps_x)[0]
        ins = [(onward(value, y), value, back(value, y), taps_y, adjoint_z) for value in (low, high)]
        scratch = [ext, pltpu.VMEM(*part), pltpu.VMEM(*part)]
        own = [call(update_kernel, [part], scratch, *ins[n], own[n])[0] for n in range(2)]
    share = rows // views
    pieces = exchanged(jnp.concatenate(own).reshape(views, share, width, depth))
    return call(collect_kernel, [((share, width * views, depth), f32)], [], pieces)[0]


def solution(mesh):
    in_specs = (
        P("gx", "gy", None),
        P("view", "gx", "gy", None),
        P("view", None),
        P("view", None),
        P("view", None),
    )
    out_specs = P(("gx", "view"), "gy", None)
    return jax.shard_map(body, mesh=mesh, in_specs=in_specs, out_specs=out_specs, check_vma=False)
```

time: 222 us -> 179 us (0.81)
  waiting for transfers between devices: 101 us -> 39.1 us
  blocking collectives: 0 us -> 10.2 us
  Pallas kernels: 29.3 us -> 38.8 us
  starting transfers between devices: 88 us -> 81.2 us
  local copies, waits for them, and re-layouts: 1.92 us -> 8.41 us
    ppermute x25 -> x21, waiting for transfers between devices: 101 us -> 35.6 us  [the longest x10 28.7 us: onward(): return lax.ppermute(value, axes, shifted(lax.axis_size(axes), 1))]
    ppermute x25 -> x21, starting transfers between devices: 88 us -> 70.5 us  [the longest x10 35.1 us: back(): return lax.ppermute(value, axes, shifted(lax.axis_size(axes), -1))]
    all_to_all x0 -> x2, starting transfers between devices: none -> 10.8 us  [exchanged(): return lax.all_to_all(pieces, 'view', 0, 0, tiled=True)]
    all_to_all x0 -> x1, blocking collectives: none -> 10.2 us  [exchanged(): return lax.all_to_all(pieces, 'view', 0, 0, tiled=True)]
    pallas_call x11 -> x19, Pallas kernels: 29.3 us -> 38.8 us  [call(): pl.pallas_call(kernel, out_shape=[jax.ShapeDtypeStruct(s, d) for s, d in...]
    unnamed x10 -> x18, local copies, waits for them, and re-layouts: 1.82 us -> 5.74 us
    all_to_all x0 -> x2, waiting for transfers between devices: none -> 3.52 us  [exchanged(): return lax.all_to_all(pieces, 'view', 0, 0, tiled=True)]
  transfers between devices with their start and end apart: 25 -> 23, of which waited for: 18 -> 14; matrix products, arithmetic and copies ran while one was open for 0% -> 1% of each run, Pallas kernels for 1% -> 20%
where the time goes in v3:
time: 179 us; the launch traced here: 178 us
  starting transfers between devices  81.2 us (45%)
  waiting for transfers between devices  39.1 us (22%)
  Pallas kernels  38.8 us (22%)
  blocking collectives  10.2 us (6%)
  local copies, waits for them, and re-layouts  8.41 us (5%)
    pallas_call x19, Pallas kernels, call(): pl.pallas_call(kernel, out_shape=[jax.ShapeDtypeStruct(s, d) for s, d in...  38.8 us
    ppermute x10, starting transfers between devices, back(): return lax.ppermute(value, axes, shifted(lax.axis_size(axes), -1))  35.1 us
    ppermute x10, waiting for transfers between devices, onward(): return lax.ppermute(value, axes, shifted(lax.axis_size(axes), 1))  28.7 us
    ppermute x10, starting transfers between devices, onward(): return lax.ppermute(value, axes, shifted(lax.axis_size(axes), 1))  26.4 us
    all_to_all x2, starting transfers between devices, exchanged(): return lax.all_to_all(pieces, 'view', 0, 0, tiled=True)  10.8 us
    all_to_all x1, blocking collectives, exchanged(): return lax.all_to_all(pieces, 'view', 0, 0, tiled=True)  10.2 us
    ppermute x1, starting transfers between devices, across(): lax.ppermute(value, ('gy', 'view'), pairs + [(b, a) for a, b in pairs])  9 us
    unnamed x18, local copies, waits for them, and re-layouts  5.74 us
  transfers between devices with their start and end apart: 23, of which 14 were waited for; matrix products, arithmetic and copies ran while one was open for 1% of the time, Pallas kernels for 20%

profile of v3, /device:TPU:22, one launch (start us, length us, event | category | flops | bytes accessed | tf_op | source)
XLA Modules:
  0.0 178.2 jit_solution(9588606504879354172)
XLA Ops:
  1.4 7.3 %all-to-all-start = ((f32[4,8,128]{2,1,0:T(8,128)}), f32[4,8,128]{2,1,0:T(8,128)S(1)}, u32[]{:S(2)}, u32[]{:S(2)}) async-start(f32[4,8,128]{2,1,0:T(8,128)} %broadcast_in_dim.7), calls=%async_computation | async-start | bytes 32768 | tf_op jit(solution)/shard_map/all_to_all | solution.py:221
  10.7 3.5 %all-to-all-done.spreads_ref = f32[4,8,128]{2,1,0:T(8,128)S(1)} async-done(((f32[4,8,128]{2,1,0:T(8,128)}), f32[4,8,128]{2,1,0:T(8,128)S(1)}, u32[]{:S(2)}, u32[]{:S(2)}) %all-to-all-start) | async-done | bytes 16416 | tf_op jit(solution)/shard_map/all_to_all | solution.py:221
  14.3 3.5 %all-to-all-start.1 = ((f32[4,32,16,128]{3,2,1,0:T(8,128)}), f32[4,32,16,128]{3,2,1,0:T(8,128)S(1)}, u32[]{:S(2)}, u32[]{:S(2)}) async-start(f32[4,32,16,128]{3,2,1,0:T(8,128)} %shard_map.58), calls=%async_computation.1 | async-start | bytes 2097152 | tf_op jit(solution)/shard_map/all_to_all | solution.py:221
  18.8 9.0 %collective-permute-start = (f32[32,16,128]{2,1,0:T(8,128)S(1)}, f32[32,16,128]{2,1,0:T(8,128)S(1)}, u32[]{:S(2)}, u32[]{:S(2)}) collective-permute-start(f32[32,16,128]{2,1,0:T(8,128)S(1)} %constant_dynamic-slice_fusion.2), channel_id=1, source_target_pairs={{3,4},{7,8},{11,12},{15,16},{19,20},{23,24},{27,28},{4,3},{8,7},{1... | collective-permute-start | bytes 786440 | tf_op jit(solution)/shard_map/ppermute | solution.py:217
  46.4 2.7 %shard_map.59.after_ref.own_ref = f32[4,16,16,128]{3,2,1,0:T(8,128)S(1)} custom-call(f32[4,16,16,128]{3,2,1,0:T(8,128)S(1)} %copy-done.2, f32[4,16,16,128]{3,2,1,0:T(8,128)} %shard_map.57.own_ref.after_ref, f32[4,16,16,128]{3,2,1,0:T(8,128)S(1)} %copy-done.5, f32[4,33,8,128]{3,2,1,0:T(8,128)S(1)} %get-tuple-element.10.taps_ref, ...), custom_call_target="tpu_custom_call" | custom-call | tf_op jit(solution)/shard_map/pallas_call | solution.py:20
  49.1 4.2 %collective-permute-start.2 = (f32[4,16,16,128]{3,2,1,0:T(8,128)S(1)}, f32[4,16,16,128]{3,2,1,0:T(8,128)S(1)}, u32[]{:S(2)}, u32[]{:S(2)}) collective-permute-start(f32[4,16,16,128]{3,2,1,0:T(8,128)S(1)} %shard_map.59.after_ref.own_ref), channel_id=1, source_target_pairs={{0,32},{32,64},{64,96},{96,128},{128,160},{160,192},{192,224},{224... | collective-permute-start | bytes 1572872 | tf_op jit(solution)/shard_map/ppermute | solution.py:207
  53.3 2.9 %shard_map.60.own_ref.before_ref = f32[4,16,16,128]{3,2,1,0:T(8,128)S(1)} custom-call(f32[4,16,16,128]{3,2,1,0:T(8,128)} %collective-permute-done.3.before_ref, f32[4,16,16,128]{3,2,1,0:T(8,128)S(1)} %copy-done.2, f32[4,16,16,128]{3,2,1,0:T(8,128)} %shard_map.57.own_ref.after_ref, f32[4,33,8,128]{3,2,1,0:T(8,128)S(1)} %get-tuple-element.10.taps_ref, ...), custom_call_target="tpu_custom_call" | custom-call | tf_op jit(solution)/shard_map/pallas_call | solution.py:20
  62.3 5.8 %collective-permute-start.5 = (f32[4,16,16,128]{3,2,1,0:T(8,128)}, f32[4,16,16,128]{3,2,1,0:T(8,128)}, u32[]{:S(2)}, u32[]{:S(2)}) collective-permute-start(f32[4,16,16,128]{3,2,1,0:T(8,128)} %shard_map.61.own_ref), channel_id=1, source_target_pairs={{1,0},{2,1},{3,2},{4,3},{5,4},{6,5},{7,6},{8,7},{9,8},{10,9},{11,1... | collective-permute-start | bytes 1572872 | tf_op jit(solution)/shard_map/ppermute | solution.py:211
  72.2 6.0 %collective-permute-start.10 = (f32[4,16,16,128]{3,2,1,0:T(8,128)}, f32[4,16,16,128]{3,2,1,0:T(8,128)}, u32[]{:S(2)}, u32[]{:S(2)}) collective-permute-start(f32[4,16,16,128]{3,2,1,0:T(8,128)} %shard_map.64.own_ref), channel_id=1, source_target_pairs={{1,0},{2,1},{3,2},{4,3},{5,4},{6,5},{7,6},{8,7},{9,8},{10,9},{11,1... | collective-permute-start | bytes 1572872 | tf_op jit(solution)/shard_map/ppermute | solution.py:211
  81.2 5.6 %collective-permute-done.4.before_ref = f32[4,16,16,128]{3,2,1,0:T(8,128)} collective-permute-done((f32[4,16,16,128]{3,2,1,0:T(8,128)}, f32[4,16,16,128]{3,2,1,0:T(8,128)}, u32[]{:S(2)}, u32[]{:S(2)}) %collective-permute-start.4) | collective-permute-done | bytes 524320 | tf_op jit(solution)/shard_map/ppermute | solution.py:207
  86.8 3.8 %shard_map.62.own_ref.estimate_ref = f32[16,16,128]{2,1,0:T(8,128)S(1)} custom-call(f32[4,16,16,128]{3,2,1,0:T(8,128)} %collective-permute-done.4.before_ref, f32[4,16,16,128]{3,2,1,0:T(8,128)} %shard_map.61.own_ref, f32[4,16,16,128]{3,2,1,0:T(8,128)} %collective-permute-done.5.after_ref, f32[4,33,8,128]{3,2,1,0:T(8,128)S(1)} %get-tuple-element.9.taps_ref, ...), custom_call_target="tpu_custom_call" | custom-call | tf_op jit(solution)/shard_map/pallas_call | solution.py:20
  92.6 3.9 %collective-permute-start.6 = (f32[16,16,128]{2,1,0:T(8,128)S(1)}, f32[16,16,128]{2,1,0:T(8,128)S(1)}, u32[]{:S(2)}, u32[]{:S(2)}) collective-permute-start(f32[16,16,128]{2,1,0:T(8,128)S(1)} %shard_map.62.own_ref.estimate_ref), channel_id=1, source_target_pairs={{0,1},{1,2},{2,3},{3,4},{4,5},{5,6},{6,7},{7,8},{8,9},{9,10},{10,1... | collective-permute-start | bytes 393224 | tf_op jit(solution)/shard_map/ppermute | solution.py:207
  97.1 3.8 %shard_map.65.own_ref.estimate_ref = f32[16,16,128]{2,1,0:T(8,128)S(1)} custom-call(f32[4,16,16,128]{3,2,1,0:T(8,128)} %collective-permute-done.9.before_ref, f32[4,16,16,128]{3,2,1,0:T(8,128)} %shard_map.64.own_ref, f32[4,16,16,128]{3,2,1,0:T(8,128)} %collective-permute-done.10.after_ref, f32[4,33,8,128]{3,2,1,0:T(8,128)S(1)} %get-tuple-element.9.taps_ref, ...), custom_call_target="tpu_custom_call" | custom-call | tf_op jit(solution)/shard_map/pallas_call | solution.py:20
  101.0 3.5 %collective-permute-start.12 = (f32[16,16,128]{2,1,0:T(8,128)S(1)}, f32[16,16,128]{2,1,0:T(8,128)S(1)}, u32[]{:S(2)}, u32[]{:S(2)}) collective-permute-start(f32[16,16,128]{2,1,0:T(8,128)S(1)} %shard_map.65.own_ref.estimate_ref), channel_id=1, source_target_pairs={{1,0},{2,1},{3,2},{4,3},{5,4},{6,5},{7,6},{8,7},{9,8},{10,9},{11,1... | collective-permute-start | bytes 393224 | tf_op jit(solution)/shard_map/ppermute | solution.py:211
  110.1 3.3 %collective-permute-done.11.before_ref = f32[16,16,128]{2,1,0:T(8,128)S(1)} collective-permute-done((f32[16,16,128]{2,1,0:T(8,128)S(1)}, f32[16,16,128]{2,1,0:T(8,128)S(1)}, u32[]{:S(2)}, u32[]{:S(2)}) %collective-permute-start.11) | collective-permute-done | bytes 131104 | tf_op jit(solution)/shard_map/ppermute | solution.py:207
  118.5 3.9 %collective-permute-start.14 = (f32[4,16,16,128]{3,2,1,0:T(8,128)S(1)}, f32[4,16,16,128]{3,2,1,0:T(8,128)S(1)}, u32[]{:S(2)}, u32[]{:S(2)}) collective-permute-start(f32[4,16,16,128]{3,2,1,0:T(8,128)S(1)} %shard_map.67.after_ref.own_ref), channel_id=1, source_target_pairs={{0,32},{32,64},{64,96},{96,128},{128,160},{160,192},{192,224},{224... | collective-permute-start | bytes 1572872 | tf_op jit(solution)/shard_map/ppermute | solution.py:207
  122.4 2.9 %collective-permute-done.15.before_ref = f32[4,16,16,128]{3,2,1,0:T(8,128)S(1)} collective-permute-done((f32[4,16,16,128]{3,2,1,0:T(8,128)S(1)}, f32[4,16,16,128]{3,2,1,0:T(8,128)S(1)}, u32[]{:S(2)}, u32[]{:S(2)}) %collective-permute-start.15) | collective-permute-done | bytes 524320 | tf_op jit(solution)/shard_map/ppermute | solution.py:207
  132.2 4.1 %collective-permute-start.17 = (f32[4,16,16,128]{3,2,1,0:T(8,128)S(1)}, f32[4,16,16,128]{3,2,1,0:T(8,128)S(1)}, u32[]{:S(2)}, u32[]{:S(2)}) collective-permute-start(f32[4,16,16,128]{3,2,1,0:T(8,128)S(1)} %shard_map.69.own_ref), channel_id=1, source_target_pairs={{1,0},{2,1},{3,2},{4,3},{5,4},{6,5},{7,6},{8,7},{9,8},{10,9},{11,1... | collective-permute-start | bytes 1572872 | tf_op jit(solution)/shard_map/ppermute | solution.py:211
  139.6 6.0 %collective-permute-start.20 = (f32[4,16,16,128]{3,2,1,0:T(8,128)S(1)}, f32[4,16,16,128]{3,2,1,0:T(8,128)S(1)}, u32[]{:S(2)}, u32[]{:S(2)}) collective-permute-start(f32[4,16,16,128]{3,2,1,0:T(8,128)S(1)} %shard_map.71.own_ref), channel_id=1, source_target_pairs={{1,0},{2,1},{3,2},{4,3},{5,4},{6,5},{7,6},{8,7},{9,8},{10,9},{11,1... | collective-permute-start | bytes 1572872 | tf_op jit(solution)/shard_map/ppermute | solution.py:211
  148.9 6.3 %collective-permute-done.16.before_ref = f32[4,16,16,128]{3,2,1,0:T(8,128)S(1)} collective-permute-done((f32[4,16,16,128]{3,2,1,0:T(8,128)S(1)}, f32[4,16,16,128]{3,2,1,0:T(8,128)S(1)}, u32[]{:S(2)}, u32[]{:S(2)}) %collective-permute-start.16) | collective-permute-done | bytes 524320 | tf_op jit(solution)/shard_map/ppermute | solution.py:207
  155.2 2.5 %shard_map.70 = f32[16,16,128]{2,1,0:T(8,128)S(1)} custom-call(f32[4,16,16,128]{3,2,1,0:T(8,128)S(1)} %collective-permute-done.16.before_ref, f32[4,16,16,128]{3,2,1,0:T(8,128)S(1)} %shard_map.69.own_ref, f32[4,16,16,128]{3,2,1,0:T(8,128)S(1)} %collective-permute-done.17.after_ref, f32[4,33,8,128]{3,2,1,0:T(8,128)S(1)} %get-tuple-element.9.taps_ref, ...), custom_call_target="tpu_custom_call" | custom-call | tf_op jit(solution)/shard_map/pallas_call | solution.py:20
  158.8 6.0 %collective-permute-done.19.before_ref = f32[4,16,16,128]{3,2,1,0:T(8,128)S(1)} collective-permute-done((f32[4,16,16,128]{3,2,1,0:T(8,128)S(1)}, f32[4,16,16,128]{3,2,1,0:T(8,128)S(1)}, u32[]{:S(2)}, u32[]{:S(2)}) %collective-permute-start.19) | collective-permute-done | bytes 524320 | tf_op jit(solution)/shard_map/ppermute | solution.py:207
  164.8 2.5 %shard_map.72 = f32[16,16,128]{2,1,0:T(8,128)S(1)} custom-call(f32[4,16,16,128]{3,2,1,0:T(8,128)S(1)} %collective-permute-done.19.before_ref, f32[4,16,16,128]{3,2,1,0:T(8,128)S(1)} %shard_map.71.own_ref, f32[4,16,16,128]{3,2,1,0:T(8,128)S(1)} %collective-permute-done.20.after_ref, f32[4,33,8,128]{3,2,1,0:T(8,128)S(1)} %get-tuple-element.9.taps_ref, ...), custom_call_target="tpu_custom_call" | custom-call | tf_op jit(solution)/shard_map/pallas_call | solution.py:20
  167.3 10.2 %all_to_all.15.pieces_ref = f32[4,8,16,128]{3,2,1,0:T(8,128)S(1)} all-to-all(f32[4,8,16,128]{3,2,1,0:T(8,128)S(1)} %bitcast.4), channel_id=1, replica_groups=mesh['gx'=16,'gy'=8,'view'=4] {'view'}, dimensions={0} | all-to-all | bytes 524288 | tf_op jit(solution)/shard_map/all_to_all | solution.py:221
  (68 shorter events, 64.8 us)
Async XLA Ops:
  1.4 12.9 %all-to-all-start = ((f32[4,8,128]{2,1,0:T(8,128)}), f32[4,8,128]{2,1,0:T(8,128)S(1)}, u32[]{:S(2)}, u32[]{:S(2)}) async-start(f32[4,8,128]{2,1,0:T(8,128)} %broadcast_in_dim.7), calls=%async_computation | async-start | bytes 32768 | tf_op jit(solution)/shard_map/all_to_all | solution.py:221
  14.3 30.1 %all-to-all-start.1 = ((f32[4,32,16,128]{3,2,1,0:T(8,128)}), f32[4,32,16,128]{3,2,1,0:T(8,128)S(1)}, u32[]{:S(2)}, u32[]{:S(2)}) async-start(f32[4,32,16,128]{3,2,1,0:T(8,128)} %shard_map.58), calls=%async_computation.1 | async-start | bytes 2097152 | tf_op jit(solution)/shard_map/all_to_all | solution.py:221
  18.8 13.6 %collective-permute-start = (f32[32,16,128]{2,1,0:T(8,128)S(1)}, f32[32,16,128]{2,1,0:T(8,128)S(1)}, u32[]{:S(2)}, u32[]{:S(2)}) collective-permute-start(f32[32,16,128]{2,1,0:T(8,128)S(1)} %constant_dynamic-slice_fusion.2), channel_id=1, source_target_pairs={{3,4},{7,8},{11,12},{15,16},{19,20},{23,24},{27,28},{4,3},{8,7},{1... | collective-permute-start | bytes 786440 | tf_op jit(solution)/shard_map/ppermute | solution.py:217
  34.9 4.1 %copy-start.1 = (f32[4,16,16,128]{3,2,1,0:T(8,128)}, f32[4,16,16,128]{3,2,1,0:T(8,128)S(1)}, u32[]{:S(2)}) copy-start(f32[4,16,16,128]{3,2,1,0:T(8,128)S(1)} %shard_map.56.before_ref.own_ref) | copy-start | bytes 1572868
  34.9 8.6 %collective-permute-start.1 = (f32[4,16,16,128]{3,2,1,0:T(8,128)S(1)}, f32[4,16,16,128]{3,2,1,0:T(8,128)S(1)}, u32[]{:S(2)}, u32[]{:S(2)}) collective-permute-start(f32[4,16,16,128]{3,2,1,0:T(8,128)S(1)} %shard_map.56.before_ref.own_ref), channel_id=1, source_target_pairs={{32,0},{64,32},{96,64},{128,96},{160,128},{192,160},{224,192},{256... | collective-permute-start | bytes 1572872 | tf_op jit(solution)/shard_map/ppermute | solution.py:211
  39.0 14.3 %collective-permute-start.3 = (f32[4,16,16,128]{3,2,1,0:T(8,128)}, f32[4,16,16,128]{3,2,1,0:T(8,128)}, u32[]{:S(2)}, u32[]{:S(2)}) collective-permute-start(f32[4,16,16,128]{3,2,1,0:T(8,128)} %shard_map.57.own_ref.after_ref), channel_id=1, source_target_pairs={{0,32},{32,64},{64,96},{96,128},{128,160},{160,192},{192,224},{224... | collective-permute-start | bytes 1572872 | tf_op jit(solution)/shard_map/ppermute | solution.py:207
  49.1 11.1 %collective-permute-start.2 = (f32[4,16,16,128]{3,2,1,0:T(8,128)S(1)}, f32[4,16,16,128]{3,2,1,0:T(8,128)S(1)}, u32[]{:S(2)}, u32[]{:S(2)}) collective-permute-start(f32[4,16,16,128]{3,2,1,0:T(8,128)S(1)} %shard_map.59.after_ref.own_ref), channel_id=1, source_target_pairs={{0,32},{32,64},{64,96},{96,128},{128,160},{160,192},{192,224},{224... | collective-permute-start | bytes 1572872 | tf_op jit(solution)/shard_map/ppermute | solution.py:207
  56.2 13.9 %collective-permute-start.8 = (f32[4,16,16,128]{3,2,1,0:T(8,128)S(1)}, f32[4,16,16,128]{3,2,1,0:T(8,128)S(1)}, u32[]{:S(2)}, u32[]{:S(2)}) collective-permute-start(f32[4,16,16,128]{3,2,1,0:T(8,128)S(1)} %shard_map.60.own_ref.before_ref), channel_id=1, source_target_pairs={{32,0},{64,32},{96,64},{128,96},{160,128},{192,160},{224,192},{256... | collective-permute-start | bytes 1572872 | tf_op jit(solution)/shard_map/ppermute | solution.py:211
  62.3 18.8 %collective-permute-start.5 = (f32[4,16,16,128]{3,2,1,0:T(8,128)}, f32[4,16,16,128]{3,2,1,0:T(8,128)}, u32[]{:S(2)}, u32[]{:S(2)}) collective-permute-start(f32[4,16,16,128]{3,2,1,0:T(8,128)} %shard_map.61.own_ref), channel_id=1, source_target_pairs={{1,0},{2,1},{3,2},{4,3},{5,4},{6,5},{7,6},{8,7},{9,8},{10,9},{11,1... | collective-permute-start | bytes 1572872 | tf_op jit(solution)/shard_map/ppermute | solution.py:211
  68.1 18.7 %collective-permute-start.4 = (f32[4,16,16,128]{3,2,1,0:T(8,128)}, f32[4,16,16,128]{3,2,1,0:T(8,128)}, u32[]{:S(2)}, u32[]{:S(2)}) collective-permute-start(f32[4,16,16,128]{3,2,1,0:T(8,128)} %shard_map.61.own_ref), channel_id=1, source_target_pairs={{0,1},{1,2},{2,3},{3,4},{4,5},{5,6},{6,7},{7,8},{8,9},{9,10},{10,1... | collective-permute-start | bytes 1572872 | tf_op jit(solution)/shard_map/ppermute | solution.py:207
  72.2 24.3 %collective-permute-start.10 = (f32[4,16,16,128]{3,2,1,0:T(8,128)}, f32[4,16,16,128]{3,2,1,0:T(8,128)}, u32[]{:S(2)}, u32[]{:S(2)}) collective-permute-start(f32[4,16,16,128]{3,2,1,0:T(8,128)} %shard_map.64.own_ref), channel_id=1, source_target_pairs={{1,0},{2,1},{3,2},{4,3},{5,4},{6,5},{7,6},{8,7},{9,8},{10,9},{11,1... | collective-permute-start | bytes 1572872 | tf_op jit(solution)/shard_map/ppermute | solution.py:211
  78.2 18.9 %collective-permute-start.9 = (f32[4,16,16,128]{3,2,1,0:T(8,128)}, f32[4,16,16,128]{3,2,1,0:T(8,128)}, u32[]{:S(2)}, u32[]{:S(2)}) collective-permute-start(f32[4,16,16,128]{3,2,1,0:T(8,128)} %shard_map.64.own_ref), channel_id=1, source_target_pairs={{0,1},{1,2},{2,3},{3,4},{4,5},{5,6},{6,7},{7,8},{8,9},{9,10},{10,1... | collective-permute-start | bytes 1572872 | tf_op jit(solution)/shard_map/ppermute | solution.py:207
  90.7 16.2 %collective-permute-start.7 = (f32[16,16,128]{2,1,0:T(8,128)S(1)}, f32[16,16,128]{2,1,0:T(8,128)S(1)}, u32[]{:S(2)}, u32[]{:S(2)}) collective-permute-start(f32[16,16,128]{2,1,0:T(8,128)S(1)} %shard_map.62.own_ref.estimate_ref), channel_id=1, source_target_pairs={{1,0},{2,1},{3,2},{4,3},{5,4},{6,5},{7,6},{8,7},{9,8},{10,9},{11,1... | collective-permute-start | bytes 393224 | tf_op jit(solution)/shard_map/ppermute | solution.py:211
  92.6 14.2 %collective-permute-start.6 = (f32[16,16,128]{2,1,0:T(8,128)S(1)}, f32[16,16,128]{2,1,0:T(8,128)S(1)}, u32[]{:S(2)}, u32[]{:S(2)}) collective-permute-start(f32[16,16,128]{2,1,0:T(8,128)S(1)} %shard_map.62.own_ref.estimate_ref), channel_id=1, source_target_pairs={{0,1},{1,2},{2,3},{3,4},{4,5},{5,6},{6,7},{7,8},{8,9},{9,10},{10,1... | collective-permute-start | bytes 393224 | tf_op jit(solution)/shard_map/ppermute | solution.py:207
  101.0 9.2 %collective-permute-start.12 = (f32[16,16,128]{2,1,0:T(8,128)S(1)}, f32[16,16,128]{2,1,0:T(8,128)S(1)}, u32[]{:S(2)}, u32[]{:S(2)}) collective-permute-start(f32[16,16,128]{2,1,0:T(8,128)S(1)} %shard_map.65.own_ref.estimate_ref), channel_id=1, source_target_pairs={{1,0},{2,1},{3,2},{4,3},{5,4},{6,5},{7,6},{8,7},{9,8},{10,9},{11,1... | collective-permute-start | bytes 393224 | tf_op jit(solution)/shard_map/ppermute | solution.py:211
  104.4 9.0 %collective-permute-start.11 = (f32[16,16,128]{2,1,0:T(8,128)S(1)}, f32[16,16,128]{2,1,0:T(8,128)S(1)}, u32[]{:S(2)}, u32[]{:S(2)}) collective-permute-start(f32[16,16,128]{2,1,0:T(8,128)S(1)} %shard_map.65.own_ref.estimate_ref), channel_id=1, source_target_pairs={{0,1},{1,2},{2,3},{3,4},{4,5},{5,6},{6,7},{7,8},{8,9},{9,10},{10,1... | collective-permute-start | bytes 393224 | tf_op jit(solution)/shard_map/ppermute | solution.py:207
  108.2 8.6 %collective-permute-start.13 = (f32[4,16,16,128]{3,2,1,0:T(8,128)S(1)}, f32[4,16,16,128]{3,2,1,0:T(8,128)S(1)}, u32[]{:S(2)}, u32[]{:S(2)}) collective-permute-start(f32[4,16,16,128]{3,2,1,0:T(8,128)S(1)} %shard_map.63.before_ref.own_ref), channel_id=1, source_target_pairs={{32,0},{64,32},{96,64},{128,96},{160,128},{192,160},{224,192},{256... | collective-permute-start | bytes 1572872 | tf_op jit(solution)/shard_map/ppermute | solution.py:211
  114.7 10.5 %collective-permute-start.15 = (f32[4,16,16,128]{3,2,1,0:T(8,128)S(1)}, f32[4,16,16,128]{3,2,1,0:T(8,128)S(1)}, u32[]{:S(2)}, u32[]{:S(2)}) collective-permute-start(f32[4,16,16,128]{3,2,1,0:T(8,128)S(1)} %shard_map.66.own_ref.after_ref), channel_id=1, source_target_pairs={{0,32},{32,64},{64,96},{96,128},{128,160},{160,192},{192,224},{224... | collective-permute-start | bytes 1572872 | tf_op jit(solution)/shard_map/ppermute | solution.py:207
  118.5 12.4 %collective-permute-start.14 = (f32[4,16,16,128]{3,2,1,0:T(8,128)S(1)}, f32[4,16,16,128]{3,2,1,0:T(8,128)S(1)}, u32[]{:S(2)}, u32[]{:S(2)}) collective-permute-start(f32[4,16,16,128]{3,2,1,0:T(8,128)S(1)} %shard_map.67.after_ref.own_ref), channel_id=1, source_target_pairs={{0,32},{32,64},{64,96},{96,128},{128,160},{160,192},{192,224},{224... | collective-permute-start | bytes 1572872 | tf_op jit(solution)/shard_map/ppermute | solution.py:207
  126.9 11.4 %collective-permute-start.18 = (f32[4,16,16,128]{3,2,1,0:T(8,128)S(1)}, f32[4,16,16,128]{3,2,1,0:T(8,128)S(1)}, u32[]{:S(2)}, u32[]{:S(2)}) collective-permute-start(f32[4,16,16,128]{3,2,1,0:T(8,128)S(1)} %shard_map.68.own_ref.before_ref), channel_id=1, source_target_pairs={{32,0},{64,32},{96,64},{128,96},{160,128},{192,160},{224,192},{256... | collective-permute-start | bytes 1572872 | tf_op jit(solution)/shard_map/ppermute | solution.py:211
  132.2 16.7 %collective-permute-start.17 = (f32[4,16,16,128]{3,2,1,0:T(8,128)S(1)}, f32[4,16,16,128]{3,2,1,0:T(8,128)S(1)}, u32[]{:S(2)}, u32[]{:S(2)}) collective-permute-start(f32[4,16,16,128]{3,2,1,0:T(8,128)S(1)} %shard_map.69.own_ref), channel_id=1, source_target_pairs={{1,0},{2,1},{3,2},{4,3},{5,4},{6,5},{7,6},{8,7},{9,8},{10,9},{11,1... | collective-permute-start | bytes 1572872 | tf_op jit(solution)/shard_map/ppermute | solution.py:211
  136.3 18.9 %collective-permute-start.16 = (f32[4,16,16,128]{3,2,1,0:T(8,128)S(1)}, f32[4,16,16,128]{3,2,1,0:T(8,128)S(1)}, u32[]{:S(2)}, u32[]{:S(2)}) collective-permute-start(f32[4,16,16,128]{3,2,1,0:T(8,128)S(1)} %shard_map.69.own_ref), channel_id=1, source_target_pairs={{0,1},{1,2},{2,3},{3,4},{4,5},{5,6},{6,7},{7,8},{8,9},{9,10},{10,1... | collective-permute-start | bytes 1572872 | tf_op jit(solution)/shard_map/ppermute | solution.py:207
  139.6 19.2 %collective-permute-start.20 = (f32[4,16,16,128]{3,2,1,0:T(8,128)S(1)}, f32[4,16,16,128]{3,2,1,0:T(8,128)S(1)}, u32[]{:S(2)}, u32[]{:S(2)}) collective-permute-start(f32[4,16,16,128]{3,2,1,0:T(8,128)S(1)} %shard_map.71.own_ref), channel_id=1, source_target_pairs={{1,0},{2,1},{3,2},{4,3},{5,4},{6,5},{7,6},{8,7},{9,8},{10,9},{11,1... | collective-permute-start | bytes 1572872 | tf_op jit(solution)/shard_map/ppermute | solution.py:211
  145.7 19.1 %collective-permute-start.19 = (f32[4,16,16,128]{3,2,1,0:T(8,128)S(1)}, f32[4,16,16,128]{3,2,1,0:T(8,128)S(1)}, u32[]{:S(2)}, u32[]{:S(2)}) collective-permute-start(f32[4,16,16,128]{3,2,1,0:T(8,128)S(1)} %shard_map.71.own_ref), channel_id=1, source_target_pairs={{0,1},{1,2},{2,3},{3,4},{4,5},{5,6},{6,7},{7,8},{8,9},{9,10},{10,1... | collective-permute-start | bytes 1572872 | tf_op jit(solution)/shard_map/ppermute | solution.py:207
  (8 other events, 7.1 us)

commit v4 on v3

--- a/solution.py
+++ b/solution.py
@@ -23,7 +23,7 @@
         in_specs=specs,
         out_specs=[VMEM] * len(outs),
         scratch_shapes=scratch,
-        compiler_params=pltpu.CompilerParams(vmem_limit_bytes=24 * 2**20),
+        compiler_params=pltpu.CompilerParams(vmem_limit_bytes=10 * 2**20),
     )(*args)
 
 
@@ -39,15 +39,29 @@
         out_ref[view] = data_ref[:, view * width : (view + 1) * width, :].astype(jnp.float32)
 
 
-def prepare_kernel(spreads_ref, taps_x_ref, taps_y_ref, forward_ref, adjoint_ref):
+def part_kernel(v_ref, tile_ref, out_ref):
+    width = out_ref.shape[1]
+    out_ref[...] = tile_ref[:, pl.ds(pl.multiple_of(v_ref[0] * width, width), width), :]
+
+
+def normal_taps(spreads_ref, view):
+    spreads = spreads_ref[view, :, :TAPS]
+    return spreads / jnp.sum(spreads, axis=1, keepdims=True)
+
+
+def taps_kernel(spreads_ref, taps_x_ref, taps_y_ref):
+    for view in range(spreads_ref.shape[0]):
+        normal = normal_taps(spreads_ref, view)
+        for n, target in ((0, taps_x_ref), (1, taps_y_ref)):
+            for t in range(TAPS):
+                target[view, t] = jnp.broadcast_to(normal[n : n + 1, t : t + 1], (8, LANES))
+
+
+def matrices_kernel(spreads_ref, forward_ref, adjoint_ref):
     row = lax.broadcasted_iota(jnp.int32, (LANES, LANES), 0)
     column = lax.broadcasted_iota(jnp.int32, (LANES, LANES), 1)
     for view in range(spreads_ref.shape[0]):
-        spreads = spreads_ref[view, :, :TAPS]
-        normal = spreads / jnp.sum(spreads, axis=1, keepdims=True)
-        for n, target in ((0, taps_x_ref), (1, taps_y_ref)):
-            for t in range(TAPS):
-                target[view, t] = jnp.broadcast_to(normal[n : n + 1, t : t + 1], (8, LANES))
+        normal = normal_taps(spreads_ref, view)
         for target, offset in ((forward_ref, column - row + HALF), (adjoint_ref, row - column + HALF)):
             band = jnp.zeros((LANES, LANES), jnp.float32)
             for t in range(TAPS):
@@ -164,11 +178,25 @@
         out_ref[view] = data_ref[view, pl.ds(first, rows)] / blur_z(mid_ref[view], matrix_ref[view])
 
 
+def blurred_kernel(before_ref, own_ref, after_ref, taps_ref, matrix_ref, out_ref, mid_ref):
+    loop_x((before_ref, own_ref, after_ref), taps_ref, False, mid_ref)
+    for view in range(out_ref.shape[0]):
+        out_ref[view] = blur_z(mid_ref[view], matrix_ref[view])
+
+
+def divide_kernel(first, data_ref, blurred_ref, out_ref):
+    views, rows = out_ref.shape[:2]
+    for view in range(views):
+        out_ref[view] = data_ref[view, pl.ds(first, rows)] / blurred_ref[view]
+
+
 def adjoint_x_kernel(before_ref, own_ref, after_ref, taps_ref, out_ref):
     loop_x((before_ref, own_ref, after_ref), taps_ref, True, out_ref)
 
 
-def corrected(before_ref, own_ref, after_ref, taps_ref, matrix_ref, estimate_ref, ext_ref, mid_ref, total_ref):
+def update_kernel(
+    first, before_ref, own_ref, after_ref, taps_ref, matrix_ref, estimate_ref, out_ref, ext_ref, mid_ref, total_ref
+):
     views, rows, width, _ = own_ref.shape
     block = 4
 
@@ -186,11 +214,7 @@
         terms = jnp.log(blur_z(mid_ref[...], matrix_ref[view]))
         total_ref[...] = jnp.where(view == 0, terms, terms + total_ref[...])
 
-    return estimate_ref[...] * jnp.exp(total_ref[...] / views)
-
-
-def update_kernel(before_ref, own_ref, after_ref, taps_ref, matrix_ref, estimate_ref, out_ref, *scratch):
-    out_ref[...] = corrected(before_ref, own_ref, after_ref, taps_ref, matrix_ref, estimate_ref, *scratch)
+    out_ref[...] = estimate_ref[pl.ds(first, rows)] * jnp.exp(total_ref[...] / views)
 
 
 def collect_kernel(pieces_ref, out_ref):
@@ -237,15 +261,15 @@
     part = ((half, width, depth), f32)
     ext = pltpu.VMEM((half, width + 2 * HALF, depth), f32)
 
-    own = lax.dynamic_slice_in_dim(estimate, v * width, width, 1)
+    own = call(part_kernel, [((rows, width, depth), f32)], [], v_word, estimate)[0]
     spreads = jnp.concatenate([spread_x, spread_y, spread_z, jnp.ones((5, TAPS), f32)])
-    spreads = exchanged(jnp.broadcast_to(jnp.pad(spreads, ((0, 0), (0, LANES - TAPS))), (views, 8, LANES)))
+    spreads = jnp.broadcast_to(jnp.pad(spreads, ((0, 0), (0, LANES - TAPS))), (views, 8, LANES))
+    data = call(deal_kernel, [((views, rows, width, depth), f32)], [], views_data[0])[0]
+    spreads = exchanged(spreads)
+    data = exchanged(data)
     beside = across(own)
-    data = exchanged(call(deal_kernel, [((views, rows, width, depth), f32)], [], views_data[0])[0])
-    taps_x, taps_y, forward_z, adjoint_z = call(
-        prepare_kernel, [taps_shape, taps_shape, matrix_shape, matrix_shape], [], spreads
-    )
-    own = [own[:half], own[half:]]
+    taps_x, taps_y = call(taps_kernel, [taps_shape, taps_shape], [], spreads)
+    forward_z, adjoint_z = call(matrices_kernel, [matrix_shape, matrix_shape], [], spreads)
     for step_number in range(ITERS):
         if step_number == 0:
             blurred = [
@@ -260,18 +284,25 @@
         low, high = blurred
         before, after = onward(high, "gx"), back(low, "gx")
         mid = [pltpu.VMEM(*half_shape)]
-        ratio_low = call(
-            functools.partial(ratio_kernel, 0), [half_shape], mid, before, low, high, taps_x, forward_z, data
-        )[0]
-        ratio_high = call(
-            functools.partial(ratio_kernel, half), [half_shape], mid, low, high, after, taps_x, forward_z, data
-        )[0]
+        ratios = []
+        for first, rows_in in ((0, (before, low, high)), (half, (low, high, after))):
+            if step_number == 0:
+                blurred = call(blurred_kernel, [half_shape], mid, *rows_in, taps_x, forward_z)[0]
+                ratios.append(call(functools.partial(divide_kernel, first), [half_shape], [], data, blurred)[0])
+            else:
+                kernel = functools.partial(ratio_kernel, first)
+                ratios.append(call(kernel, [half_shape], mid, *rows_in, taps_x, forward_z, data)[0])
+        ratio_low, ratio_high = ratios
         before, after = onward(ratio_high, "gx"), back(ratio_low, "gx")
         high = call(adjoint_x_kernel, [half_shape], [], ratio_low, ratio_high, after, taps_x)[0]
         low = call(adjoint_x_kernel, [half_shape], [], before, ratio_low, ratio_high, taps_x)[0]
         ins = [(onward(value, y), value, back(value, y), taps_y, adjoint_z) for value in (low, high)]
         scratch = [ext, pltpu.VMEM(*part), pltpu.VMEM(*part)]
-        own = [call(update_kernel, [part], scratch, *ins[n], own[n])[0] for n in range(2)]
+        olds = [(0, own[0]), (0, own[1])] if step_number else [(0, own), (half, own)]
+        own = [
+            call(functools.partial(update_kernel, first), [part], scratch, *ins[n], old)[0]
+            for n, (first, old) in enumerate(olds)
+        ]
     share = rows // views
     pieces = exchanged(jnp.concatenate(own).reshape(views, share, width, depth))
     return call(collect_kernel, [((share, width * views, depth), f32)], [], pieces)[0]

time: 179 us -> 173 us (0.966)
  local copies, waits for them, and re-layouts: 8.41 us -> 4.17 us
  Pallas kernels: 38.8 us -> 34.8 us
    pallas_call x19 -> x23, Pallas kernels: 38.8 us -> 34.8 us  [call(): pl.pallas_call(kernel, out_shape=[jax.ShapeDtypeStruct(s, d) for s, d in...]
    ppermute x10, starting transfers between devices: 26.4 us -> 28.8 us  [onward(): return lax.ppermute(value, axes, shifted(lax.axis_size(axes), 1))]
    unnamed x18, local copies, waits for them, and re-layouts: 5.74 us -> 3.47 us
  transfers between devices with their start and end apart: 23 -> 23, of which waited for: 14 -> 15; matrix products, arithmetic and copies ran while one was open for 1% -> 0% of each run, Pallas kernels for 20% -> 18%
where the time goes in v4:
time: 173 us; the launch traced here: 172 us
  starting transfers between devices  82.1 us (47%)
  waiting for transfers between devices  40.3 us (23%)
  Pallas kernels  34.8 us (20%)
  blocking collectives  10.4 us (6%)
  local copies, waits for them, and re-layouts  4.17 us (2%)
    pallas_call x23, Pallas kernels, call(): pl.pallas_call(kernel, out_shape=[jax.ShapeDtypeStruct(s, d) for s, d in...  34.8 us
    ppermute x10, starting transfers between devices, back(): return lax.ppermute(value, axes, shifted(lax.axis_size(axes), -1))  33.5 us
    ppermute x10, starting transfers between devices, onward(): return lax.ppermute(value, axes, shifted(lax.axis_size(axes), 1))  28.8 us
    ppermute x10, waiting for transfers between devices, onward(): return lax.ppermute(value, axes, shifted(lax.axis_size(axes), 1))  27.1 us
    all_to_all x2, starting transfers between devices, exchanged(): return lax.all_to_all(pieces, 'view', 0, 0, tiled=True)  10.8 us
    all_to_all x1, blocking collectives, exchanged(): return lax.all_to_all(pieces, 'view', 0, 0, tiled=True)  10.4 us
    ppermute x1, starting transfers between devices, across(): lax.ppermute(value, ('gy', 'view'), pairs + [(b, a) for a, b in pairs])  8.99 us
    ppermute x10, waiting for transfers between devices, back(): return lax.ppermute(value, axes, shifted(lax.axis_size(axes), -1))  5.94 us
  transfers between devices with their start and end apart: 23, of which 15 were waited for; matrix products, arithmetic and copies ran while one was open for 0% of the time, Pallas kernels for 18%

profile of v4, /device:TPU:22, one launch (start us, length us, event | category | flops | bytes accessed | tf_op | source)
XLA Modules:
  0.0 172.3 jit_solution(435696162767041499)
XLA Ops:
  1.4 7.3 %all-to-all-start.1 = ((f32[4,8,128]{2,1,0:T(8,128)}), f32[4,8,128]{2,1,0:T(8,128)S(1)}, u32[]{:S(2)}, u32[]{:S(2)}) async-start(f32[4,8,128]{2,1,0:T(8,128)} %broadcast_in_dim.7), calls=%async_computation.1 | async-start | bytes 32768 | tf_op jit(solution)/shard_map/all_to_all | solution.py:245
  10.7 3.5 %all-to-all-done.1.spreads_ref = f32[4,8,128]{2,1,0:T(8,128)S(1)} async-done(((f32[4,8,128]{2,1,0:T(8,128)}), f32[4,8,128]{2,1,0:T(8,128)S(1)}, u32[]{:S(2)}, u32[]{:S(2)}) %all-to-all-start.1) | async-done | bytes 16416 | tf_op jit(solution)/shard_map/all_to_all | solution.py:245
  14.3 3.5 %all-to-all-start = ((f32[4,32,16,128]{3,2,1,0:T(8,128)}), f32[4,32,16,128]{3,2,1,0:T(8,128)S(1)}, u32[]{:S(2)}, u32[]{:S(2)}) async-start(f32[4,32,16,128]{3,2,1,0:T(8,128)} %shard_map.55), calls=%async_computation | async-start | bytes 2097152 | tf_op jit(solution)/shard_map/all_to_all | solution.py:245
  17.8 9.0 %collective-permute-start = (f32[32,16,128]{2,1,0:T(8,128)S(1)}, f32[32,16,128]{2,1,0:T(8,128)S(1)}, u32[]{:S(2)}, u32[]{:S(2)}) collective-permute-start(f32[32,16,128]{2,1,0:T(8,128)S(1)} %shard_map.56.estimate_ref), channel_id=1, source_target_pairs={{3,4},{7,8},{11,12},{15,16},{19,20},{23,24},{27,28},{4,3},{8,7},{1... | collective-permute-start | bytes 786440 | tf_op jit(solution)/shard_map/ppermute | solution.py:241
  27.6 3.8 %collective-permute-done.across_ref = f32[32,16,128]{2,1,0:T(8,128)S(1)} collective-permute-done((f32[32,16,128]{2,1,0:T(8,128)S(1)}, f32[32,16,128]{2,1,0:T(8,128)S(1)}, u32[]{:S(2)}, u32[]{:S(2)}) %collective-permute-start) | collective-permute-done | bytes 262176 | tf_op jit(solution)/shard_map/ppermute | solution.py:241
  36.8 2.4 %collective-permute-start.3 = (f32[4,16,16,128]{3,2,1,0:T(8,128)}, f32[4,16,16,128]{3,2,1,0:T(8,128)}, u32[]{:S(2)}, u32[]{:S(2)}) collective-permute-start(f32[4,16,16,128]{3,2,1,0:T(8,128)} %shard_map.59.own_ref.after_ref), channel_id=1, source_target_pairs={{0,32},{32,64},{64,96},{96,128},{128,160},{160,192},{192,224},{224... | collective-permute-start | bytes 1572872 | tf_op jit(solution)/shard_map/ppermute | solution.py:231
  41.4 2.7 %shard_map.61.blurred_ref = f32[4,16,16,128]{3,2,1,0:T(8,128)S(1)} custom-call(f32[4,16,16,128]{3,2,1,0:T(8,128)S(1)} %shard_map.58.before_ref.own_ref, f32[4,16,16,128]{3,2,1,0:T(8,128)} %shard_map.59.own_ref.after_ref, f32[4,16,16,128]{3,2,1,0:T(8,128)S(1)} %collective-permute-done.1.after_ref, f32[4,33,8,128]{3,2,1,0:T(8,128)S(1)} %get-tuple-element.10.taps_ref, ...), custom_call_target="tpu_custom_call" | custom-call | tf_op jit(solution)/shard_map/pallas_call | solution.py:20
  46.0 4.3 %collective-permute-start.2 = (f32[4,16,16,128]{3,2,1,0:T(8,128)S(1)}, f32[4,16,16,128]{3,2,1,0:T(8,128)S(1)}, u32[]{:S(2)}, u32[]{:S(2)}) collective-permute-start(f32[4,16,16,128]{3,2,1,0:T(8,128)S(1)} %shard_map.62.after_ref.own_ref), channel_id=1, source_target_pairs={{0,32},{32,64},{64,96},{96,128},{128,160},{160,192},{192,224},{224... | collective-permute-start | bytes 1572872 | tf_op jit(solution)/shard_map/ppermute | solution.py:231
  50.3 2.8 %shard_map.63.blurred_ref = f32[4,16,16,128]{3,2,1,0:T(8,128)S(1)} custom-call(f32[4,16,16,128]{3,2,1,0:T(8,128)} %collective-permute-done.3.before_ref, f32[4,16,16,128]{3,2,1,0:T(8,128)S(1)} %copy-done.2, f32[4,16,16,128]{3,2,1,0:T(8,128)} %shard_map.59.own_ref.after_ref, f32[4,33,8,128]{3,2,1,0:T(8,128)S(1)} %get-tuple-element.10.taps_ref, ...), custom_call_target="tpu_custom_call" | custom-call | tf_op jit(solution)/shard_map/pallas_call | solution.py:20
  58.5 5.8 %collective-permute-start.5 = (f32[4,16,16,128]{3,2,1,0:T(8,128)S(1)}, f32[4,16,16,128]{3,2,1,0:T(8,128)S(1)}, u32[]{:S(2)}, u32[]{:S(2)}) collective-permute-start(f32[4,16,16,128]{3,2,1,0:T(8,128)S(1)} %shard_map.65.own_ref), channel_id=1, source_target_pairs={{1,0},{2,1},{3,2},{4,3},{5,4},{6,5},{7,6},{8,7},{9,8},{10,9},{11,1... | collective-permute-start | bytes 1572872 | tf_op jit(solution)/shard_map/ppermute | solution.py:235
  67.6 6.0 %collective-permute-start.10 = (f32[4,16,16,128]{3,2,1,0:T(8,128)S(1)}, f32[4,16,16,128]{3,2,1,0:T(8,128)S(1)}, u32[]{:S(2)}, u32[]{:S(2)}) collective-permute-start(f32[4,16,16,128]{3,2,1,0:T(8,128)S(1)} %shard_map.68.own_ref), channel_id=1, source_target_pairs={{1,0},{2,1},{3,2},{4,3},{5,4},{6,5},{7,6},{8,7},{9,8},{10,9},{11,1... | collective-permute-start | bytes 1572872 | tf_op jit(solution)/shard_map/ppermute | solution.py:235
  76.7 6.5 %collective-permute-done.4.before_ref = f32[4,16,16,128]{3,2,1,0:T(8,128)S(1)} collective-permute-done((f32[4,16,16,128]{3,2,1,0:T(8,128)S(1)}, f32[4,16,16,128]{3,2,1,0:T(8,128)S(1)}, u32[]{:S(2)}, u32[]{:S(2)}) %collective-permute-start.4) | collective-permute-done | bytes 524320 | tf_op jit(solution)/shard_map/ppermute | solution.py:231
  83.2 2.5 %shard_map.66.own_ref.estimate_ref = f32[16,16,128]{2,1,0:T(8,128)S(1)} custom-call(f32[4,16,16,128]{3,2,1,0:T(8,128)S(1)} %collective-permute-done.4.before_ref, f32[4,16,16,128]{3,2,1,0:T(8,128)S(1)} %shard_map.65.own_ref, f32[4,16,16,128]{3,2,1,0:T(8,128)S(1)} %collective-permute-done.5.after_ref, f32[4,33,8,128]{3,2,1,0:T(8,128)S(1)} %get-tuple-element.9.taps_ref, ...), custom_call_target="tpu_custom_call" | custom-call | tf_op jit(solution)/shard_map/pallas_call | solution.py:20
  87.6 3.9 %collective-permute-start.6 = (f32[16,16,128]{2,1,0:T(8,128)S(1)}, f32[16,16,128]{2,1,0:T(8,128)S(1)}, u32[]{:S(2)}, u32[]{:S(2)}) collective-permute-start(f32[16,16,128]{2,1,0:T(8,128)S(1)} %shard_map.66.own_ref.estimate_ref), channel_id=1, source_target_pairs={{0,1},{1,2},{2,3},{3,4},{4,5},{5,6},{6,7},{7,8},{8,9},{9,10},{10,1... | collective-permute-start | bytes 393224 | tf_op jit(solution)/shard_map/ppermute | solution.py:231
  93.7 2.5 %shard_map.69.own_ref.estimate_ref = f32[16,16,128]{2,1,0:T(8,128)S(1)} custom-call(f32[4,16,16,128]{3,2,1,0:T(8,128)S(1)} %collective-permute-done.9.before_ref, f32[4,16,16,128]{3,2,1,0:T(8,128)S(1)} %shard_map.68.own_ref, f32[4,16,16,128]{3,2,1,0:T(8,128)S(1)} %collective-permute-done.10.after_ref, f32[4,33,8,128]{3,2,1,0:T(8,128)S(1)} %get-tuple-element.9.taps_ref, ...), custom_call_target="tpu_custom_call" | custom-call | tf_op jit(solution)/shard_map/pallas_call | solution.py:20
  98.1 3.9 %collective-permute-start.11 = (f32[16,16,128]{2,1,0:T(8,128)S(1)}, f32[16,16,128]{2,1,0:T(8,128)S(1)}, u32[]{:S(2)}, u32[]{:S(2)}) collective-permute-start(f32[16,16,128]{2,1,0:T(8,128)S(1)} %shard_map.69.own_ref.estimate_ref), channel_id=1, source_target_pairs={{0,1},{1,2},{2,3},{3,4},{4,5},{5,6},{6,7},{7,8},{8,9},{9,10},{10,1... | collective-permute-start | bytes 393224 | tf_op jit(solution)/shard_map/ppermute | solution.py:231
  113.7 4.7 %collective-permute-start.14 = (f32[4,16,16,128]{3,2,1,0:T(8,128)S(1)}, f32[4,16,16,128]{3,2,1,0:T(8,128)S(1)}, u32[]{:S(2)}, u32[]{:S(2)}) collective-permute-start(f32[4,16,16,128]{3,2,1,0:T(8,128)S(1)} %shard_map.71.after_ref.own_ref), channel_id=1, source_target_pairs={{0,32},{32,64},{64,96},{96,128},{128,160},{160,192},{192,224},{224... | collective-permute-start | bytes 1572872 | tf_op jit(solution)/shard_map/ppermute | solution.py:231
  126.0 4.0 %collective-permute-start.17 = (f32[4,16,16,128]{3,2,1,0:T(8,128)S(1)}, f32[4,16,16,128]{3,2,1,0:T(8,128)S(1)}, u32[]{:S(2)}, u32[]{:S(2)}) collective-permute-start(f32[4,16,16,128]{3,2,1,0:T(8,128)S(1)} %shard_map.73.own_ref), channel_id=1, source_target_pairs={{1,0},{2,1},{3,2},{4,3},{5,4},{6,5},{7,6},{8,7},{9,8},{10,9},{11,1... | collective-permute-start | bytes 1572872 | tf_op jit(solution)/shard_map/ppermute | solution.py:235
  133.3 6.0 %collective-permute-start.20 = (f32[4,16,16,128]{3,2,1,0:T(8,128)S(1)}, f32[4,16,16,128]{3,2,1,0:T(8,128)S(1)}, u32[]{:S(2)}, u32[]{:S(2)}) collective-permute-start(f32[4,16,16,128]{3,2,1,0:T(8,128)S(1)} %shard_map.75.own_ref), channel_id=1, source_target_pairs={{1,0},{2,1},{3,2},{4,3},{5,4},{6,5},{7,6},{8,7},{9,8},{10,9},{11,1... | collective-permute-start | bytes 1572872 | tf_op jit(solution)/shard_map/ppermute | solution.py:235
  142.7 6.2 %collective-permute-done.16.before_ref = f32[4,16,16,128]{3,2,1,0:T(8,128)S(1)} collective-permute-done((f32[4,16,16,128]{3,2,1,0:T(8,128)S(1)}, f32[4,16,16,128]{3,2,1,0:T(8,128)S(1)}, u32[]{:S(2)}, u32[]{:S(2)}) %collective-permute-start.16) | collective-permute-done | bytes 524320 | tf_op jit(solution)/shard_map/ppermute | solution.py:231
  148.9 2.5 %shard_map.74 = f32[16,16,128]{2,1,0:T(8,128)S(1)} custom-call(f32[4,16,16,128]{3,2,1,0:T(8,128)S(1)} %collective-permute-done.16.before_ref, f32[4,16,16,128]{3,2,1,0:T(8,128)S(1)} %shard_map.73.own_ref, f32[4,16,16,128]{3,2,1,0:T(8,128)S(1)} %collective-permute-done.17.after_ref, f32[4,33,8,128]{3,2,1,0:T(8,128)S(1)} %get-tuple-element.9.taps_ref, ...), custom_call_target="tpu_custom_call" | custom-call | tf_op jit(solution)/shard_map/pallas_call | solution.py:20
  152.8 5.9 %collective-permute-done.19.before_ref = f32[4,16,16,128]{3,2,1,0:T(8,128)S(1)} collective-permute-done((f32[4,16,16,128]{3,2,1,0:T(8,128)S(1)}, f32[4,16,16,128]{3,2,1,0:T(8,128)S(1)}, u32[]{:S(2)}, u32[]{:S(2)}) %collective-permute-start.19) | collective-permute-done | bytes 524320 | tf_op jit(solution)/shard_map/ppermute | solution.py:231
  158.7 2.5 %shard_map.76 = f32[16,16,128]{2,1,0:T(8,128)S(1)} custom-call(f32[4,16,16,128]{3,2,1,0:T(8,128)S(1)} %collective-permute-done.19.before_ref, f32[4,16,16,128]{3,2,1,0:T(8,128)S(1)} %shard_map.75.own_ref, f32[4,16,16,128]{3,2,1,0:T(8,128)S(1)} %collective-permute-done.20.after_ref, f32[4,33,8,128]{3,2,1,0:T(8,128)S(1)} %get-tuple-element.9.taps_ref, ...), custom_call_target="tpu_custom_call" | custom-call | tf_op jit(solution)/shard_map/pallas_call | solution.py:20
  161.2 10.4 %all_to_all.15.pieces_ref = f32[4,8,16,128]{3,2,1,0:T(8,128)S(1)} all-to-all(f32[4,8,16,128]{3,2,1,0:T(8,128)S(1)} %bitcast.4), channel_id=1, replica_groups=mesh['gx'=16,'gy'=8,'view'=4] {'view'}, dimensions={0} | all-to-all | bytes 524288 | tf_op jit(solution)/shard_map/all_to_all | solution.py:245
  (70 shorter events, 59.3 us)
Async XLA Ops:
  1.4 12.9 %all-to-all-start.1 = ((f32[4,8,128]{2,1,0:T(8,128)}), f32[4,8,128]{2,1,0:T(8,128)S(1)}, u32[]{:S(2)}, u32[]{:S(2)}) async-start(f32[4,8,128]{2,1,0:T(8,128)} %broadcast_in_dim.7), calls=%async_computation.1 | async-start | bytes 32768 | tf_op jit(solution)/shard_map/all_to_all | solution.py:245
  14.3 30.6 %all-to-all-start = ((f32[4,32,16,128]{3,2,1,0:T(8,128)}), f32[4,32,16,128]{3,2,1,0:T(8,128)S(1)}, u32[]{:S(2)}, u32[]{:S(2)}) async-start(f32[4,32,16,128]{3,2,1,0:T(8,128)} %shard_map.55), calls=%async_computation | async-start | bytes 2097152 | tf_op jit(solution)/shard_map/all_to_all | solution.py:245
  17.8 13.6 %collective-permute-start = (f32[32,16,128]{2,1,0:T(8,128)S(1)}, f32[32,16,128]{2,1,0:T(8,128)S(1)}, u32[]{:S(2)}, u32[]{:S(2)}) collective-permute-start(f32[32,16,128]{2,1,0:T(8,128)S(1)} %shard_map.56.estimate_ref), channel_id=1, source_target_pairs={{3,4},{7,8},{11,12},{15,16},{19,20},{23,24},{27,28},{4,3},{8,7},{1... | collective-permute-start | bytes 786440 | tf_op jit(solution)/shard_map/ppermute | solution.py:241
  32.8 8.6 %copy-start.1 = (f32[4,16,16,128]{3,2,1,0:T(8,128)}, f32[4,16,16,128]{3,2,1,0:T(8,128)S(1)}, u32[]{:S(2)}) copy-start(f32[4,16,16,128]{3,2,1,0:T(8,128)S(1)} %shard_map.58.before_ref.own_ref) | copy-start | bytes 1572868
  32.8 8.6 %collective-permute-start.1 = (f32[4,16,16,128]{3,2,1,0:T(8,128)S(1)}, f32[4,16,16,128]{3,2,1,0:T(8,128)S(1)}, u32[]{:S(2)}, u32[]{:S(2)}) collective-permute-start(f32[4,16,16,128]{3,2,1,0:T(8,128)S(1)} %shard_map.58.before_ref.own_ref), channel_id=1, source_target_pairs={{32,0},{64,32},{96,64},{128,96},{160,128},{192,160},{224,192},{256... | collective-permute-start | bytes 1572872 | tf_op jit(solution)/shard_map/ppermute | solution.py:235
  36.8 13.4 %collective-permute-start.3 = (f32[4,16,16,128]{3,2,1,0:T(8,128)}, f32[4,16,16,128]{3,2,1,0:T(8,128)}, u32[]{:S(2)}, u32[]{:S(2)}) collective-permute-start(f32[4,16,16,128]{3,2,1,0:T(8,128)} %shard_map.59.own_ref.after_ref), channel_id=1, source_target_pairs={{0,32},{32,64},{64,96},{96,128},{128,160},{160,192},{192,224},{224... | collective-permute-start | bytes 1572872 | tf_op jit(solution)/shard_map/ppermute | solution.py:231
  46.0 11.2 %collective-permute-start.2 = (f32[4,16,16,128]{3,2,1,0:T(8,128)S(1)}, f32[4,16,16,128]{3,2,1,0:T(8,128)S(1)}, u32[]{:S(2)}, u32[]{:S(2)}) collective-permute-start(f32[4,16,16,128]{3,2,1,0:T(8,128)S(1)} %shard_map.62.after_ref.own_ref), channel_id=1, source_target_pairs={{0,32},{32,64},{64,96},{96,128},{128,160},{160,192},{192,224},{224... | collective-permute-start | bytes 1572872 | tf_op jit(solution)/shard_map/ppermute | solution.py:231
  53.2 13.0 %collective-permute-start.8 = (f32[4,16,16,128]{3,2,1,0:T(8,128)S(1)}, f32[4,16,16,128]{3,2,1,0:T(8,128)S(1)}, u32[]{:S(2)}, u32[]{:S(2)}) collective-permute-start(f32[4,16,16,128]{3,2,1,0:T(8,128)S(1)} %shard_map.64.own_ref.before_ref), channel_id=1, source_target_pairs={{32,0},{64,32},{96,64},{128,96},{160,128},{192,160},{224,192},{256... | collective-permute-start | bytes 1572872 | tf_op jit(solution)/shard_map/ppermute | solution.py:235
  58.5 18.2 %collective-permute-start.5 = (f32[4,16,16,128]{3,2,1,0:T(8,128)S(1)}, f32[4,16,16,128]{3,2,1,0:T(8,128)S(1)}, u32[]{:S(2)}, u32[]{:S(2)}) collective-permute-start(f32[4,16,16,128]{3,2,1,0:T(8,128)S(1)} %shard_map.65.own_ref), channel_id=1, source_target_pairs={{1,0},{2,1},{3,2},{4,3},{5,4},{6,5},{7,6},{8,7},{9,8},{10,9},{11,1... | collective-permute-start | bytes 1572872 | tf_op jit(solution)/shard_map/ppermute | solution.py:235
  64.3 18.9 %collective-permute-start.4 = (f32[4,16,16,128]{3,2,1,0:T(8,128)S(1)}, f32[4,16,16,128]{3,2,1,0:T(8,128)S(1)}, u32[]{:S(2)}, u32[]{:S(2)}) collective-permute-start(f32[4,16,16,128]{3,2,1,0:T(8,128)S(1)} %shard_map.65.own_ref), channel_id=1, source_target_pairs={{0,1},{1,2},{2,3},{3,4},{4,5},{5,6},{6,7},{7,8},{8,9},{9,10},{10,1... | collective-permute-start | bytes 1572872 | tf_op jit(solution)/shard_map/ppermute | solution.py:231
  67.6 23.9 %collective-permute-start.10 = (f32[4,16,16,128]{3,2,1,0:T(8,128)S(1)}, f32[4,16,16,128]{3,2,1,0:T(8,128)S(1)}, u32[]{:S(2)}, u32[]{:S(2)}) collective-permute-start(f32[4,16,16,128]{3,2,1,0:T(8,128)S(1)} %shard_map.68.own_ref), channel_id=1, source_target_pairs={{1,0},{2,1},{3,2},{4,3},{5,4},{6,5},{7,6},{8,7},{9,8},{10,9},{11,1... | collective-permute-start | bytes 1572872 | tf_op jit(solution)/shard_map/ppermute | solution.py:235
  73.7 20.1 %collective-permute-start.9 = (f32[4,16,16,128]{3,2,1,0:T(8,128)S(1)}, f32[4,16,16,128]{3,2,1,0:T(8,128)S(1)}, u32[]{:S(2)}, u32[]{:S(2)}) collective-permute-start(f32[4,16,16,128]{3,2,1,0:T(8,128)S(1)} %shard_map.68.own_ref), channel_id=1, source_target_pairs={{0,1},{1,2},{2,3},{3,4},{4,5},{5,6},{6,7},{7,8},{8,9},{9,10},{10,1... | collective-permute-start | bytes 1572872 | tf_op jit(solution)/shard_map/ppermute | solution.py:231
  85.7 16.4 %collective-permute-start.7 = (f32[16,16,128]{2,1,0:T(8,128)S(1)}, f32[16,16,128]{2,1,0:T(8,128)S(1)}, u32[]{:S(2)}, u32[]{:S(2)}) collective-permute-start(f32[16,16,128]{2,1,0:T(8,128)S(1)} %shard_map.66.own_ref.estimate_ref), channel_id=1, source_target_pairs={{1,0},{2,1},{3,2},{4,3},{5,4},{6,5},{7,6},{8,7},{9,8},{10,9},{11,1... | collective-permute-start | bytes 393224 | tf_op jit(solution)/shard_map/ppermute | solution.py:235
  87.6 14.5 %collective-permute-start.6 = (f32[16,16,128]{2,1,0:T(8,128)S(1)}, f32[16,16,128]{2,1,0:T(8,128)S(1)}, u32[]{:S(2)}, u32[]{:S(2)}) collective-permute-start(f32[16,16,128]{2,1,0:T(8,128)S(1)} %shard_map.66.own_ref.estimate_ref), channel_id=1, source_target_pairs={{0,1},{1,2},{2,3},{3,4},{4,5},{5,6},{6,7},{7,8},{8,9},{9,10},{10,1... | collective-permute-start | bytes 393224 | tf_op jit(solution)/shard_map/ppermute | solution.py:231
  96.2 9.2 %collective-permute-start.12 = (f32[16,16,128]{2,1,0:T(8,128)S(1)}, f32[16,16,128]{2,1,0:T(8,128)S(1)}, u32[]{:S(2)}, u32[]{:S(2)}) collective-permute-start(f32[16,16,128]{2,1,0:T(8,128)S(1)} %shard_map.69.own_ref.estimate_ref), channel_id=1, source_target_pairs={{1,0},{2,1},{3,2},{4,3},{5,4},{6,5},{7,6},{8,7},{9,8},{10,9},{11,1... | collective-permute-start | bytes 393224 | tf_op jit(solution)/shard_map/ppermute | solution.py:235
  98.1 9.0 %collective-permute-start.11 = (f32[16,16,128]{2,1,0:T(8,128)S(1)}, f32[16,16,128]{2,1,0:T(8,128)S(1)}, u32[]{:S(2)}, u32[]{:S(2)}) collective-permute-start(f32[16,16,128]{2,1,0:T(8,128)S(1)} %shard_map.69.own_ref.estimate_ref), channel_id=1, source_target_pairs={{0,1},{1,2},{2,3},{3,4},{4,5},{5,6},{6,7},{7,8},{8,9},{9,10},{10,1... | collective-permute-start | bytes 393224 | tf_op jit(solution)/shard_map/ppermute | solution.py:231
  103.4 8.6 %collective-permute-start.13 = (f32[4,16,16,128]{3,2,1,0:T(8,128)S(1)}, f32[4,16,16,128]{3,2,1,0:T(8,128)S(1)}, u32[]{:S(2)}, u32[]{:S(2)}) collective-permute-start(f32[4,16,16,128]{3,2,1,0:T(8,128)S(1)} %shard_map.67.before_ref.own_ref), channel_id=1, source_target_pairs={{32,0},{64,32},{96,64},{128,96},{160,128},{192,160},{224,192},{256... | collective-permute-start | bytes 1572872 | tf_op jit(solution)/shard_map/ppermute | solution.py:235
  108.5 10.5 %collective-permute-start.15 = (f32[4,16,16,128]{3,2,1,0:T(8,128)S(1)}, f32[4,16,16,128]{3,2,1,0:T(8,128)S(1)}, u32[]{:S(2)}, u32[]{:S(2)}) collective-permute-start(f32[4,16,16,128]{3,2,1,0:T(8,128)S(1)} %shard_map.70.own_ref.after_ref), channel_id=1, source_target_pairs={{0,32},{32,64},{64,96},{96,128},{128,160},{160,192},{192,224},{224... | collective-permute-start | bytes 1572872 | tf_op jit(solution)/shard_map/ppermute | solution.py:231
  113.7 11.0 %collective-permute-start.14 = (f32[4,16,16,128]{3,2,1,0:T(8,128)S(1)}, f32[4,16,16,128]{3,2,1,0:T(8,128)S(1)}, u32[]{:S(2)}, u32[]{:S(2)}) collective-permute-start(f32[4,16,16,128]{3,2,1,0:T(8,128)S(1)} %shard_map.71.after_ref.own_ref), channel_id=1, source_target_pairs={{0,32},{32,64},{64,96},{96,128},{128,160},{160,192},{192,224},{224... | collective-permute-start | bytes 1572872 | tf_op jit(solution)/shard_map/ppermute | solution.py:231
  120.6 11.4 %collective-permute-start.18 = (f32[4,16,16,128]{3,2,1,0:T(8,128)S(1)}, f32[4,16,16,128]{3,2,1,0:T(8,128)S(1)}, u32[]{:S(2)}, u32[]{:S(2)}) collective-permute-start(f32[4,16,16,128]{3,2,1,0:T(8,128)S(1)} %shard_map.72.own_ref.before_ref), channel_id=1, source_target_pairs={{32,0},{64,32},{96,64},{128,96},{160,128},{192,160},{224,192},{256... | collective-permute-start | bytes 1572872 | tf_op jit(solution)/shard_map/ppermute | solution.py:235
  126.0 16.7 %collective-permute-start.17 = (f32[4,16,16,128]{3,2,1,0:T(8,128)S(1)}, f32[4,16,16,128]{3,2,1,0:T(8,128)S(1)}, u32[]{:S(2)}, u32[]{:S(2)}) collective-permute-start(f32[4,16,16,128]{3,2,1,0:T(8,128)S(1)} %shard_map.73.own_ref), channel_id=1, source_target_pairs={{1,0},{2,1},{3,2},{4,3},{5,4},{6,5},{7,6},{8,7},{9,8},{10,9},{11,1... | collective-permute-start | bytes 1572872 | tf_op jit(solution)/shard_map/ppermute | solution.py:235
  130.0 18.9 %collective-permute-start.16 = (f32[4,16,16,128]{3,2,1,0:T(8,128)S(1)}, f32[4,16,16,128]{3,2,1,0:T(8,128)S(1)}, u32[]{:S(2)}, u32[]{:S(2)}) collective-permute-start(f32[4,16,16,128]{3,2,1,0:T(8,128)S(1)} %shard_map.73.own_ref), channel_id=1, source_target_pairs={{0,1},{1,2},{2,3},{3,4},{4,5},{5,6},{6,7},{7,8},{8,9},{9,10},{10,1... | collective-permute-start | bytes 1572872 | tf_op jit(solution)/shard_map/ppermute | solution.py:231
  133.3 19.5 %collective-permute-start.20 = (f32[4,16,16,128]{3,2,1,0:T(8,128)S(1)}, f32[4,16,16,128]{3,2,1,0:T(8,128)S(1)}, u32[]{:S(2)}, u32[]{:S(2)}) collective-permute-start(f32[4,16,16,128]{3,2,1,0:T(8,128)S(1)} %shard_map.75.own_ref), channel_id=1, source_target_pairs={{1,0},{2,1},{3,2},{4,3},{5,4},{6,5},{7,6},{8,7},{9,8},{10,9},{11,1... | collective-permute-start | bytes 1572872 | tf_op jit(solution)/shard_map/ppermute | solution.py:235
  139.4 19.3 %collective-permute-start.19 = (f32[4,16,16,128]{3,2,1,0:T(8,128)S(1)}, f32[4,16,16,128]{3,2,1,0:T(8,128)S(1)}, u32[]{:S(2)}, u32[]{:S(2)}) collective-permute-start(f32[4,16,16,128]{3,2,1,0:T(8,128)S(1)} %shard_map.75.own_ref), channel_id=1, source_target_pairs={{0,1},{1,2},{2,3},{3,4},{4,5},{5,6},{6,7},{7,8},{8,9},{9,10},{10,1... | collective-permute-start | bytes 1572872 | tf_op jit(solution)/shard_map/ppermute | solution.py:231
  (8 other events, 16.3 us)

commit v5 on v4

v5 whole, which is shorter than its diff:
```python
import functools

import jax
import jax.numpy as jnp
from jax import lax
from jax.experimental import pallas as pl
from jax.experimental.pallas import tpu as pltpu
from jax.sharding import PartitionSpec as P

ITERS = 2
TAPS = 33
HALF = 16
LANES = 128
VMEM = pl.BlockSpec(memory_space=pltpu.VMEM)
SMEM = pl.BlockSpec(memory_space=pltpu.SMEM)


def call(kernel, outs, scratch, *args):
    specs = [SMEM if a.dtype == jnp.int32 else VMEM for a in args]
    return pl.pallas_call(
        kernel,
        out_shape=[jax.ShapeDtypeStruct(s, d) for s, d in outs],
        in_specs=specs,
        out_specs=[VMEM] * len(outs),
        scratch_shapes=scratch,
        compiler_params=pltpu.CompilerParams(vmem_limit_bytes=10 * 2**20),
    )(*args)


def split(value):
    high = value.astype(jnp.bfloat16)
    low = (value - high.astype(jnp.float32)).astype(jnp.bfloat16)
    return high, low


def deal_kernel(data_ref, out_ref):
    views, _, width, _ = out_ref.shape
    for view in range(views):
        out_ref[view] = data_ref[:, view * width : (view + 1) * width, :].astype(jnp.float32)


def part_kernel(v_ref, tile_ref, out_ref):
    width = out_ref.shape[1]
    out_ref[...] = tile_ref[:, pl.ds(pl.multiple_of(v_ref[0] * width, width), width), :]


def normal_taps(spreads_ref, view):
    spreads = spreads_ref[view, :, :TAPS]
    return spreads / jnp.sum(spreads, axis=1, keepdims=True)


def band(taps, offset):
    matrix = jnp.zeros(offset.shape, jnp.float32)
    for t in range(TAPS):
        matrix = jnp.where(offset == t, jnp.broadcast_to(taps[:, t : t + 1], offset.shape), matrix)
    return matrix


def bands(taps, adjoint):
    row = lax.broadcasted_iota(jnp.int32, (HALF, 9 * HALF), 0)
    lane = lax.broadcasted_iota(jnp.int32, (HALF, 9 * HALF), 1)
    first, last = lane < 3 * HALF, lane >= 6 * HALF
    column = jnp.where(first, lane, jnp.where(last, lane - 6 * HALF, lane - 3 * HALF))
    matrix = band(taps, column - row if adjoint else row - column + 2 * HALF)
    high = matrix.astype(jnp.bfloat16).astype(jnp.float32)
    return jnp.where(jnp.logical_or(first, last), high, matrix - high).astype(jnp.bfloat16)


def forward_bands_kernel(spreads_ref, x_ref, y_ref):
    for view in range(spreads_ref.shape[0]):
        normal = normal_taps(spreads_ref, view)
        x_ref[view] = bands(normal[0:1], False)
        y_ref[view * HALF : (view + 1) * HALF] = bands(normal[1:2], False)


def matrices_kernel(spreads_ref, x_ref, y_ref, forward_ref, adjoint_ref):
    row = lax.broadcasted_iota(jnp.int32, (LANES, LANES), 0)
    column = lax.broadcasted_iota(jnp.int32, (LANES, LANES), 1)
    for view in range(spreads_ref.shape[0]):
        normal = normal_taps(spreads_ref, view)
        x_ref[view] = bands(normal[0:1], True)
        y_ref[view] = bands(normal[1:2], True)
        for target, offset in ((forward_ref, column - row + HALF), (adjoint_ref, row - column + HALF)):
            high, low = split(band(normal[2:3], offset))
            for k in (0, LANES):
                target[view, k : k + LANES, :LANES] = high
                target[view, k : k + LANES, LANES:] = low


def banded(matrix, pieces):
    high, low = split(jnp.concatenate(pieces, axis=0))
    return jnp.dot(matrix, jnp.concatenate([high, high, low], axis=0), preferred_element_type=jnp.float32)


def beside(ref, count):
    return jnp.concatenate([ref[i] for i in range(count)], axis=1)


def blur_x(refs, matrix, out_ref):
    rows, width, _ = out_ref.shape
    flat = [ref.reshape(rows * width, LANES) for ref in refs]
    pieces = [jnp.concatenate([ref[pl.ds(j, rows, stride=width), :] for j in range(width)], axis=1) for ref in flat]
    blurred = banded(matrix, pieces)
    target = out_ref.reshape(rows * width, LANES)
    for j in range(width):
        target[pl.ds(j, rows, stride=width), :] = blurred[:, j * LANES : (j + 1) * LANES]


def blur_z(value, matrix):
    rows, width, _ = value.shape
    high, low = split(value.reshape(rows * width, LANES))
    product = jnp.dot(jnp.concatenate([high, low], axis=1), matrix, preferred_element_type=jnp.float32)
    return (product[:, :LANES] + product[:, LANES:]).reshape(rows, width, LANES)


def forward_y(refs, matrix_ref, out_ref):
    views, rows, width, _ = out_ref.shape
    blurred = banded(matrix_ref[...], [beside(ref, rows) for ref in refs])
    for view in range(views):
        for i in range(rows):
            out_ref[view, i] = blurred[view * width : (view + 1) * width, i * LANES : (i + 1) * LANES]


def forward_y_kernel(before_ref, own_ref, after_ref, matrix_ref, out_ref):
    forward_y((before_ref, own_ref, after_ref), matrix_ref, out_ref)


def first_forward_y_kernel(first, v_ref, tile_ref, across_ref, matrix_ref, out_ref, *part_refs):
    rows, width = out_ref.shape[1:3]
    views = tile_ref.shape[1] // width
    there = pl.ds(first, rows)
    for n, part_ref in enumerate(part_refs):
        place = v_ref[0] + n - 1
        inside = jnp.logical_and(place >= 0, place < views)

        @pl.when(inside)
        def _():
            part_ref[...] = tile_ref[there, pl.ds(pl.multiple_of(place * width, width), width), :]

        @pl.when(jnp.logical_not(inside))
        def _():
            part_ref[...] = across_ref[there]

    forward_y(part_refs, matrix_ref, out_ref)


def blurred_kernel(before_ref, own_ref, after_ref, bands_ref, matrix_ref, out_ref, mid_ref):
    for view in range(out_ref.shape[0]):
        blur_x([ref.at[view] for ref in (before_ref, own_ref, after_ref)], bands_ref[view], mid_ref.at[view])
        out_ref[view] = blur_z(mid_ref[view], matrix_ref[view])


def divide_kernel(first, data_ref, blurred_ref, out_ref):
    views, rows = out_ref.shape[:2]
    for view in range(views):
        out_ref[view] = data_ref[view, pl.ds(first, rows)] / blurred_ref[view]


def ratio_kernel(first, before_ref, own_ref, after_ref, bands_ref, matrix_ref, data_ref, out_ref, mid_ref):
    views, rows = out_ref.shape[:2]
    for view in range(views):
        blur_x([ref.at[view] for ref in (before_ref, own_ref, after_ref)], bands_ref[view], mid_ref.at[view])
        out_ref[view] = data_ref[view, pl.ds(first, rows)] / blur_z(mid_ref[view], matrix_ref[view])


def adjoint_x_kernel(before_ref, own_ref, after_ref, bands_ref, out_ref):
    for view in range(out_ref.shape[0]):
        blur_x([ref.at[view] for ref in (before_ref, own_ref, after_ref)], bands_ref[view], out_ref.at[view])


def update_kernel(first, before_ref, own_ref, after_ref, bands_ref, matrix_ref, estimate_ref, out_ref, mid_ref):
    views, rows = own_ref.shape[:2]
    total = None
    for view in range(views):
        blurred = banded(bands_ref[view], [beside(ref.at[view], rows) for ref in (before_ref, own_ref, after_ref)])
        for i in range(rows):
            mid_ref[view, i] = blurred[:, i * LANES : (i + 1) * LANES]
        terms = jnp.log(blur_z(mid_ref[view], matrix_ref[view]))
        total = terms if total is None else total + terms
    out_ref[...] = estimate_ref[pl.ds(first, rows)] * jnp.exp(total / views)


def collect_kernel(pieces_ref, out_ref):
    views, _, width, _ = pieces_ref.shape
    for view in range(views):
        out_ref[:, view * width : (view + 1) * width, :] = pieces_ref[view]


def shifted(size, by):
    return [(i, i + by) for i in range(size) if 0 <= i + by < size]


def onward(value, axes):
    return lax.ppermute(value, axes, shifted(lax.axis_size(axes), 1))


def back(value, axes):
    return lax.ppermute(value, axes, shifted(lax.axis_size(axes), -1))


def across(value):
    tiles, views = lax.axis_size("gy"), lax.axis_size("view")
    pairs = [(gy * views + views - 1, (gy + 1) * views) for gy in range(tiles - 1)]
    return lax.ppermute(value, ("gy", "view"), pairs + [(b, a) for a, b in pairs])


def exchanged(pieces):
    return lax.all_to_all(pieces, "view", 0, 0, tiled=True)


def body(estimate, views_data, spread_x, spread_y, spread_z):
    rows, width, depth = estimate.shape
    views = lax.axis_size("view")
    width = width // views
    half = rows // 2
    assert width == HALF and half == HALF and depth == LANES
    f32 = jnp.float32
    v = lax.axis_index("view")
    v_word = v.astype(jnp.int32).reshape(1)
    y = ("gy", "view")
    half_shape = ((views, half, width, depth), f32)
    bands_shape = ((views, HALF, 9 * HALF), jnp.bfloat16)
    matrix_shape = ((views, 2 * LANES, 2 * LANES), jnp.bfloat16)
    part = ((half, width, depth), f32)
    mid = [pltpu.VMEM(*half_shape)]

    own = call(part_kernel, [((rows, width, depth), f32)], [], v_word, estimate)[0]
    spreads = jnp.concatenate([spread_x, spread_y, spread_z, jnp.ones((5, TAPS), f32)])
    spreads = jnp.broadcast_to(jnp.pad(spreads, ((0, 0), (0, LANES - TAPS))), (views, 8, LANES))
    data = call(deal_kernel, [((views, rows, width, depth), f32)], [], views_data[0])[0]
    spreads = exchanged(spreads)
    data = exchanged(data)
    edge = across(own)
    forward_x, forward_y = call(
        forward_bands_kernel, [bands_shape, ((views * HALF, 9 * HALF), jnp.bfloat16)], [], spreads
    )
    adjoint_x, adjoint_y, forward_z, adjoint_z = call(
        matrices_kernel, [bands_shape, bands_shape, matrix_shape, matrix_shape], [], spreads
    )
    for step_number in range(ITERS):
        if step_number == 0:
            blurred = [
                call(
                    functools.partial(first_forward_y_kernel, n * half), [half_shape], [pltpu.VMEM(*part)] * 3,
                    v_word, estimate, edge, forward_y,
                )[0]
                for n in range(2)
            ]
        else:
            edges = [(onward(own[n], y), back(own[n], y)) for n in range(2)]
            blurred = [
                call(forward_y_kernel, [half_shape], [], edges[n][0], own[n], edges[n][1], forward_y)[0] for n in range(2)
            ]
        low, high = blurred
        before, after = onward(high, "gx"), back(low, "gx")
        ratios = []
        for first, rows_in in ((0, (before, low, high)), (half, (low, high, after))):
            if step_number == 0:
                blurred = call(blurred_kernel, [half_shape], mid, *rows_in, forward_x, forward_z)[0]
                ratios.append(call(functools.partial(divide_kernel, first), [half_shape], [], data, blurred)[0])
            else:
                kernel = functools.partial(ratio_kernel, first)
                ratios.append(call(kernel, [half_shape], mid, *rows_in, forward_x, forward_z, data)[0])
        ratio_low, ratio_high = ratios
        before, after = onward(ratio_high, "gx"), back(ratio_low, "gx")
        high = call(adjoint_x_kernel, [half_shape], [], ratio_low, ratio_high, after, adjoint_x)[0]
        low = call(adjoint_x_kernel, [half_shape], [], before, ratio_low, ratio_high, adjoint_x)[0]
        ins = [(onward(value, y), value, back(value, y), adjoint_y, adjoint_z) for value in (low, high)]
        olds = [(0, own[0]), (0, own[1])] if step_number else [(0, own), (half, own)]
        own = [
            call(functools.partial(update_kernel, first), [part], mid, *ins[n], old)[0]
            for n, (first, old) in enumerate(olds)
        ]
    share = rows // views
    pieces = exchanged(jnp.concatenate(own).reshape(views, share, width, depth))
    return call(collect_kernel, [((share, width * views, depth), f32)], [], pieces)[0]


def solution(mesh):
    in_specs = (
        P("gx", "gy", None),
        P("view", "gx", "gy", None),
        P("view", None),
        P("view", None),
        P("view", None),
    )
    out_specs = P(("gx", "view"), "gy", None)
    return jax.shard_map(body, mesh=mesh, in_specs=in_specs, out_specs=out_specs, check_vma=False)
```

time: 173 us -> 166 us (0.960)
  the two profiles are of different devices: /device:TPU:22 before, /device:TPU:46 now
where the time goes in v5:
time: 166 us; the launch traced here: 165 us
  starting transfers between devices  79.6 us (48%)
  waiting for transfers between devices  51.8 us (31%)
  Pallas kernels  17.5 us (11%)
  blocking collectives  11.5 us (7%)
  local copies, waits for them, and re-layouts  4.16 us (3%)
    ppermute x10, starting transfers between devices, back(): return lax.ppermute(value, axes, shifted(lax.axis_size(axes), -1))  34.8 us
    ppermute x10, waiting for transfers between devices, onward(): return lax.ppermute(value, axes, shifted(lax.axis_size(axes), 1))  32.3 us
    ppermute x10, starting transfers between devices, onward(): return lax.ppermute(value, axes, shifted(lax.axis_size(axes), 1))  25 us
    pallas_call x23, Pallas kernels, call(): pl.pallas_call(kernel, out_shape=[jax.ShapeDtypeStruct(s, d) for s, d in...  17.5 us
    ppermute x10, waiting for transfers between devices, back(): return lax.ppermute(value, axes, shifted(lax.axis_size(axes), -1))  12.1 us
    all_to_all x1, blocking collectives, exchanged(): return lax.all_to_all(pieces, 'view', 0, 0, tiled=True)  11.5 us
    all_to_all x2, starting transfers between devices, exchanged(): return lax.all_to_all(pieces, 'view', 0, 0, tiled=True)  10.8 us
    ppermute x1, starting transfers between devices, across(): lax.ppermute(value, ('gy', 'view'), pairs + [(b, a) for a, b in pairs])  8.99 us
  transfers between devices with their start and end apart: 23, of which 15 were waited for; matrix products, arithmetic and copies ran while one was open for 0% of the time, Pallas kernels for 10%

profile of v5, /device:TPU:46, one launch (start us, length us, event | category | flops | bytes accessed | tf_op | source)
XLA Modules:
  0.0 165.0 jit_solution(6424167809717833389)
XLA Ops:
  1.4 7.3 %all-to-all-start.1 = ((f32[4,8,128]{2,1,0:T(8,128)}), f32[4,8,128]{2,1,0:T(8,128)S(1)}, u32[]{:S(2)}, u32[]{:S(2)}) async-start(f32[4,8,128]{2,1,0:T(8,128)} %broadcast_in_dim.7), calls=%async_computation.1 | async-start | bytes 32768 | tf_op jit(solution)/shard_map/all_to_all | solution.py:208
  10.7 3.5 %all-to-all-done.1.spreads_ref = f32[4,8,128]{2,1,0:T(8,128)S(1)} async-done(((f32[4,8,128]{2,1,0:T(8,128)}), f32[4,8,128]{2,1,0:T(8,128)S(1)}, u32[]{:S(2)}, u32[]{:S(2)}) %all-to-all-start.1) | async-done | bytes 16416 | tf_op jit(solution)/shard_map/all_to_all | solution.py:208
  14.3 3.5 %all-to-all-start = ((f32[4,32,16,128]{3,2,1,0:T(8,128)}), f32[4,32,16,128]{3,2,1,0:T(8,128)S(1)}, u32[]{:S(2)}, u32[]{:S(2)}) async-start(f32[4,32,16,128]{3,2,1,0:T(8,128)} %shard_map.55), calls=%async_computation | async-start | bytes 2097152 | tf_op jit(solution)/shard_map/all_to_all | solution.py:208
  17.8 9.0 %collective-permute-start = (f32[32,16,128]{2,1,0:T(8,128)S(1)}, f32[32,16,128]{2,1,0:T(8,128)S(1)}, u32[]{:S(2)}, u32[]{:S(2)}) collective-permute-start(f32[32,16,128]{2,1,0:T(8,128)S(1)} %shard_map.56.estimate_ref), channel_id=1, source_target_pairs={{3,4},{7,8},{11,12},{15,16},{19,20},{23,24},{27,28},{4,3},{8,7},{1... | collective-permute-start | bytes 786440 | tf_op jit(solution)/shard_map/ppermute | solution.py:204
  27.6 3.8 %collective-permute-done.across_ref = f32[32,16,128]{2,1,0:T(8,128)S(1)} collective-permute-done((f32[32,16,128]{2,1,0:T(8,128)S(1)}, f32[32,16,128]{2,1,0:T(8,128)S(1)}, u32[]{:S(2)}, u32[]{:S(2)}) %collective-permute-start) | collective-permute-done | bytes 262176 | tf_op jit(solution)/shard_map/ppermute | solution.py:204
  33.9 3.6 %collective-permute-start.1 = (f32[4,16,16,128]{3,2,1,0:T(8,128)S(1)}, f32[4,16,16,128]{3,2,1,0:T(8,128)}, u32[]{:S(2)}, u32[]{:S(2)}) collective-permute-start(f32[4,16,16,128]{3,2,1,0:T(8,128)S(1)} %shard_map.58.before_ref.own_ref), channel_id=1, source_target_pairs={{32,0},{64,32},{96,64},{128,96},{160,128},{192,160},{224,192},{256... | collective-permute-start | bytes 1572872 | tf_op jit(solution)/shard_map/ppermute | solution.py:198
  37.5 2.4 %shard_map.60 = (bf16[4,16,144]{2,1,0:T(8,128)(2,1)S(1)}, bf16[4,16,144]{2,1,0:T(8,128)(2,1)S(1)}, bf16[4,256,256]{2,1,0:T(8,128)(2,1)S(1)}, bf16[4,256,256]{2,1,0:T(8,128)(2,1)S(1)}) custom-call(f32[4,8,128]{2,1,0:T(8,128)S(1)} %all-to-all-done.1.spreads_ref), custom_call_target="tpu_custom_call" | custom-call | tf_op jit(solution)/shard_map/pallas_call | solution.py:20
  39.9 2.2 %collective-permute-done.3.before_ref = f32[4,16,16,128]{3,2,1,0:T(8,128)S(1)} collective-permute-done((f32[4,16,16,128]{3,2,1,0:T(8,128)S(1)}, f32[4,16,16,128]{3,2,1,0:T(8,128)S(1)}, u32[]{:S(2)}, u32[]{:S(2)}) %collective-permute-start.3) | collective-permute-done | bytes 524320 | tf_op jit(solution)/shard_map/ppermute | solution.py:194
  49.4 2.4 %collective-permute-start.2 = (f32[4,16,16,128]{3,2,1,0:T(8,128)S(1)}, f32[4,16,16,128]{3,2,1,0:T(8,128)S(1)}, u32[]{:S(2)}, u32[]{:S(2)}) collective-permute-start(f32[4,16,16,128]{3,2,1,0:T(8,128)S(1)} %shard_map.62.after_ref.own_ref), channel_id=1, source_target_pairs={{0,32},{32,64},{64,96},{96,128},{128,160},{160,192},{192,224},{224... | collective-permute-start | bytes 1572872 | tf_op jit(solution)/shard_map/ppermute | solution.py:194
  54.5 5.8 %collective-permute-start.10 = (f32[4,16,16,128]{3,2,1,0:T(8,128)S(1)}, f32[4,16,16,128]{3,2,1,0:T(8,128)S(1)}, u32[]{:S(2)}, u32[]{:S(2)}) collective-permute-start(f32[4,16,16,128]{3,2,1,0:T(8,128)S(1)} %shard_map.68.own_ref), channel_id=1, source_target_pairs={{1,0},{2,1},{3,2},{4,3},{5,4},{6,5},{7,6},{8,7},{9,8},{10,9},{11,1... | collective-permute-start | bytes 1572872 | tf_op jit(solution)/shard_map/ppermute | solution.py:198
  62.8 6.1 %collective-permute-start.5 = (f32[4,16,16,128]{3,2,1,0:T(8,128)S(1)}, f32[4,16,16,128]{3,2,1,0:T(8,128)S(1)}, u32[]{:S(2)}, u32[]{:S(2)}) collective-permute-start(f32[4,16,16,128]{3,2,1,0:T(8,128)S(1)} %shard_map.65.own_ref), channel_id=1, source_target_pairs={{1,0},{2,1},{3,2},{4,3},{5,4},{6,5},{7,6},{8,7},{9,8},{10,9},{11,1... | collective-permute-start | bytes 1572872 | tf_op jit(solution)/shard_map/ppermute | solution.py:198
  72.6 6.5 %collective-permute-done.9.before_ref = f32[4,16,16,128]{3,2,1,0:T(8,128)S(1)} collective-permute-done((f32[4,16,16,128]{3,2,1,0:T(8,128)S(1)}, f32[4,16,16,128]{3,2,1,0:T(8,128)S(1)}, u32[]{:S(2)}, u32[]{:S(2)}) %collective-permute-start.9) | collective-permute-done | bytes 524320 | tf_op jit(solution)/shard_map/ppermute | solution.py:194
  81.8 3.9 %collective-permute-start.11 = (f32[16,16,128]{2,1,0:T(8,128)S(1)}, f32[16,16,128]{2,1,0:T(8,128)S(1)}, u32[]{:S(2)}, u32[]{:S(2)}) collective-permute-start(f32[16,16,128]{2,1,0:T(8,128)S(1)} %shard_map.69.own_ref.estimate_ref), channel_id=1, source_target_pairs={{0,1},{1,2},{2,3},{3,4},{4,5},{5,6},{6,7},{7,8},{8,9},{9,10},{10,1... | collective-permute-start | bytes 393224 | tf_op jit(solution)/shard_map/ppermute | solution.py:194
  85.8 4.5 %collective-permute-done.4.before_ref = f32[4,16,16,128]{3,2,1,0:T(8,128)S(1)} collective-permute-done((f32[4,16,16,128]{3,2,1,0:T(8,128)S(1)}, f32[4,16,16,128]{3,2,1,0:T(8,128)S(1)}, u32[]{:S(2)}, u32[]{:S(2)}) %collective-permute-start.4) | collective-permute-done | bytes 524320 | tf_op jit(solution)/shard_map/ppermute | solution.py:194
  93.1 3.9 %collective-permute-start.6 = (f32[16,16,128]{2,1,0:T(8,128)S(1)}, f32[16,16,128]{2,1,0:T(8,128)S(1)}, u32[]{:S(2)}, u32[]{:S(2)}) collective-permute-start(f32[16,16,128]{2,1,0:T(8,128)S(1)} %shard_map.66.own_ref.estimate_ref), channel_id=1, source_target_pairs={{0,1},{1,2},{2,3},{3,4},{4,5},{5,6},{6,7},{7,8},{8,9},{9,10},{10,1... | collective-permute-start | bytes 393224 | tf_op jit(solution)/shard_map/ppermute | solution.py:194
  99.2 2.9 %collective-permute-done.6.before_ref = f32[16,16,128]{2,1,0:T(8,128)S(1)} collective-permute-done((f32[16,16,128]{2,1,0:T(8,128)S(1)}, f32[16,16,128]{2,1,0:T(8,128)S(1)}, u32[]{:S(2)}, u32[]{:S(2)}) %collective-permute-start.6) | collective-permute-done | bytes 131104 | tf_op jit(solution)/shard_map/ppermute | solution.py:194
  104.2 3.6 %collective-permute-done.15.before_ref = f32[4,16,16,128]{3,2,1,0:T(8,128)S(1)} collective-permute-done((f32[4,16,16,128]{3,2,1,0:T(8,128)S(1)}, f32[4,16,16,128]{3,2,1,0:T(8,128)S(1)}, u32[]{:S(2)}, u32[]{:S(2)}) %collective-permute-start.15) | collective-permute-done | bytes 524320 | tf_op jit(solution)/shard_map/ppermute | solution.py:194
  112.2 3.3 %collective-permute-start.14 = (f32[4,16,16,128]{3,2,1,0:T(8,128)S(1)}, f32[4,16,16,128]{3,2,1,0:T(8,128)S(1)}, u32[]{:S(2)}, u32[]{:S(2)}) collective-permute-start(f32[4,16,16,128]{3,2,1,0:T(8,128)S(1)} %shard_map.71.after_ref.own_ref), channel_id=1, source_target_pairs={{0,32},{32,64},{64,96},{96,128},{128,160},{160,192},{192,224},{224... | collective-permute-start | bytes 1572872 | tf_op jit(solution)/shard_map/ppermute | solution.py:194
  118.1 4.0 %collective-permute-start.20 = (f32[4,16,16,128]{3,2,1,0:T(8,128)S(1)}, f32[4,16,16,128]{3,2,1,0:T(8,128)S(1)}, u32[]{:S(2)}, u32[]{:S(2)}) collective-permute-start(f32[4,16,16,128]{3,2,1,0:T(8,128)S(1)} %shard_map.75.own_ref), channel_id=1, source_target_pairs={{1,0},{2,1},{3,2},{4,3},{5,4},{6,5},{7,6},{8,7},{9,8},{10,9},{11,1... | collective-permute-start | bytes 1572872 | tf_op jit(solution)/shard_map/ppermute | solution.py:198
  125.3 5.4 %collective-permute-start.17 = (f32[4,16,16,128]{3,2,1,0:T(8,128)S(1)}, f32[4,16,16,128]{3,2,1,0:T(8,128)S(1)}, u32[]{:S(2)}, u32[]{:S(2)}) collective-permute-start(f32[4,16,16,128]{3,2,1,0:T(8,128)S(1)} %shard_map.73.own_ref), channel_id=1, source_target_pairs={{1,0},{2,1},{3,2},{4,3},{5,4},{6,5},{7,6},{8,7},{9,8},{10,9},{11,1... | collective-permute-start | bytes 1572872 | tf_op jit(solution)/shard_map/ppermute | solution.py:198
  134.8 6.1 %collective-permute-done.19.before_ref = f32[4,16,16,128]{3,2,1,0:T(8,128)S(1)} collective-permute-done((f32[4,16,16,128]{3,2,1,0:T(8,128)S(1)}, f32[4,16,16,128]{3,2,1,0:T(8,128)S(1)}, u32[]{:S(2)}, u32[]{:S(2)}) %collective-permute-start.19) | collective-permute-done | bytes 524320 | tf_op jit(solution)/shard_map/ppermute | solution.py:194
  141.8 4.2 %collective-permute-done.17.after_ref = f32[4,16,16,128]{3,2,1,0:T(8,128)S(1)} collective-permute-done((f32[4,16,16,128]{3,2,1,0:T(8,128)S(1)}, f32[4,16,16,128]{3,2,1,0:T(8,128)S(1)}, u32[]{:S(2)}, u32[]{:S(2)}) %collective-permute-start.17) | collective-permute-done | bytes 524320 | tf_op jit(solution)/shard_map/ppermute | solution.py:198
  146.1 5.9 %collective-permute-done.16.before_ref = f32[4,16,16,128]{3,2,1,0:T(8,128)S(1)} collective-permute-done((f32[4,16,16,128]{3,2,1,0:T(8,128)S(1)}, f32[4,16,16,128]{3,2,1,0:T(8,128)S(1)}, u32[]{:S(2)}, u32[]{:S(2)}) %collective-permute-start.16) | collective-permute-done | bytes 524320 | tf_op jit(solution)/shard_map/ppermute | solution.py:194
  152.8 11.5 %all_to_all.15.pieces_ref = f32[4,8,16,128]{3,2,1,0:T(8,128)S(1)} all-to-all(f32[4,8,16,128]{3,2,1,0:T(8,128)S(1)} %bitcast.4), channel_id=1, replica_groups=mesh['gx'=16,'gy'=8,'view'=4] {'view'}, dimensions={0} | all-to-all | bytes 524288 | tf_op jit(solution)/shard_map/all_to_all | solution.py:208
  (66 shorter events, 49.2 us)
Async XLA Ops:
  1.4 12.9 %all-to-all-start.1 = ((f32[4,8,128]{2,1,0:T(8,128)}), f32[4,8,128]{2,1,0:T(8,128)S(1)}, u32[]{:S(2)}, u32[]{:S(2)}) async-start(f32[4,8,128]{2,1,0:T(8,128)} %broadcast_in_dim.7), calls=%async_computation.1 | async-start | bytes 32768 | tf_op jit(solution)/shard_map/all_to_all | solution.py:208
  10.7 7.1 %copy-start = (f32[32,64,128]{2,1,0:T(8,128)S(1)}, f32[32,64,128]{2,1,0:T(8,128)}, u32[]{:S(2)}) copy-start(f32[32,64,128]{2,1,0:T(8,128)} %tile_ref.5) | copy-start | bytes 3145732
  14.3 29.9 %all-to-all-start = ((f32[4,32,16,128]{3,2,1,0:T(8,128)}), f32[4,32,16,128]{3,2,1,0:T(8,128)S(1)}, u32[]{:S(2)}, u32[]{:S(2)}) async-start(f32[4,32,16,128]{3,2,1,0:T(8,128)} %shard_map.55), calls=%async_computation | async-start | bytes 2097152 | tf_op jit(solution)/shard_map/all_to_all | solution.py:208
  17.8 13.6 %collective-permute-start = (f32[32,16,128]{2,1,0:T(8,128)S(1)}, f32[32,16,128]{2,1,0:T(8,128)S(1)}, u32[]{:S(2)}, u32[]{:S(2)}) collective-permute-start(f32[32,16,128]{2,1,0:T(8,128)S(1)} %shard_map.56.estimate_ref), channel_id=1, source_target_pairs={{3,4},{7,8},{11,12},{15,16},{19,20},{23,24},{27,28},{4,3},{8,7},{1... | collective-permute-start | bytes 786440 | tf_op jit(solution)/shard_map/ppermute | solution.py:204
  31.7 10.5 %collective-permute-start.3 = (f32[4,16,16,128]{3,2,1,0:T(8,128)S(1)}, f32[4,16,16,128]{3,2,1,0:T(8,128)S(1)}, u32[]{:S(2)}, u32[]{:S(2)}) collective-permute-start(f32[4,16,16,128]{3,2,1,0:T(8,128)S(1)} %shard_map.59.own_ref.after_ref), channel_id=1, source_target_pairs={{0,32},{32,64},{64,96},{96,128},{128,160},{160,192},{192,224},{224... | collective-permute-start | bytes 1572872 | tf_op jit(solution)/shard_map/ppermute | solution.py:194
  33.9 13.3 %collective-permute-start.1 = (f32[4,16,16,128]{3,2,1,0:T(8,128)S(1)}, f32[4,16,16,128]{3,2,1,0:T(8,128)}, u32[]{:S(2)}, u32[]{:S(2)}) collective-permute-start(f32[4,16,16,128]{3,2,1,0:T(8,128)S(1)} %shard_map.58.before_ref.own_ref), channel_id=1, source_target_pairs={{32,0},{64,32},{96,64},{128,96},{160,128},{192,160},{224,192},{256... | collective-permute-start | bytes 1572872 | tf_op jit(solution)/shard_map/ppermute | solution.py:198
  45.2 8.6 %collective-permute-start.8 = (f32[4,16,16,128]{3,2,1,0:T(8,128)S(1)}, f32[4,16,16,128]{3,2,1,0:T(8,128)S(1)}, u32[]{:S(2)}, u32[]{:S(2)}) collective-permute-start(f32[4,16,16,128]{3,2,1,0:T(8,128)S(1)} %shard_map.64.own_ref.before_ref), channel_id=1, source_target_pairs={{32,0},{64,32},{96,64},{128,96},{160,128},{192,160},{224,192},{256... | collective-permute-start | bytes 1572872 | tf_op jit(solution)/shard_map/ppermute | solution.py:198
  49.4 12.8 %collective-permute-start.2 = (f32[4,16,16,128]{3,2,1,0:T(8,128)S(1)}, f32[4,16,16,128]{3,2,1,0:T(8,128)S(1)}, u32[]{:S(2)}, u32[]{:S(2)}) collective-permute-start(f32[4,16,16,128]{3,2,1,0:T(8,128)S(1)} %shard_map.62.after_ref.own_ref), channel_id=1, source_target_pairs={{0,32},{32,64},{64,96},{96,128},{128,160},{160,192},{192,224},{224... | collective-permute-start | bytes 1572872 | tf_op jit(solution)/shard_map/ppermute | solution.py:194
  54.5 18.1 %collective-permute-start.10 = (f32[4,16,16,128]{3,2,1,0:T(8,128)S(1)}, f32[4,16,16,128]{3,2,1,0:T(8,128)S(1)}, u32[]{:S(2)}, u32[]{:S(2)}) collective-permute-start(f32[4,16,16,128]{3,2,1,0:T(8,128)S(1)} %shard_map.68.own_ref), channel_id=1, source_target_pairs={{1,0},{2,1},{3,2},{4,3},{5,4},{6,5},{7,6},{8,7},{9,8},{10,9},{11,1... | collective-permute-start | bytes 1572872 | tf_op jit(solution)/shard_map/ppermute | solution.py:198
  60.3 18.8 %collective-permute-start.9 = (f32[4,16,16,128]{3,2,1,0:T(8,128)S(1)}, f32[4,16,16,128]{3,2,1,0:T(8,128)S(1)}, u32[]{:S(2)}, u32[]{:S(2)}) collective-permute-start(f32[4,16,16,128]{3,2,1,0:T(8,128)S(1)} %shard_map.68.own_ref), channel_id=1, source_target_pairs={{0,1},{1,2},{2,3},{3,4},{4,5},{5,6},{6,7},{7,8},{8,9},{9,10},{10,1... | collective-permute-start | bytes 1572872 | tf_op jit(solution)/shard_map/ppermute | solution.py:194
  62.8 22.9 %collective-permute-start.5 = (f32[4,16,16,128]{3,2,1,0:T(8,128)S(1)}, f32[4,16,16,128]{3,2,1,0:T(8,128)S(1)}, u32[]{:S(2)}, u32[]{:S(2)}) collective-permute-start(f32[4,16,16,128]{3,2,1,0:T(8,128)S(1)} %shard_map.65.own_ref), channel_id=1, source_target_pairs={{1,0},{2,1},{3,2},{4,3},{5,4},{6,5},{7,6},{8,7},{9,8},{10,9},{11,1... | collective-permute-start | bytes 1572872 | tf_op jit(solution)/shard_map/ppermute | solution.py:198
  68.9 21.4 %collective-permute-start.4 = (f32[4,16,16,128]{3,2,1,0:T(8,128)S(1)}, f32[4,16,16,128]{3,2,1,0:T(8,128)S(1)}, u32[]{:S(2)}, u32[]{:S(2)}) collective-permute-start(f32[4,16,16,128]{3,2,1,0:T(8,128)S(1)} %shard_map.65.own_ref), channel_id=1, source_target_pairs={{0,1},{1,2},{2,3},{3,4},{4,5},{5,6},{6,7},{7,8},{8,9},{9,10},{10,1... | collective-permute-start | bytes 1572872 | tf_op jit(solution)/shard_map/ppermute | solution.py:194
  79.9 17.1 %collective-permute-start.12 = (f32[16,16,128]{2,1,0:T(8,128)S(1)}, f32[16,16,128]{2,1,0:T(8,128)S(1)}, u32[]{:S(2)}, u32[]{:S(2)}) collective-permute-start(f32[16,16,128]{2,1,0:T(8,128)S(1)} %shard_map.69.own_ref.estimate_ref), channel_id=1, source_target_pairs={{1,0},{2,1},{3,2},{4,3},{5,4},{6,5},{7,6},{8,7},{9,8},{10,9},{11,1... | collective-permute-start | bytes 393224 | tf_op jit(solution)/shard_map/ppermute | solution.py:198
  81.8 15.2 %collective-permute-start.11 = (f32[16,16,128]{2,1,0:T(8,128)S(1)}, f32[16,16,128]{2,1,0:T(8,128)S(1)}, u32[]{:S(2)}, u32[]{:S(2)}) collective-permute-start(f32[16,16,128]{2,1,0:T(8,128)S(1)} %shard_map.69.own_ref.estimate_ref), channel_id=1, source_target_pairs={{0,1},{1,2},{2,3},{3,4},{4,5},{5,6},{6,7},{7,8},{8,9},{9,10},{10,1... | collective-permute-start | bytes 393224 | tf_op jit(solution)/shard_map/ppermute | solution.py:194
  91.1 8.0 %collective-permute-start.7 = (f32[16,16,128]{2,1,0:T(8,128)S(1)}, f32[16,16,128]{2,1,0:T(8,128)S(1)}, u32[]{:S(2)}, u32[]{:S(2)}) collective-permute-start(f32[16,16,128]{2,1,0:T(8,128)S(1)} %shard_map.66.own_ref.estimate_ref), channel_id=1, source_target_pairs={{1,0},{2,1},{3,2},{4,3},{5,4},{6,5},{7,6},{8,7},{9,8},{10,9},{11,1... | collective-permute-start | bytes 393224 | tf_op jit(solution)/shard_map/ppermute | solution.py:198
  93.1 9.0 %collective-permute-start.6 = (f32[16,16,128]{2,1,0:T(8,128)S(1)}, f32[16,16,128]{2,1,0:T(8,128)S(1)}, u32[]{:S(2)}, u32[]{:S(2)}) collective-permute-start(f32[16,16,128]{2,1,0:T(8,128)S(1)} %shard_map.66.own_ref.estimate_ref), channel_id=1, source_target_pairs={{0,1},{1,2},{2,3},{3,4},{4,5},{5,6},{6,7},{7,8},{8,9},{9,10},{10,1... | collective-permute-start | bytes 393224 | tf_op jit(solution)/shard_map/ppermute | solution.py:194
  97.2 10.5 %collective-permute-start.15 = (f32[4,16,16,128]{3,2,1,0:T(8,128)S(1)}, f32[4,16,16,128]{3,2,1,0:T(8,128)S(1)}, u32[]{:S(2)}, u32[]{:S(2)}) collective-permute-start(f32[4,16,16,128]{3,2,1,0:T(8,128)S(1)} %shard_map.70.own_ref.after_ref), channel_id=1, source_target_pairs={{0,32},{32,64},{64,96},{96,128},{128,160},{160,192},{192,224},{224... | collective-permute-start | bytes 1572872 | tf_op jit(solution)/shard_map/ppermute | solution.py:194
  102.3 8.7 %collective-permute-start.13 = (f32[4,16,16,128]{3,2,1,0:T(8,128)S(1)}, f32[4,16,16,128]{3,2,1,0:T(8,128)S(1)}, u32[]{:S(2)}, u32[]{:S(2)}) collective-permute-start(f32[4,16,16,128]{3,2,1,0:T(8,128)S(1)} %shard_map.67.before_ref.own_ref), channel_id=1, source_target_pairs={{32,0},{64,32},{96,64},{128,96},{160,128},{192,160},{224,192},{256... | collective-permute-start | bytes 1572872 | tf_op jit(solution)/shard_map/ppermute | solution.py:198
  108.9 8.6 %collective-permute-start.18 = (f32[4,16,16,128]{3,2,1,0:T(8,128)S(1)}, f32[4,16,16,128]{3,2,1,0:T(8,128)S(1)}, u32[]{:S(2)}, u32[]{:S(2)}) collective-permute-start(f32[4,16,16,128]{3,2,1,0:T(8,128)S(1)} %shard_map.72.own_ref.before_ref), channel_id=1, source_target_pairs={{32,0},{64,32},{96,64},{128,96},{160,128},{192,160},{224,192},{256... | collective-permute-start | bytes 1572872 | tf_op jit(solution)/shard_map/ppermute | solution.py:198
  112.2 12.5 %collective-permute-start.14 = (f32[4,16,16,128]{3,2,1,0:T(8,128)S(1)}, f32[4,16,16,128]{3,2,1,0:T(8,128)S(1)}, u32[]{:S(2)}, u32[]{:S(2)}) collective-permute-start(f32[4,16,16,128]{3,2,1,0:T(8,128)S(1)} %shard_map.71.after_ref.own_ref), channel_id=1, source_target_pairs={{0,32},{32,64},{64,96},{96,128},{128,160},{160,192},{192,224},{224... | collective-permute-start | bytes 1572872 | tf_op jit(solution)/shard_map/ppermute | solution.py:194
  118.1 16.7 %collective-permute-start.20 = (f32[4,16,16,128]{3,2,1,0:T(8,128)S(1)}, f32[4,16,16,128]{3,2,1,0:T(8,128)S(1)}, u32[]{:S(2)}, u32[]{:S(2)}) collective-permute-start(f32[4,16,16,128]{3,2,1,0:T(8,128)S(1)} %shard_map.75.own_ref), channel_id=1, source_target_pairs={{1,0},{2,1},{3,2},{4,3},{5,4},{6,5},{7,6},{8,7},{9,8},{10,9},{11,1... | collective-permute-start | bytes 1572872 | tf_op jit(solution)/shard_map/ppermute | solution.py:198
  122.2 18.8 %collective-permute-start.19 = (f32[4,16,16,128]{3,2,1,0:T(8,128)S(1)}, f32[4,16,16,128]{3,2,1,0:T(8,128)S(1)}, u32[]{:S(2)}, u32[]{:S(2)}) collective-permute-start(f32[4,16,16,128]{3,2,1,0:T(8,128)S(1)} %shard_map.75.own_ref), channel_id=1, source_target_pairs={{0,1},{1,2},{2,3},{3,4},{4,5},{5,6},{6,7},{7,8},{8,9},{9,10},{10,1... | collective-permute-start | bytes 1572872 | tf_op jit(solution)/shard_map/ppermute | solution.py:194
  125.3 20.7 %collective-permute-start.17 = (f32[4,16,16,128]{3,2,1,0:T(8,128)S(1)}, f32[4,16,16,128]{3,2,1,0:T(8,128)S(1)}, u32[]{:S(2)}, u32[]{:S(2)}) collective-permute-start(f32[4,16,16,128]{3,2,1,0:T(8,128)S(1)} %shard_map.73.own_ref), channel_id=1, source_target_pairs={{1,0},{2,1},{3,2},{4,3},{5,4},{6,5},{7,6},{8,7},{9,8},{10,9},{11,1... | collective-permute-start | bytes 1572872 | tf_op jit(solution)/shard_map/ppermute | solution.py:198
  130.8 21.1 %collective-permute-start.16 = (f32[4,16,16,128]{3,2,1,0:T(8,128)S(1)}, f32[4,16,16,128]{3,2,1,0:T(8,128)S(1)}, u32[]{:S(2)}, u32[]{:S(2)}) collective-permute-start(f32[4,16,16,128]{3,2,1,0:T(8,128)S(1)} %shard_map.73.own_ref), channel_id=1, source_target_pairs={{0,1},{1,2},{2,3},{3,4},{4,5},{5,6},{6,7},{7,8},{8,9},{9,10},{10,1... | collective-permute-start | bytes 1572872 | tf_op jit(solution)/shard_map/ppermute | solution.py:194
  (6 other events, 4.9 us)

commit v6 on v5

v6 whole, which is shorter than its diff:
```python
import functools

import jax
import jax.numpy as jnp
from jax import lax
from jax.experimental import pallas as pl
from jax.experimental.pallas import tpu as pltpu
from jax.sharding import PartitionSpec as P

ITERS = 2
TAPS = 33
HALF = 16
LANES = 128
VMEM = pl.BlockSpec(memory_space=pltpu.VMEM)
SMEM = pl.BlockSpec(memory_space=pltpu.SMEM)
ANY = pl.BlockSpec(memory_space=pl.ANY)


def call(kernel, outs, scratch, *args, away=(), mebibytes=10):
    specs = [SMEM if a.dtype == jnp.int32 else ANY if n in away else VMEM for n, a in enumerate(args)]
    return pl.pallas_call(
        kernel,
        out_shape=[jax.ShapeDtypeStruct(s, d) for s, d in outs],
        in_specs=specs,
        out_specs=[VMEM] * len(outs),
        scratch_shapes=scratch,
        compiler_params=pltpu.CompilerParams(vmem_limit_bytes=mebibytes * 2**20),
    )(*args)


def split(value):
    high = value.astype(jnp.bfloat16)
    low = (value - high.astype(jnp.float32)).astype(jnp.bfloat16)
    return high, low


def pack_kernel(data_ref, *refs):
    spreads_refs, (out_ref, tile_ref, taps_ref, arrived) = refs[:-4], refs[-4:]
    copies = [pltpu.make_async_copy(data_ref, tile_ref, arrived.at[0])]
    for n, spread_ref in enumerate(spreads_refs):
        copies.append(pltpu.make_async_copy(spread_ref, taps_ref.at[n], arrived.at[1 + n]))
    for copy in copies:
        copy.start()
    for copy in copies:
        copy.wait()
    views, length, _ = out_ref.shape
    rows, width = data_ref.shape[0], data_ref.shape[1] // views
    cells = rows * width
    for view in range(views):
        piece = tile_ref[:, view * width : (view + 1) * width, :].astype(jnp.float32)
        out_ref[view, :cells] = piece.reshape(cells, LANES)
        out_ref[view, cells:] = jnp.zeros((length - cells, LANES), jnp.float32)
        for n in range(len(spreads_refs)):
            out_ref[view, cells + n : cells + n + 1, :TAPS] = taps_ref[n]


def part_kernel(v_ref, tile_ref, out_ref):
    width = out_ref.shape[1]
    out_ref[...] = tile_ref[:, pl.ds(pl.multiple_of(v_ref[0] * width, width), width), :]


def shifted_taps(packed_ref, view, axis, rows, shift):
    row = packed_ref.shape[1] - 8 + axis
    spread = packed_ref[view, row : row + 1, :]
    taps = jnp.broadcast_to(spread / jnp.sum(spread, axis=1, keepdims=True), (rows, LANES))
    turned = pltpu.roll(taps, (LANES - shift) % LANES, 1, stride=1, stride_axis=0)
    a = lax.broadcasted_iota(jnp.int32, (rows, LANES), 0)
    b = lax.broadcasted_iota(jnp.int32, (rows, LANES), 1)
    t = b - a + shift
    return jnp.where(jnp.logical_and(t >= 0, t < TAPS), turned, 0.0)


def flipped(matrix):
    columns = matrix.T[:HALF]
    return jnp.concatenate([columns, jnp.zeros((HALF, LANES - columns.shape[1]), columns.dtype)], axis=1)


def store_bands(matrix, out_ref):
    width = 3 * HALF
    high = matrix.astype(jnp.bfloat16).astype(jnp.float32)
    lane = lax.broadcasted_iota(jnp.int32, (HALF, LANES), 1)
    again = pltpu.roll(high, 2 * width, 1)
    start = high + pltpu.roll(matrix - high, width, 1) + jnp.where(lane >= 2 * width, again, 0.0)
    out_ref[:, :LANES] = start.astype(jnp.bfloat16)
    out_ref[:, LANES:] = again[:, : 3 * width - LANES].astype(jnp.bfloat16)


def store_z(matrix, out_ref):
    high, low = split(matrix)
    for k in (0, LANES):
        out_ref[k : k + LANES, :LANES] = high
        out_ref[k : k + LANES, LANES:] = low


def forward_matrices_kernel(packed_ref, x_ref, y_ref, z_ref):
    for view in range(packed_ref.shape[0]):
        for axis, target in ((0, x_ref.at[view]), (1, y_ref.at[pl.ds(view * HALF, HALF)])):
            store_bands(flipped(shifted_taps(packed_ref, view, axis, 3 * HALF, 2 * HALF)), target)
        store_z(shifted_taps(packed_ref, view, 2, LANES, HALF), z_ref.at[view])


def adjoint_matrices_kernel(packed_ref, x_ref, y_ref, z_ref):
    for view in range(packed_ref.shape[0]):
        for axis, target in ((0, x_ref.at[view]), (1, y_ref.at[view])):
            store_bands(shifted_taps(packed_ref, view, axis, HALF, 0), target)
        store_z(shifted_taps(packed_ref, view, 2, LANES, HALF).T, z_ref.at[view])


def banded(matrix, pieces):
    high, low = split(jnp.concatenate(pieces, axis=0))
    return jnp.dot(matrix, jnp.concatenate([high, high, low], axis=0), preferred_element_type=jnp.float32)


def beside(ref, count):
    return jnp.concatenate([ref[i] for i in range(count)], axis=1)


def blur_x(refs, matrix, out_ref):
    rows, width, _ = out_ref.shape
    flat = [ref.reshape(rows * width, LANES) for ref in refs]
    pieces = [jnp.concatenate([ref[pl.ds(j, rows, stride=width), :] for j in range(width)], axis=1) for ref in flat]
    blurred = banded(matrix, pieces)
    target = out_ref.reshape(rows * width, LANES)
    for j in range(width):
        target[pl.ds(j, rows, stride=width), :] = blurred[:, j * LANES : (j + 1) * LANES]


def blur_z(value, matrix):
    rows, width, _ = value.shape
    high, low = split(value.reshape(rows * width, LANES))
    product = jnp.dot(jnp.concatenate([high, low], axis=1), matrix, preferred_element_type=jnp.float32)
    return (product[:, :LANES] + product[:, LANES:]).reshape(rows, width, LANES)


def forward_y(pieces, matrix_ref, out_ref):
    views, rows, width, _ = out_ref.shape
    blurred = banded(matrix_ref[...], pieces)
    for view in range(views):
        for i in range(rows):
            out_ref[view, i] = blurred[view * width : (view + 1) * width, i * LANES : (i + 1) * LANES]


def forward_y_kernel(before_ref, own_ref, after_ref, matrix_ref, out_ref):
    rows = own_ref.shape[0]
    forward_y([beside(ref, rows) for ref in (before_ref, own_ref, after_ref)], matrix_ref, out_ref)


def extended_kernel(v_ref, tile_ref, across_ref, *out_refs):
    rows, width = out_refs[0].shape[0], out_refs[0].shape[1] // 3
    views = tile_ref.shape[1] // width
    for n in range(3):
        place = v_ref[0] + n - 1
        inside = jnp.logical_and(place >= 0, place < views)
        for half, out_ref in enumerate(out_refs):
            there = pl.ds(half * rows, rows)

            @pl.when(inside)
            def _():
                columns = pl.ds(pl.multiple_of(place * width, width), width)
                out_ref[:, n * width : (n + 1) * width, :] = tile_ref[there, columns, :]

            @pl.when(jnp.logical_not(inside))
            def _():
                out_ref[:, n * width : (n + 1) * width, :] = across_ref[there]


def extended_y_kernel(*refs):
    count = len(refs) // 2
    matrix_ref = refs[count]
    for ext_ref, out_ref in zip(refs[:count], refs[count + 1 :]):
        forward_y([beside(ext_ref, ext_ref.shape[0])], matrix_ref, out_ref)


def ratio_kernel(first, before_ref, own_ref, after_ref, bands_ref, matrix_ref, data_ref, out_ref, mid_ref):
    views, rows, width, _ = out_ref.shape
    for view in range(views):
        blur_x([ref.at[view] for ref in (before_ref, own_ref, after_ref)], bands_ref[view], mid_ref.at[view])
        data = data_ref[view, pl.ds(first * width, rows * width)].reshape(rows, width, LANES)
        out_ref[view] = data / blur_z(mid_ref[view], matrix_ref[view])


def adjoint_x_kernel(before_ref, own_ref, after_ref, bands_ref, out_ref):
    for view in range(out_ref.shape[0]):
        blur_x([ref.at[view] for ref in (before_ref, own_ref, after_ref)], bands_ref[view], out_ref.at[view])


def update_kernel(first, before_ref, own_ref, after_ref, bands_ref, matrix_ref, estimate_ref, out_ref, mid_ref):
    views, rows = own_ref.shape[:2]
    total = None
    for view in range(views):
        blurred = banded(bands_ref[view], [beside(ref.at[view], rows) for ref in (before_ref, own_ref, after_ref)])
        for i in range(rows):
            mid_ref[view, i] = blurred[:, i * LANES : (i + 1) * LANES]
        terms = jnp.log(blur_z(mid_ref[view], matrix_ref[view]))
        total = terms if total is None else total + terms
    out_ref[...] = estimate_ref[pl.ds(first, rows)] * jnp.exp(total / views)


def collect_kernel(pieces_ref, out_ref):
    views, _, width, _ = pieces_ref.shape
    for view in range(views):
        out_ref[:, view * width : (view + 1) * width, :] = pieces_ref[view]


def shifted(size, by):
    return [(i, i + by) for i in range(size) if 0 <= i + by < size]


def onward(value, axes):
    return lax.ppermute(value, axes, shifted(lax.axis_size(axes), 1))


def back(value, axes):
    return lax.ppermute(value, axes, shifted(lax.axis_size(axes), -1))


def across(value):
    tiles, views = lax.axis_size("gy"), lax.axis_size("view")
    pairs = [(gy * views + views - 1, (gy + 1) * views) for gy in range(tiles - 1)]
    return lax.ppermute(value, ("gy", "view"), pairs + [(b, a) for a, b in pairs])


def exchanged(pieces):
    return lax.all_to_all(pieces, "view", 0, 0, tiled=True)


def body(estimate, views_data, spread_x, spread_y, spread_z):
    rows, width, depth = estimate.shape
    views = lax.axis_size("view")
    width = width // views
    half = rows // 2
    assert width == HALF and half == HALF and depth == LANES
    f32 = jnp.float32
    v = lax.axis_index("view")
    v_word = v.astype(jnp.int32).reshape(1)
    y = ("gy", "view")
    half_shape = ((views, half, width, depth), f32)
    bands_shape = ((views, HALF, 9 * HALF), jnp.bfloat16)
    matrix_shape = ((views, 2 * LANES, 2 * LANES), jnp.bfloat16)
    part = ((half, width, depth), f32)
    mid = [pltpu.VMEM(*half_shape)]

    own = call(part_kernel, [((rows, width, depth), f32)], [], v_word, estimate)[0]
    packed = call(
        pack_kernel, [((views, rows * width + 8, depth), f32)],
        [pltpu.VMEM(estimate.shape, views_data.dtype), pltpu.VMEM((3, 1, TAPS), f32), pltpu.SemaphoreType.DMA((4,))],
        views_data[0], spread_x, spread_y, spread_z, away=range(4), mebibytes=56,
    )[0]
    packed = exchanged(packed)
    ext_shape = ((half, 3 * width, depth), f32)
    low, high = call(extended_kernel, [ext_shape] * 2, [], v_word, estimate, across(own))
    rows_in = [onward(high, "gx"), low, high, back(low, "gx")]
    forward_x, forward_y, forward_z = call(
        forward_matrices_kernel, [bands_shape, ((views * HALF, 9 * HALF), jnp.bfloat16), matrix_shape], [], packed
    )
    adjoint_x, adjoint_y, adjoint_z = call(
        adjoint_matrices_kernel, [bands_shape, bands_shape, matrix_shape], [], packed
    )
    for step_number in range(ITERS):
        if step_number == 0:
            before, low, high, after = call(extended_y_kernel, [half_shape] * 4, [], *rows_in, forward_y)
        else:
            low, high = [
                call(forward_y_kernel, [half_shape], [], onward(value, y), value, back(value, y), forward_y)[0]
                for value in own
            ]
            before, after = onward(high, "gx"), back(low, "gx")
        ratio_low, ratio_high = [
            call(functools.partial(ratio_kernel, n * half), [half_shape], mid, *three, forward_x, forward_z, packed)[0]
            for n, three in enumerate(((before, low, high), (low, high, after)))
        ]
        before, after = onward(ratio_high, "gx"), back(ratio_low, "gx")
        high = call(adjoint_x_kernel, [half_shape], [], ratio_low, ratio_high, after, adjoint_x)[0]
        low = call(adjoint_x_kernel, [half_shape], [], before, ratio_low, ratio_high, adjoint_x)[0]
        ins = [(onward(value, y), value, back(value, y), adjoint_y, adjoint_z) for value in (low, high)]
        olds = [(0, own[0]), (0, own[1])] if step_number else [(0, own), (half, own)]
        own = [
            call(functools.partial(update_kernel, first), [part], mid, *ins[n], old)[0]
            for n, (first, old) in enumerate(olds)
        ]
    share = rows // views
    pieces = exchanged(jnp.concatenate(own).reshape(views, share, width, depth))
    return call(collect_kernel, [((share, width * views, depth), f32)], [], pieces)[0]


def solution(mesh):
    in_specs = (
        P("gx", "gy", None),
        P("view", "gx", "gy", None),
        P("view", None),
        P("view", None),
        P("view", None),
    )
    out_specs = P(("gx", "view"), "gy", None)
    return jax.shard_map(body, mesh=mesh, in_specs=in_specs, out_specs=out_specs, check_vma=False)
```

time: 166 us -> 158 us (0.952)
  the two profiles are of different devices: /device:TPU:46 before, /device:TPU:16 now
where the time goes in v6:
time: 158 us; the launch traced here: 157 us
  waiting for transfers between devices  67.5 us (43%)
  starting transfers between devices  58.4 us (37%)
  Pallas kernels  16.9 us (11%)
  blocking collectives  13.7 us (9%)
    ppermute x10, starting transfers between devices, onward(): return lax.ppermute(value, axes, shifted(lax.axis_size(axes), 1))  31.4 us
    ppermute x10, waiting for transfers between devices, back(): return lax.ppermute(value, axes, shifted(lax.axis_size(axes), -1))  26 us
    ppermute x10, waiting for transfers between devices, onward(): return lax.ppermute(value, axes, shifted(lax.axis_size(axes), 1))  21.8 us
    all_to_all x1, waiting for transfers between devices, exchanged(): return lax.all_to_all(pieces, 'view', 0, 0, tiled=True)  19.7 us
    ppermute x10, starting transfers between devices, back(): return lax.ppermute(value, axes, shifted(lax.axis_size(axes), -1))  18.9 us
    pallas_call x21, Pallas kernels, call(): pl.pallas_call(kernel, out_shape=[jax.ShapeDtypeStruct(s, d) for s, d in...  16.9 us
    all_to_all x1, blocking collectives, exchanged(): return lax.all_to_all(pieces, 'view', 0, 0, tiled=True)  13.7 us
    all_to_all x1, starting transfers between devices, exchanged(): return lax.all_to_all(pieces, 'view', 0, 0, tiled=True)  7.4 us
  transfers between devices with their start and end apart: 22, of which 12 were waited for; matrix products, arithmetic and copies ran while one was open for 0% of the time, Pallas kernels for 7%

profile of v6, /device:TPU:16, one launch (start us, length us, event | category | flops | bytes accessed | tf_op | source)
XLA Modules:
  0.0 156.8 jit_solution(1935277939114352956)
XLA Ops:
  0.0 2.2 %shard_map.57 = f32[4,520,128]{2,1,0:T(8,128)} custom-call(bf16[32,64,128]{2,1,0:T(8,128)(2,1)} %bitcast.4, f32[1,33]{1,0:T(1,128)} %refs_0_.1, f32[1,33]{1,0:T(1,128)} %refs_1_.1, f32[1,33]{1,0:T(1,128)} %refs_2_.1), custom_call_target="tpu_custom_call" | custom-call | tf_op jit(solution)/shard_map/pallas_call | solution.py:21
  2.2 7.4 %all-to-all-start = ((f32[4,520,128]{2,1,0:T(8,128)}), f32[4,520,128]{2,1,0:T(8,128)S(1)}, u32[]{:S(2)}, u32[]{:S(2)}) async-start(f32[4,520,128]{2,1,0:T(8,128)} %shard_map.57), calls=%async_computation | async-start | bytes 2129920 | tf_op jit(solution)/shard_map/all_to_all | solution.py:224
  10.4 1.9 %collective-permute-start.1 = (f32[16,48,128]{2,1,0:T(8,128)S(1)}, f32[16,48,128]{2,1,0:T(8,128)S(1)}, u32[]{:S(2)}, u32[]{:S(2)}) collective-permute-start(f32[16,48,128]{2,1,0:T(8,128)S(1)} %get-tuple-element.17.refs_2_), channel_id=1, source_target_pairs={{0,32},{32,64},{64,96},{96,128},{128,160},{160,192},{192,224},{224... | collective-permute-start | bytes 1179656 | tf_op jit(solution)/shard_map/ppermute | solution.py:210
  12.3 3.6 %collective-permute-start.2 = (f32[16,48,128]{2,1,0:T(8,128)S(1)}, f32[16,48,128]{2,1,0:T(8,128)S(1)}, u32[]{:S(2)}, u32[]{:S(2)}) collective-permute-start(f32[16,48,128]{2,1,0:T(8,128)S(1)} %get-tuple-element.18.refs_1_), channel_id=1, source_target_pairs={{32,0},{64,32},{96,64},{128,96},{160,128},{192,160},{224,192},{256... | collective-permute-start | bytes 1179656 | tf_op jit(solution)/shard_map/ppermute | solution.py:214
  16.0 19.7 %all-to-all-done.packed_ref.data_ref = f32[4,520,128]{2,1,0:T(8,128)S(1)} async-done(((f32[4,520,128]{2,1,0:T(8,128)}), f32[4,520,128]{2,1,0:T(8,128)S(1)}, u32[]{:S(2)}, u32[]{:S(2)}) %all-to-all-start) | async-done | bytes 1064992 | tf_op jit(solution)/shard_map/all_to_all | solution.py:224
  41.8 3.6 %collective-permute-start.8 = (f32[4,16,16,128]{3,2,1,0:T(8,128)S(1)}, f32[4,16,16,128]{3,2,1,0:T(8,128)S(1)}, u32[]{:S(2)}, u32[]{:S(2)}) collective-permute-start(f32[4,16,16,128]{3,2,1,0:T(8,128)S(1)} %shard_map.61.own_ref.before_ref), channel_id=1, source_target_pairs={{32,0},{64,32},{96,64},{128,96},{160,128},{192,160},{224,192},{256... | collective-permute-start | bytes 1572872 | tf_op jit(solution)/shard_map/ppermute | solution.py:214
  46.6 2.7 %collective-permute-done.3.before_ref = f32[4,16,16,128]{3,2,1,0:T(8,128)S(1)} collective-permute-done((f32[4,16,16,128]{3,2,1,0:T(8,128)S(1)}, f32[4,16,16,128]{3,2,1,0:T(8,128)S(1)}, u32[]{:S(2)}, u32[]{:S(2)}) %collective-permute-start.3) | collective-permute-done | bytes 524320 | tf_op jit(solution)/shard_map/ppermute | solution.py:210
  54.5 5.2 %collective-permute-start.9 = (f32[4,16,16,128]{3,2,1,0:T(8,128)S(1)}, f32[4,16,16,128]{3,2,1,0:T(8,128)S(1)}, u32[]{:S(2)}, u32[]{:S(2)}) collective-permute-start(f32[4,16,16,128]{3,2,1,0:T(8,128)S(1)} %shard_map.66.own_ref), channel_id=1, source_target_pairs={{0,1},{1,2},{2,3},{3,4},{4,5},{5,6},{6,7},{7,8},{8,9},{9,10},{10,1... | collective-permute-start | bytes 1572872 | tf_op jit(solution)/shard_map/ppermute | solution.py:210
  59.7 3.9 %collective-permute-done.4.before_ref = f32[4,16,16,128]{3,2,1,0:T(8,128)S(1)} collective-permute-done((f32[4,16,16,128]{3,2,1,0:T(8,128)S(1)}, f32[4,16,16,128]{3,2,1,0:T(8,128)S(1)}, u32[]{:S(2)}, u32[]{:S(2)}) %collective-permute-start.4) | collective-permute-done | bytes 524320 | tf_op jit(solution)/shard_map/ppermute | solution.py:210
  63.5 4.4 %collective-permute-done.5.after_ref = f32[4,16,16,128]{3,2,1,0:T(8,128)S(1)} collective-permute-done((f32[4,16,16,128]{3,2,1,0:T(8,128)S(1)}, f32[4,16,16,128]{3,2,1,0:T(8,128)S(1)}, u32[]{:S(2)}, u32[]{:S(2)}) %collective-permute-start.5) | collective-permute-done | bytes 524320 | tf_op jit(solution)/shard_map/ppermute | solution.py:214
  68.8 3.1 %collective-permute-start.6 = (f32[16,16,128]{2,1,0:T(8,128)S(1)}, f32[16,16,128]{2,1,0:T(8,128)S(1)}, u32[]{:S(2)}, u32[]{:S(2)}) collective-permute-start(f32[16,16,128]{2,1,0:T(8,128)S(1)} %shard_map.64.own_ref.estimate_ref), channel_id=1, source_target_pairs={{0,1},{1,2},{2,3},{3,4},{4,5},{5,6},{6,7},{7,8},{8,9},{9,10},{10,1... | collective-permute-start | bytes 393224 | tf_op jit(solution)/shard_map/ppermute | solution.py:210
  73.2 5.3 %collective-permute-done.10.after_ref = f32[4,16,16,128]{3,2,1,0:T(8,128)S(1)} collective-permute-done((f32[4,16,16,128]{3,2,1,0:T(8,128)S(1)}, f32[4,16,16,128]{3,2,1,0:T(8,128)S(1)}, u32[]{:S(2)}, u32[]{:S(2)}) %collective-permute-start.10) | collective-permute-done | bytes 524320 | tf_op jit(solution)/shard_map/ppermute | solution.py:214
  79.3 2.7 %collective-permute-start.11 = (f32[16,16,128]{2,1,0:T(8,128)S(1)}, f32[16,16,128]{2,1,0:T(8,128)S(1)}, u32[]{:S(2)}, u32[]{:S(2)}) collective-permute-start(f32[16,16,128]{2,1,0:T(8,128)S(1)} %shard_map.67.own_ref.estimate_ref), channel_id=1, source_target_pairs={{0,1},{1,2},{2,3},{3,4},{4,5},{5,6},{6,7},{7,8},{8,9},{9,10},{10,1... | collective-permute-start | bytes 393224 | tf_op jit(solution)/shard_map/ppermute | solution.py:210
  85.5 7.5 %collective-permute-done.12.after_ref = f32[16,16,128]{2,1,0:T(8,128)S(1)} collective-permute-done((f32[16,16,128]{2,1,0:T(8,128)S(1)}, f32[16,16,128]{2,1,0:T(8,128)S(1)}, u32[]{:S(2)}, u32[]{:S(2)}) %collective-permute-start.12) | collective-permute-done | bytes 131104 | tf_op jit(solution)/shard_map/ppermute | solution.py:214
  96.3 3.9 %collective-permute-start.14 = (f32[4,16,16,128]{3,2,1,0:T(8,128)S(1)}, f32[4,16,16,128]{3,2,1,0:T(8,128)S(1)}, u32[]{:S(2)}, u32[]{:S(2)}) collective-permute-start(f32[4,16,16,128]{3,2,1,0:T(8,128)S(1)} %shard_map.69.after_ref.own_ref), channel_id=1, source_target_pairs={{0,32},{32,64},{64,96},{96,128},{128,160},{160,192},{192,224},{224... | collective-permute-start | bytes 1572872 | tf_op jit(solution)/shard_map/ppermute | solution.py:210
  100.2 3.5 %collective-permute-done.15.before_ref = f32[4,16,16,128]{3,2,1,0:T(8,128)S(1)} collective-permute-done((f32[4,16,16,128]{3,2,1,0:T(8,128)S(1)}, f32[4,16,16,128]{3,2,1,0:T(8,128)S(1)}, u32[]{:S(2)}, u32[]{:S(2)}) %collective-permute-start.15) | collective-permute-done | bytes 524320 | tf_op jit(solution)/shard_map/ppermute | solution.py:210
  106.8 2.5 %collective-permute-done.14.before_ref = f32[4,16,16,128]{3,2,1,0:T(8,128)S(1)} collective-permute-done((f32[4,16,16,128]{3,2,1,0:T(8,128)S(1)}, f32[4,16,16,128]{3,2,1,0:T(8,128)S(1)}, u32[]{:S(2)}, u32[]{:S(2)}) %collective-permute-start.14) | collective-permute-done | bytes 524320 | tf_op jit(solution)/shard_map/ppermute | solution.py:210
  109.9 4.9 %collective-permute-start.16 = (f32[4,16,16,128]{3,2,1,0:T(8,128)S(1)}, f32[4,16,16,128]{3,2,1,0:T(8,128)S(1)}, u32[]{:S(2)}, u32[]{:S(2)}) collective-permute-start(f32[4,16,16,128]{3,2,1,0:T(8,128)S(1)} %shard_map.71.own_ref), channel_id=1, source_target_pairs={{0,1},{1,2},{2,3},{3,4},{4,5},{5,6},{6,7},{7,8},{8,9},{9,10},{10,1... | collective-permute-start | bytes 1572872 | tf_op jit(solution)/shard_map/ppermute | solution.py:210
  116.8 4.6 %collective-permute-start.19 = (f32[4,16,16,128]{3,2,1,0:T(8,128)S(1)}, f32[4,16,16,128]{3,2,1,0:T(8,128)S(1)}, u32[]{:S(2)}, u32[]{:S(2)}) collective-permute-start(f32[4,16,16,128]{3,2,1,0:T(8,128)S(1)} %shard_map.73.own_ref), channel_id=1, source_target_pairs={{0,1},{1,2},{2,3},{3,4},{4,5},{5,6},{6,7},{7,8},{8,9},{9,10},{10,1... | collective-permute-start | bytes 1572872 | tf_op jit(solution)/shard_map/ppermute | solution.py:210
  122.7 4.4 %collective-permute-done.16.before_ref = f32[4,16,16,128]{3,2,1,0:T(8,128)S(1)} collective-permute-done((f32[4,16,16,128]{3,2,1,0:T(8,128)S(1)}, f32[4,16,16,128]{3,2,1,0:T(8,128)S(1)}, u32[]{:S(2)}, u32[]{:S(2)}) %collective-permute-start.16) | collective-permute-done | bytes 524320 | tf_op jit(solution)/shard_map/ppermute | solution.py:210
  127.1 4.4 %collective-permute-done.17.after_ref = f32[4,16,16,128]{3,2,1,0:T(8,128)S(1)} collective-permute-done((f32[4,16,16,128]{3,2,1,0:T(8,128)S(1)}, f32[4,16,16,128]{3,2,1,0:T(8,128)S(1)}, u32[]{:S(2)}, u32[]{:S(2)}) %collective-permute-start.17) | collective-permute-done | bytes 524320 | tf_op jit(solution)/shard_map/ppermute | solution.py:214
  132.4 4.8 %collective-permute-done.19.before_ref = f32[4,16,16,128]{3,2,1,0:T(8,128)S(1)} collective-permute-done((f32[4,16,16,128]{3,2,1,0:T(8,128)S(1)}, f32[4,16,16,128]{3,2,1,0:T(8,128)S(1)}, u32[]{:S(2)}, u32[]{:S(2)}) %collective-permute-start.19) | collective-permute-done | bytes 524320 | tf_op jit(solution)/shard_map/ppermute | solution.py:210
  137.2 4.4 %collective-permute-done.20.after_ref = f32[4,16,16,128]{3,2,1,0:T(8,128)S(1)} collective-permute-done((f32[4,16,16,128]{3,2,1,0:T(8,128)S(1)}, f32[4,16,16,128]{3,2,1,0:T(8,128)S(1)}, u32[]{:S(2)}, u32[]{:S(2)}) %collective-permute-start.20) | collective-permute-done | bytes 524320 | tf_op jit(solution)/shard_map/ppermute | solution.py:214
  142.4 13.7 %all_to_all.10.pieces_ref = f32[4,8,16,128]{3,2,1,0:T(8,128)S(1)} all-to-all(f32[4,8,16,128]{3,2,1,0:T(8,128)S(1)} %bitcast.3), channel_id=1, replica_groups=mesh['gx'=16,'gy'=8,'view'=4] {'view'}, dimensions={0} | all-to-all | bytes 524288 | tf_op jit(solution)/shard_map/all_to_all | solution.py:224
  (45 shorter events, 32.2 us)
Async XLA Ops:
  2.2 7.4 %copy-start = (f32[32,64,128]{2,1,0:T(8,128)S(1)}, f32[32,64,128]{2,1,0:T(8,128)}, u32[]{:S(2)}) copy-start(f32[32,64,128]{2,1,0:T(8,128)} %tile_ref.3) | copy-start | bytes 3145732
  2.2 33.5 %all-to-all-start = ((f32[4,520,128]{2,1,0:T(8,128)}), f32[4,520,128]{2,1,0:T(8,128)S(1)}, u32[]{:S(2)}, u32[]{:S(2)}) async-start(f32[4,520,128]{2,1,0:T(8,128)} %shard_map.57), calls=%async_computation | async-start | bytes 2129920 | tf_op jit(solution)/shard_map/all_to_all | solution.py:224
  9.6 0.7 collective-permute-start
  10.4 26.7 %collective-permute-start.1 = (f32[16,48,128]{2,1,0:T(8,128)S(1)}, f32[16,48,128]{2,1,0:T(8,128)S(1)}, u32[]{:S(2)}, u32[]{:S(2)}) collective-permute-start(f32[16,48,128]{2,1,0:T(8,128)S(1)} %get-tuple-element.17.refs_2_), channel_id=1, source_target_pairs={{0,32},{32,64},{64,96},{96,128},{128,160},{160,192},{192,224},{224... | collective-permute-start | bytes 1179656 | tf_op jit(solution)/shard_map/ppermute | solution.py:210
  12.3 24.8 %collective-permute-start.2 = (f32[16,48,128]{2,1,0:T(8,128)S(1)}, f32[16,48,128]{2,1,0:T(8,128)S(1)}, u32[]{:S(2)}, u32[]{:S(2)}) collective-permute-start(f32[16,48,128]{2,1,0:T(8,128)S(1)} %get-tuple-element.18.refs_1_), channel_id=1, source_target_pairs={{32,0},{64,32},{96,64},{128,96},{160,128},{192,160},{224,192},{256... | collective-permute-start | bytes 1179656 | tf_op jit(solution)/shard_map/ppermute | solution.py:214
  38.7 10.5 %collective-permute-start.3 = (f32[4,16,16,128]{3,2,1,0:T(8,128)S(1)}, f32[4,16,16,128]{3,2,1,0:T(8,128)S(1)}, u32[]{:S(2)}, u32[]{:S(2)}) collective-permute-start(f32[4,16,16,128]{3,2,1,0:T(8,128)S(1)} %shard_map.60.after_ref.own_ref), channel_id=1, source_target_pairs={{0,32},{32,64},{64,96},{96,128},{128,160},{160,192},{192,224},{224... | collective-permute-start | bytes 1572872 | tf_op jit(solution)/shard_map/ppermute | solution.py:210
  41.8 10.7 %collective-permute-start.8 = (f32[4,16,16,128]{3,2,1,0:T(8,128)S(1)}, f32[4,16,16,128]{3,2,1,0:T(8,128)S(1)}, u32[]{:S(2)}, u32[]{:S(2)}) collective-permute-start(f32[4,16,16,128]{3,2,1,0:T(8,128)S(1)} %shard_map.61.own_ref.before_ref), channel_id=1, source_target_pairs={{32,0},{64,32},{96,64},{128,96},{160,128},{192,160},{224,192},{256... | collective-permute-start | bytes 1572872 | tf_op jit(solution)/shard_map/ppermute | solution.py:214
  49.9 13.7 %collective-permute-start.4 = (f32[4,16,16,128]{3,2,1,0:T(8,128)S(1)}, f32[4,16,16,128]{3,2,1,0:T(8,128)S(1)}, u32[]{:S(2)}, u32[]{:S(2)}) collective-permute-start(f32[4,16,16,128]{3,2,1,0:T(8,128)S(1)} %shard_map.63.own_ref), channel_id=1, source_target_pairs={{0,1},{1,2},{2,3},{3,4},{4,5},{5,6},{6,7},{7,8},{8,9},{9,10},{10,1... | collective-permute-start | bytes 1572872 | tf_op jit(solution)/shard_map/ppermute | solution.py:210
  51.2 16.8 %collective-permute-start.5 = (f32[4,16,16,128]{3,2,1,0:T(8,128)S(1)}, f32[4,16,16,128]{3,2,1,0:T(8,128)S(1)}, u32[]{:S(2)}, u32[]{:S(2)}) collective-permute-start(f32[4,16,16,128]{3,2,1,0:T(8,128)S(1)} %shard_map.63.own_ref), channel_id=1, source_target_pairs={{1,0},{2,1},{3,2},{4,3},{5,4},{6,5},{7,6},{8,7},{9,8},{10,9},{11,1... | collective-permute-start | bytes 1572872 | tf_op jit(solution)/shard_map/ppermute | solution.py:214
  53.2 25.3 %collective-permute-start.10 = (f32[4,16,16,128]{3,2,1,0:T(8,128)S(1)}, f32[4,16,16,128]{3,2,1,0:T(8,128)S(1)}, u32[]{:S(2)}, u32[]{:S(2)}) collective-permute-start(f32[4,16,16,128]{3,2,1,0:T(8,128)S(1)} %shard_map.66.own_ref), channel_id=1, source_target_pairs={{1,0},{2,1},{3,2},{4,3},{5,4},{6,5},{7,6},{8,7},{9,8},{10,9},{11,1... | collective-permute-start | bytes 1572872 | tf_op jit(solution)/shard_map/ppermute | solution.py:214
  54.5 24.0 %collective-permute-start.9 = (f32[4,16,16,128]{3,2,1,0:T(8,128)S(1)}, f32[4,16,16,128]{3,2,1,0:T(8,128)S(1)}, u32[]{:S(2)}, u32[]{:S(2)}) collective-permute-start(f32[4,16,16,128]{3,2,1,0:T(8,128)S(1)} %shard_map.66.own_ref), channel_id=1, source_target_pairs={{0,1},{1,2},{2,3},{3,4},{4,5},{5,6},{6,7},{7,8},{8,9},{9,10},{10,1... | collective-permute-start | bytes 1572872 | tf_op jit(solution)/shard_map/ppermute | solution.py:210
  68.8 14.5 %collective-permute-start.6 = (f32[16,16,128]{2,1,0:T(8,128)S(1)}, f32[16,16,128]{2,1,0:T(8,128)S(1)}, u32[]{:S(2)}, u32[]{:S(2)}) collective-permute-start(f32[16,16,128]{2,1,0:T(8,128)S(1)} %shard_map.64.own_ref.estimate_ref), channel_id=1, source_target_pairs={{0,1},{1,2},{2,3},{3,4},{4,5},{5,6},{6,7},{7,8},{8,9},{9,10},{10,1... | collective-permute-start | bytes 393224 | tf_op jit(solution)/shard_map/ppermute | solution.py:210
  71.9 11.4 %collective-permute-start.7 = (f32[16,16,128]{2,1,0:T(8,128)S(1)}, f32[16,16,128]{2,1,0:T(8,128)S(1)}, u32[]{:S(2)}, u32[]{:S(2)}) collective-permute-start(f32[16,16,128]{2,1,0:T(8,128)S(1)} %shard_map.64.own_ref.estimate_ref), channel_id=1, source_target_pairs={{1,0},{2,1},{3,2},{4,3},{5,4},{6,5},{7,6},{8,7},{9,8},{10,9},{11,1... | collective-permute-start | bytes 393224 | tf_op jit(solution)/shard_map/ppermute | solution.py:214
  79.3 6.2 %collective-permute-start.11 = (f32[16,16,128]{2,1,0:T(8,128)S(1)}, f32[16,16,128]{2,1,0:T(8,128)S(1)}, u32[]{:S(2)}, u32[]{:S(2)}) collective-permute-start(f32[16,16,128]{2,1,0:T(8,128)S(1)} %shard_map.67.own_ref.estimate_ref), channel_id=1, source_target_pairs={{0,1},{1,2},{2,3},{3,4},{4,5},{5,6},{6,7},{7,8},{8,9},{9,10},{10,1... | collective-permute-start | bytes 393224 | tf_op jit(solution)/shard_map/ppermute | solution.py:210
  82.0 11.0 %collective-permute-start.12 = (f32[16,16,128]{2,1,0:T(8,128)S(1)}, f32[16,16,128]{2,1,0:T(8,128)S(1)}, u32[]{:S(2)}, u32[]{:S(2)}) collective-permute-start(f32[16,16,128]{2,1,0:T(8,128)S(1)} %shard_map.67.own_ref.estimate_ref), channel_id=1, source_target_pairs={{1,0},{2,1},{3,2},{4,3},{5,4},{6,5},{7,6},{8,7},{9,8},{10,9},{11,1... | collective-permute-start | bytes 393224 | tf_op jit(solution)/shard_map/ppermute | solution.py:214
  83.5 11.6 %collective-permute-start.13 = (f32[4,16,16,128]{3,2,1,0:T(8,128)S(1)}, f32[4,16,16,128]{3,2,1,0:T(8,128)S(1)}, u32[]{:S(2)}, u32[]{:S(2)}) collective-permute-start(f32[4,16,16,128]{3,2,1,0:T(8,128)S(1)} %shard_map.65.before_ref.own_ref), channel_id=1, source_target_pairs={{32,0},{64,32},{96,64},{128,96},{160,128},{192,160},{224,192},{256... | collective-permute-start | bytes 1572872 | tf_op jit(solution)/shard_map/ppermute | solution.py:214
  93.2 10.5 %collective-permute-start.15 = (f32[4,16,16,128]{3,2,1,0:T(8,128)S(1)}, f32[4,16,16,128]{3,2,1,0:T(8,128)S(1)}, u32[]{:S(2)}, u32[]{:S(2)}) collective-permute-start(f32[4,16,16,128]{3,2,1,0:T(8,128)S(1)} %shard_map.68.own_ref.after_ref), channel_id=1, source_target_pairs={{0,32},{32,64},{64,96},{96,128},{128,160},{160,192},{192,224},{224... | collective-permute-start | bytes 1572872 | tf_op jit(solution)/shard_map/ppermute | solution.py:210
  96.3 13.0 %collective-permute-start.14 = (f32[4,16,16,128]{3,2,1,0:T(8,128)S(1)}, f32[4,16,16,128]{3,2,1,0:T(8,128)S(1)}, u32[]{:S(2)}, u32[]{:S(2)}) collective-permute-start(f32[4,16,16,128]{3,2,1,0:T(8,128)S(1)} %shard_map.69.after_ref.own_ref), channel_id=1, source_target_pairs={{0,32},{32,64},{64,96},{96,128},{128,160},{160,192},{192,224},{224... | collective-permute-start | bytes 1572872 | tf_op jit(solution)/shard_map/ppermute | solution.py:210
  104.8 11.3 %collective-permute-start.18 = (f32[4,16,16,128]{3,2,1,0:T(8,128)S(1)}, f32[4,16,16,128]{3,2,1,0:T(8,128)S(1)}, u32[]{:S(2)}, u32[]{:S(2)}) collective-permute-start(f32[4,16,16,128]{3,2,1,0:T(8,128)S(1)} %shard_map.70.own_ref.before_ref), channel_id=1, source_target_pairs={{32,0},{64,32},{96,64},{128,96},{160,128},{192,160},{224,192},{256... | collective-permute-start | bytes 1572872 | tf_op jit(solution)/shard_map/ppermute | solution.py:214
  109.9 17.2 %collective-permute-start.16 = (f32[4,16,16,128]{3,2,1,0:T(8,128)S(1)}, f32[4,16,16,128]{3,2,1,0:T(8,128)S(1)}, u32[]{:S(2)}, u32[]{:S(2)}) collective-permute-start(f32[4,16,16,128]{3,2,1,0:T(8,128)S(1)} %shard_map.71.own_ref), channel_id=1, source_target_pairs={{0,1},{1,2},{2,3},{3,4},{4,5},{5,6},{6,7},{7,8},{8,9},{9,10},{10,1... | collective-permute-start | bytes 1572872 | tf_op jit(solution)/shard_map/ppermute | solution.py:210
  114.8 16.7 %collective-permute-start.17 = (f32[4,16,16,128]{3,2,1,0:T(8,128)S(1)}, f32[4,16,16,128]{3,2,1,0:T(8,128)S(1)}, u32[]{:S(2)}, u32[]{:S(2)}) collective-permute-start(f32[4,16,16,128]{3,2,1,0:T(8,128)S(1)} %shard_map.71.own_ref), channel_id=1, source_target_pairs={{1,0},{2,1},{3,2},{4,3},{5,4},{6,5},{7,6},{8,7},{9,8},{10,9},{11,1... | collective-permute-start | bytes 1572872 | tf_op jit(solution)/shard_map/ppermute | solution.py:214
  116.8 20.4 %collective-permute-start.19 = (f32[4,16,16,128]{3,2,1,0:T(8,128)S(1)}, f32[4,16,16,128]{3,2,1,0:T(8,128)S(1)}, u32[]{:S(2)}, u32[]{:S(2)}) collective-permute-start(f32[4,16,16,128]{3,2,1,0:T(8,128)S(1)} %shard_map.73.own_ref), channel_id=1, source_target_pairs={{0,1},{1,2},{2,3},{3,4},{4,5},{5,6},{6,7},{7,8},{8,9},{9,10},{10,1... | collective-permute-start | bytes 1572872 | tf_op jit(solution)/shard_map/ppermute | solution.py:210
  121.4 20.2 %collective-permute-start.20 = (f32[4,16,16,128]{3,2,1,0:T(8,128)S(1)}, f32[4,16,16,128]{3,2,1,0:T(8,128)S(1)}, u32[]{:S(2)}, u32[]{:S(2)}) collective-permute-start(f32[4,16,16,128]{3,2,1,0:T(8,128)S(1)} %shard_map.73.own_ref), channel_id=1, source_target_pairs={{1,0},{2,1},{3,2},{4,3},{5,4},{6,5},{7,6},{8,7},{9,8},{10,9},{11,1... | collective-permute-start | bytes 1572872 | tf_op jit(solution)/shard_map/ppermute | solution.py:214

commit v7 on v6

--- a/solution.py
+++ b/solution.py
@@ -59,11 +59,14 @@
     out_ref[...] = tile_ref[:, pl.ds(pl.multiple_of(v_ref[0] * width, width), width), :]
 
 
-def shifted_taps(packed_ref, view, axis, rows, shift):
-    row = packed_ref.shape[1] - 8 + axis
-    spread = packed_ref[view, row : row + 1, :]
-    taps = jnp.broadcast_to(spread / jnp.sum(spread, axis=1, keepdims=True), (rows, LANES))
-    turned = pltpu.roll(taps, (LANES - shift) % LANES, 1, stride=1, stride_axis=0)
+def normal_taps(packed_ref):
+    spreads = packed_ref[:, packed_ref.shape[1] - 8 :, :]
+    sums = jnp.sum(spreads, axis=2, keepdims=True)
+    return spreads / jnp.where(sums > 0.0, sums, 1.0)
+
+
+def shifted_taps(taps, rows, shift):
+    turned = pltpu.roll(jnp.broadcast_to(taps, (rows, LANES)), (LANES - shift) % LANES, 1, stride=1, stride_axis=0)
     a = lax.broadcasted_iota(jnp.int32, (rows, LANES), 0)
     b = lax.broadcasted_iota(jnp.int32, (rows, LANES), 1)
     t = b - a + shift
@@ -93,17 +96,19 @@
 
 
 def forward_matrices_kernel(packed_ref, x_ref, y_ref, z_ref):
+    normal = normal_taps(packed_ref)
     for view in range(packed_ref.shape[0]):
         for axis, target in ((0, x_ref.at[view]), (1, y_ref.at[pl.ds(view * HALF, HALF)])):
-            store_bands(flipped(shifted_taps(packed_ref, view, axis, 3 * HALF, 2 * HALF)), target)
-        store_z(shifted_taps(packed_ref, view, 2, LANES, HALF), z_ref.at[view])
+            store_bands(flipped(shifted_taps(normal[view, axis : axis + 1], 3 * HALF, 2 * HALF)), target)
+        store_z(shifted_taps(normal[view, 2:3], LANES, HALF), z_ref.at[view])
 
 
 def adjoint_matrices_kernel(packed_ref, x_ref, y_ref, z_ref):
+    normal = normal_taps(packed_ref)
     for view in range(packed_ref.shape[0]):
         for axis, target in ((0, x_ref.at[view]), (1, y_ref.at[view])):
-            store_bands(shifted_taps(packed_ref, view, axis, HALF, 0), target)
-        store_z(shifted_taps(packed_ref, view, 2, LANES, HALF).T, z_ref.at[view])
+            store_bands(shifted_taps(normal[view, axis : axis + 1], HALF, 0), target)
+        store_z(shifted_taps(normal[view, 2:3], LANES, HALF).T, z_ref.at[view])
 
 
 def banded(matrix, pieces):
@@ -115,21 +120,29 @@
     return jnp.concatenate([ref[i] for i in range(count)], axis=1)
 
 
-def blur_x(refs, matrix, out_ref):
-    rows, width, _ = out_ref.shape
+def stacked(blurred):
+    count = blurred.shape[1] // LANES
+    return jnp.concatenate([blurred[:, j * LANES : (j + 1) * LANES] for j in range(count)], axis=0)
+
+
+def blurred_x(refs, matrix):
+    rows, width, _ = refs[0].shape
     flat = [ref.reshape(rows * width, LANES) for ref in refs]
     pieces = [jnp.concatenate([ref[pl.ds(j, rows, stride=width), :] for j in range(width)], axis=1) for ref in flat]
-    blurred = banded(matrix, pieces)
+    return stacked(banded(matrix, pieces))
+
+
+def by_rows(columns, out_ref):
+    rows, width, _ = out_ref.shape
     target = out_ref.reshape(rows * width, LANES)
     for j in range(width):
-        target[pl.ds(j, rows, stride=width), :] = blurred[:, j * LANES : (j + 1) * LANES]
+        target[pl.ds(j, rows, stride=width), :] = columns[j * rows : (j + 1) * rows]
 
 
 def blur_z(value, matrix):
-    rows, width, _ = value.shape
-    high, low = split(value.reshape(rows * width, LANES))
+    high, low = split(value)
     product = jnp.dot(jnp.concatenate([high, low], axis=1), matrix, preferred_element_type=jnp.float32)
-    return (product[:, :LANES] + product[:, LANES:]).reshape(rows, width, LANES)
+    return product[:, :LANES] + product[:, LANES:]
 
 
 def forward_y(pieces, matrix_ref, out_ref):
@@ -171,29 +184,29 @@
         forward_y([beside(ext_ref, ext_ref.shape[0])], matrix_ref, out_ref)
 
 
-def ratio_kernel(first, before_ref, own_ref, after_ref, bands_ref, matrix_ref, data_ref, out_ref, mid_ref):
+def ratio_kernel(first, before_ref, own_ref, after_ref, bands_ref, matrix_ref, data_ref, out_ref):
     views, rows, width, _ = out_ref.shape
     for view in range(views):
-        blur_x([ref.at[view] for ref in (before_ref, own_ref, after_ref)], bands_ref[view], mid_ref.at[view])
-        data = data_ref[view, pl.ds(first * width, rows * width)].reshape(rows, width, LANES)
-        out_ref[view] = data / blur_z(mid_ref[view], matrix_ref[view])
+        blurred = blurred_x([ref.at[view] for ref in (before_ref, own_ref, after_ref)], bands_ref[view])
+        blurred = blur_z(blurred, matrix_ref[view])
+        data = [data_ref[view, pl.ds(first * width + j, rows, stride=width), :] for j in range(width)]
+        by_rows(jnp.concatenate(data, axis=0) / blurred, out_ref.at[view])
 
 
 def adjoint_x_kernel(before_ref, own_ref, after_ref, bands_ref, out_ref):
     for view in range(out_ref.shape[0]):
-        blur_x([ref.at[view] for ref in (before_ref, own_ref, after_ref)], bands_ref[view], out_ref.at[view])
-
-
-def update_kernel(first, before_ref, own_ref, after_ref, bands_ref, matrix_ref, estimate_ref, out_ref, mid_ref):
-    views, rows = own_ref.shape[:2]
+        blurred = blurred_x([ref.at[view] for ref in (before_ref, own_ref, after_ref)], bands_ref[view])
+        by_rows(blurred, out_ref.at[view])
+
+
+def update_kernel(first, before_ref, own_ref, after_ref, bands_ref, matrix_ref, estimate_ref, out_ref):
+    views, rows, width, _ = own_ref.shape
     total = None
     for view in range(views):
         blurred = banded(bands_ref[view], [beside(ref.at[view], rows) for ref in (before_ref, own_ref, after_ref)])
-        for i in range(rows):
-            mid_ref[view, i] = blurred[:, i * LANES : (i + 1) * LANES]
-        terms = jnp.log(blur_z(mid_ref[view], matrix_ref[view]))
+        terms = jnp.log(blur_z(stacked(blurred), matrix_ref[view]))
         total = terms if total is None else total + terms
-    out_ref[...] = estimate_ref[pl.ds(first, rows)] * jnp.exp(total / views)
+    out_ref[...] = estimate_ref[pl.ds(first, rows)] * jnp.exp(total / views).reshape(rows, width, LANES)
 
 
 def collect_kernel(pieces_ref, out_ref):
@@ -238,7 +251,6 @@
     bands_shape = ((views, HALF, 9 * HALF), jnp.bfloat16)
     matrix_shape = ((views, 2 * LANES, 2 * LANES), jnp.bfloat16)
     part = ((half, width, depth), f32)
-    mid = [pltpu.VMEM(*half_shape)]
 
     own = call(part_kernel, [((rows, width, depth), f32)], [], v_word, estimate)[0]
     packed = call(
@@ -266,7 +278,7 @@
             ]
             before, after = onward(high, "gx"), back(low, "gx")
         ratio_low, ratio_high = [
-            call(functools.partial(ratio_kernel, n * half), [half_shape], mid, *three, forward_x, forward_z, packed)[0]
+            call(functools.partial(ratio_kernel, n * half), [half_shape], [], *three, forward_x, forward_z, packed)[0]
             for n, three in enumerate(((before, low, high), (low, high, after)))
         ]
         before, after = onward(ratio_high, "gx"), back(ratio_low, "gx")
@@ -275,7 +287,7 @@
         ins = [(onward(value, y), value, back(value, y), adjoint_y, adjoint_z) for value in (low, high)]
         olds = [(0, own[0]), (0, own[1])] if step_number else [(0, own), (half, own)]
         own = [
-            call(functools.partial(update_kernel, first), [part], mid, *ins[n], old)[0]
+            call(functools.partial(update_kernel, first), [part], [], *ins[n], old)[0]
             for n, (first, old) in enumerate(olds)
         ]
     share = rows // views

time: 158 us -> 156 us (0.987)
  the two profiles are of different devices: /device:TPU:16 before, /device:TPU:22 now
where the time goes in v7:
time: 156 us
  starting transfers between devices  85.1 us (55%)
  waiting for transfers between devices  42.7 us (27%)
  Pallas kernels  14.6 us (9%)
  blocking collectives  12.9 us (8%)
    ppermute x10, starting transfers between devices, back(): return lax.ppermute(value, axes, shifted(lax.axis_size(axes), -1))  45.5 us
    ppermute x10, starting transfers between devices, onward(): return lax.ppermute(value, axes, shifted(lax.axis_size(axes), 1))  23.1 us
    ppermute x10, waiting for transfers between devices, onward(): return lax.ppermute(value, axes, shifted(lax.axis_size(axes), 1))  19.8 us
    pallas_call x21, Pallas kernels, call(): pl.pallas_call(kernel, out_shape=[jax.ShapeDtypeStruct(s, d) for s, d in...  14.6 us
    all_to_all x1, blocking collectives, exchanged(): return lax.all_to_all(pieces, 'view', 0, 0, tiled=True)  12.9 us
    ppermute x10, waiting for transfers between devices, back(): return lax.ppermute(value, axes, shifted(lax.axis_size(axes), -1))  11.5 us
    ppermute x1, starting transfers between devices, across(): lax.ppermute(value, ('gy', 'view'), pairs + [(b, a) for a, b in pairs])  9.05 us
    all_to_all x1, starting transfers between devices, exchanged(): return lax.all_to_all(pieces, 'view', 0, 0, tiled=True)  7.4 us
  transfers between devices with their start and end apart: 22, of which 13 were waited for; matrix products, arithmetic and copies ran while one was open for 0% of the time, Pallas kernels for 6%

profile of v7, /device:TPU:22, one launch (start us, length us, event | category | flops | bytes accessed | tf_op | source)
XLA Modules:
  0.0 155.7 jit_solution(2815407945429293783)
XLA Ops:
  0.0 2.2 %shard_map.57 = f32[4,520,128]{2,1,0:T(8,128)} custom-call(bf16[32,64,128]{2,1,0:T(8,128)(2,1)} %bitcast.4, f32[1,33]{1,0:T(1,128)} %refs_0_.1, f32[1,33]{1,0:T(1,128)} %refs_1_.1, f32[1,33]{1,0:T(1,128)} %refs_2_.1), custom_call_target="tpu_custom_call" | custom-call | tf_op jit(solution)/shard_map/pallas_call | solution.py:21
  2.2 7.4 %all-to-all-start = ((f32[4,520,128]{2,1,0:T(8,128)}), f32[4,520,128]{2,1,0:T(8,128)S(1)}, u32[]{:S(2)}, u32[]{:S(2)}) async-start(f32[4,520,128]{2,1,0:T(8,128)} %shard_map.57), calls=%async_computation | async-start | bytes 2129920 | tf_op jit(solution)/shard_map/all_to_all | solution.py:237
  9.6 9.0 %collective-permute-start = (f32[32,16,128]{2,1,0:T(8,128)S(1)}, f32[32,16,128]{2,1,0:T(8,128)S(1)}, u32[]{:S(2)}, u32[]{:S(2)}) collective-permute-start(f32[32,16,128]{2,1,0:T(8,128)S(1)} %shard_map.55.estimate_ref), channel_id=1, source_target_pairs={{3,4},{7,8},{11,12},{15,16},{19,20},{23,24},{27,28},{4,3},{8,7},{1... | collective-permute-start | bytes 786440 | tf_op jit(solution)/shard_map/ppermute | solution.py:233
  18.7 5.7 %collective-permute-done.across_ref = f32[32,16,128]{2,1,0:T(8,128)S(1)} collective-permute-done((f32[32,16,128]{2,1,0:T(8,128)S(1)}, f32[32,16,128]{2,1,0:T(8,128)S(1)}, u32[]{:S(2)}, u32[]{:S(2)}) %collective-permute-start) | collective-permute-done | bytes 262176 | tf_op jit(solution)/shard_map/ppermute | solution.py:233
  26.4 3.6 %collective-permute-start.2 = (f32[16,48,128]{2,1,0:T(8,128)S(1)}, f32[16,48,128]{2,1,0:T(8,128)S(1)}, u32[]{:S(2)}, u32[]{:S(2)}) collective-permute-start(f32[16,48,128]{2,1,0:T(8,128)S(1)} %get-tuple-element.18.refs_1_), channel_id=1, source_target_pairs={{32,0},{64,32},{96,64},{128,96},{160,128},{192,160},{224,192},{256... | collective-permute-start | bytes 1179656 | tf_op jit(solution)/shard_map/ppermute | solution.py:227
  30.1 5.6 %all-to-all-done.packed_ref.data_ref = f32[4,520,128]{2,1,0:T(8,128)S(1)} async-done(((f32[4,520,128]{2,1,0:T(8,128)}), f32[4,520,128]{2,1,0:T(8,128)S(1)}, u32[]{:S(2)}, u32[]{:S(2)}) %all-to-all-start) | async-done | bytes 1064992 | tf_op jit(solution)/shard_map/all_to_all | solution.py:237
  37.8 2.7 %collective-permute-start.3 = (f32[4,16,16,128]{3,2,1,0:T(8,128)S(1)}, f32[4,16,16,128]{3,2,1,0:T(8,128)S(1)}, u32[]{:S(2)}, u32[]{:S(2)}) collective-permute-start(f32[4,16,16,128]{3,2,1,0:T(8,128)S(1)} %shard_map.60.after_ref.own_ref), channel_id=1, source_target_pairs={{0,32},{32,64},{64,96},{96,128},{128,160},{160,192},{192,224},{224... | collective-permute-start | bytes 1572872 | tf_op jit(solution)/shard_map/ppermute | solution.py:223
  41.5 2.9 %collective-permute-start.8 = (f32[4,16,16,128]{3,2,1,0:T(8,128)S(1)}, f32[4,16,16,128]{3,2,1,0:T(8,128)S(1)}, u32[]{:S(2)}, u32[]{:S(2)}) collective-permute-start(f32[4,16,16,128]{3,2,1,0:T(8,128)S(1)} %shard_map.61.own_ref.before_ref), channel_id=1, source_target_pairs={{32,0},{64,32},{96,64},{128,96},{160,128},{192,160},{224,192},{256... | collective-permute-start | bytes 1572872 | tf_op jit(solution)/shard_map/ppermute | solution.py:227
  44.8 3.6 %collective-permute-done.3.before_ref = f32[4,16,16,128]{3,2,1,0:T(8,128)S(1)} collective-permute-done((f32[4,16,16,128]{3,2,1,0:T(8,128)S(1)}, f32[4,16,16,128]{3,2,1,0:T(8,128)S(1)}, u32[]{:S(2)}, u32[]{:S(2)}) %collective-permute-start.3) | collective-permute-done | bytes 524320 | tf_op jit(solution)/shard_map/ppermute | solution.py:223
  50.9 6.7 %collective-permute-start.5 = (f32[4,16,16,128]{3,2,1,0:T(8,128)S(1)}, f32[4,16,16,128]{3,2,1,0:T(8,128)S(1)}, u32[]{:S(2)}, u32[]{:S(2)}) collective-permute-start(f32[4,16,16,128]{3,2,1,0:T(8,128)S(1)} %shard_map.63.own_ref), channel_id=1, source_target_pairs={{1,0},{2,1},{3,2},{4,3},{5,4},{6,5},{7,6},{8,7},{9,8},{10,9},{11,1... | collective-permute-start | bytes 1572872 | tf_op jit(solution)/shard_map/ppermute | solution.py:227
  58.2 3.9 %collective-permute-start.10 = (f32[4,16,16,128]{3,2,1,0:T(8,128)S(1)}, f32[4,16,16,128]{3,2,1,0:T(8,128)S(1)}, u32[]{:S(2)}, u32[]{:S(2)}) collective-permute-start(f32[4,16,16,128]{3,2,1,0:T(8,128)S(1)} %shard_map.66.own_ref), channel_id=1, source_target_pairs={{1,0},{2,1},{3,2},{4,3},{5,4},{6,5},{7,6},{8,7},{9,8},{10,9},{11,1... | collective-permute-start | bytes 1572872 | tf_op jit(solution)/shard_map/ppermute | solution.py:227
  64.1 2.8 %collective-permute-done.4.before_ref = f32[4,16,16,128]{3,2,1,0:T(8,128)S(1)} collective-permute-done((f32[4,16,16,128]{3,2,1,0:T(8,128)S(1)}, f32[4,16,16,128]{3,2,1,0:T(8,128)S(1)}, u32[]{:S(2)}, u32[]{:S(2)}) %collective-permute-start.4) | collective-permute-done | bytes 524320 | tf_op jit(solution)/shard_map/ppermute | solution.py:223
  66.9 3.0 %collective-permute-done.5.after_ref = f32[4,16,16,128]{3,2,1,0:T(8,128)S(1)} collective-permute-done((f32[4,16,16,128]{3,2,1,0:T(8,128)S(1)}, f32[4,16,16,128]{3,2,1,0:T(8,128)S(1)}, u32[]{:S(2)}, u32[]{:S(2)}) %collective-permute-start.5) | collective-permute-done | bytes 524320 | tf_op jit(solution)/shard_map/ppermute | solution.py:227
  72.7 6.5 %collective-permute-start.7 = (f32[16,16,128]{2,1,0:T(8,128)S(1)}, f32[16,16,128]{2,1,0:T(8,128)S(1)}, u32[]{:S(2)}, u32[]{:S(2)}) collective-permute-start(f32[16,16,128]{2,1,0:T(8,128)S(1)} %shard_map.64.own_ref.estimate_ref), channel_id=1, source_target_pairs={{1,0},{2,1},{3,2},{4,3},{5,4},{6,5},{7,6},{8,7},{9,8},{10,9},{11,1... | collective-permute-start | bytes 393224 | tf_op jit(solution)/shard_map/ppermute | solution.py:227
  83.5 6.5 %collective-permute-start.12 = (f32[16,16,128]{2,1,0:T(8,128)S(1)}, f32[16,16,128]{2,1,0:T(8,128)S(1)}, u32[]{:S(2)}, u32[]{:S(2)}) collective-permute-start(f32[16,16,128]{2,1,0:T(8,128)S(1)} %shard_map.67.own_ref.estimate_ref), channel_id=1, source_target_pairs={{1,0},{2,1},{3,2},{4,3},{5,4},{6,5},{7,6},{8,7},{9,8},{10,9},{11,1... | collective-permute-start | bytes 393224 | tf_op jit(solution)/shard_map/ppermute | solution.py:227
  94.9 4.0 %collective-permute-done.13.after_ref = f32[4,16,16,128]{3,2,1,0:T(8,128)S(1)} collective-permute-done((f32[4,16,16,128]{3,2,1,0:T(8,128)S(1)}, f32[4,16,16,128]{3,2,1,0:T(8,128)S(1)}, u32[]{:S(2)}, u32[]{:S(2)}) %collective-permute-start.13) | collective-permute-done | bytes 524320 | tf_op jit(solution)/shard_map/ppermute | solution.py:227
  99.9 4.3 %collective-permute-start.14 = (f32[4,16,16,128]{3,2,1,0:T(8,128)S(1)}, f32[4,16,16,128]{3,2,1,0:T(8,128)S(1)}, u32[]{:S(2)}, u32[]{:S(2)}) collective-permute-start(f32[4,16,16,128]{3,2,1,0:T(8,128)S(1)} %shard_map.69.after_ref.own_ref), channel_id=1, source_target_pairs={{0,32},{32,64},{64,96},{96,128},{128,160},{160,192},{192,224},{224... | collective-permute-start | bytes 1572872 | tf_op jit(solution)/shard_map/ppermute | solution.py:223
  107.1 3.7 %collective-permute-done.14.before_ref = f32[4,16,16,128]{3,2,1,0:T(8,128)S(1)} collective-permute-done((f32[4,16,16,128]{3,2,1,0:T(8,128)S(1)}, f32[4,16,16,128]{3,2,1,0:T(8,128)S(1)}, u32[]{:S(2)}, u32[]{:S(2)}) %collective-permute-start.14) | collective-permute-done | bytes 524320 | tf_op jit(solution)/shard_map/ppermute | solution.py:223
  111.5 2.4 %collective-permute-start.16 = (f32[4,16,16,128]{3,2,1,0:T(8,128)S(1)}, f32[4,16,16,128]{3,2,1,0:T(8,128)S(1)}, u32[]{:S(2)}, u32[]{:S(2)}) collective-permute-start(f32[4,16,16,128]{3,2,1,0:T(8,128)S(1)} %shard_map.71.own_ref), channel_id=1, source_target_pairs={{0,1},{1,2},{2,3},{3,4},{4,5},{5,6},{6,7},{7,8},{8,9},{9,10},{10,1... | collective-permute-start | bytes 1572872 | tf_op jit(solution)/shard_map/ppermute | solution.py:223
  113.9 5.5 %collective-permute-start.17 = (f32[4,16,16,128]{3,2,1,0:T(8,128)S(1)}, f32[4,16,16,128]{3,2,1,0:T(8,128)S(1)}, u32[]{:S(2)}, u32[]{:S(2)}) collective-permute-start(f32[4,16,16,128]{3,2,1,0:T(8,128)S(1)} %shard_map.71.own_ref), channel_id=1, source_target_pairs={{1,0},{2,1},{3,2},{4,3},{5,4},{6,5},{7,6},{8,7},{9,8},{10,9},{11,1... | collective-permute-start | bytes 1572872 | tf_op jit(solution)/shard_map/ppermute | solution.py:227
  122.0 6.0 %collective-permute-start.20 = (f32[4,16,16,128]{3,2,1,0:T(8,128)S(1)}, f32[4,16,16,128]{3,2,1,0:T(8,128)S(1)}, u32[]{:S(2)}, u32[]{:S(2)}) collective-permute-start(f32[4,16,16,128]{3,2,1,0:T(8,128)S(1)} %shard_map.73.own_ref), channel_id=1, source_target_pairs={{1,0},{2,1},{3,2},{4,3},{5,4},{6,5},{7,6},{8,7},{9,8},{10,9},{11,1... | collective-permute-start | bytes 1572872 | tf_op jit(solution)/shard_map/ppermute | solution.py:227
  128.0 2.3 %collective-permute-done.16.before_ref = f32[4,16,16,128]{3,2,1,0:T(8,128)S(1)} collective-permute-done((f32[4,16,16,128]{3,2,1,0:T(8,128)S(1)}, f32[4,16,16,128]{3,2,1,0:T(8,128)S(1)}, u32[]{:S(2)}, u32[]{:S(2)}) %collective-permute-start.16) | collective-permute-done | bytes 524320 | tf_op jit(solution)/shard_map/ppermute | solution.py:223
  132.6 7.4 %collective-permute-done.19.before_ref = f32[4,16,16,128]{3,2,1,0:T(8,128)S(1)} collective-permute-done((f32[4,16,16,128]{3,2,1,0:T(8,128)S(1)}, f32[4,16,16,128]{3,2,1,0:T(8,128)S(1)}, u32[]{:S(2)}, u32[]{:S(2)}) %collective-permute-start.19) | collective-permute-done | bytes 524320 | tf_op jit(solution)/shard_map/ppermute | solution.py:223
  142.1 12.9 %all_to_all.10.pieces_ref = f32[4,8,16,128]{3,2,1,0:T(8,128)S(1)} all-to-all(f32[4,8,16,128]{3,2,1,0:T(8,128)S(1)} %bitcast.3), channel_id=1, replica_groups=mesh['gx'=16,'gy'=8,'view'=4] {'view'}, dimensions={0} | all-to-all | bytes 524288 | tf_op jit(solution)/shard_map/all_to_all | solution.py:237
  (45 shorter events, 34.5 us)
Async XLA Ops:
  2.2 7.4 %copy-start = (f32[32,64,128]{2,1,0:T(8,128)S(1)}, f32[32,64,128]{2,1,0:T(8,128)}, u32[]{:S(2)}) copy-start(f32[32,64,128]{2,1,0:T(8,128)} %tile_ref.3) | copy-start | bytes 3145732
  2.2 33.5 %all-to-all-start = ((f32[4,520,128]{2,1,0:T(8,128)}), f32[4,520,128]{2,1,0:T(8,128)S(1)}, u32[]{:S(2)}, u32[]{:S(2)}) async-start(f32[4,520,128]{2,1,0:T(8,128)} %shard_map.57), calls=%async_computation | async-start | bytes 2129920 | tf_op jit(solution)/shard_map/all_to_all | solution.py:237
  9.6 14.8 %collective-permute-start = (f32[32,16,128]{2,1,0:T(8,128)S(1)}, f32[32,16,128]{2,1,0:T(8,128)S(1)}, u32[]{:S(2)}, u32[]{:S(2)}) collective-permute-start(f32[32,16,128]{2,1,0:T(8,128)S(1)} %shard_map.55.estimate_ref), channel_id=1, source_target_pairs={{3,4},{7,8},{11,12},{15,16},{19,20},{23,24},{27,28},{4,3},{8,7},{1... | collective-permute-start | bytes 786440 | tf_op jit(solution)/shard_map/ppermute | solution.py:233
  24.5 11.9 %collective-permute-start.1 = (f32[16,48,128]{2,1,0:T(8,128)S(1)}, f32[16,48,128]{2,1,0:T(8,128)S(1)}, u32[]{:S(2)}, u32[]{:S(2)}) collective-permute-start(f32[16,48,128]{2,1,0:T(8,128)S(1)} %get-tuple-element.17.refs_2_), channel_id=1, source_target_pairs={{0,32},{32,64},{64,96},{96,128},{128,160},{160,192},{192,224},{224... | collective-permute-start | bytes 1179656 | tf_op jit(solution)/shard_map/ppermute | solution.py:223
  26.4 10.0 %collective-permute-start.2 = (f32[16,48,128]{2,1,0:T(8,128)S(1)}, f32[16,48,128]{2,1,0:T(8,128)S(1)}, u32[]{:S(2)}, u32[]{:S(2)}) collective-permute-start(f32[16,48,128]{2,1,0:T(8,128)S(1)} %get-tuple-element.18.refs_1_), channel_id=1, source_target_pairs={{32,0},{64,32},{96,64},{128,96},{160,128},{192,160},{224,192},{256... | collective-permute-start | bytes 1179656 | tf_op jit(solution)/shard_map/ppermute | solution.py:227
  37.8 10.5 %collective-permute-start.3 = (f32[4,16,16,128]{3,2,1,0:T(8,128)S(1)}, f32[4,16,16,128]{3,2,1,0:T(8,128)S(1)}, u32[]{:S(2)}, u32[]{:S(2)}) collective-permute-start(f32[4,16,16,128]{3,2,1,0:T(8,128)S(1)} %shard_map.60.after_ref.own_ref), channel_id=1, source_target_pairs={{0,32},{32,64},{64,96},{96,128},{128,160},{160,192},{192,224},{224... | collective-permute-start | bytes 1572872 | tf_op jit(solution)/shard_map/ppermute | solution.py:223
  41.5 16.1 %collective-permute-start.8 = (f32[4,16,16,128]{3,2,1,0:T(8,128)S(1)}, f32[4,16,16,128]{3,2,1,0:T(8,128)S(1)}, u32[]{:S(2)}, u32[]{:S(2)}) collective-permute-start(f32[4,16,16,128]{3,2,1,0:T(8,128)S(1)} %shard_map.61.own_ref.before_ref), channel_id=1, source_target_pairs={{32,0},{64,32},{96,64},{128,96},{160,128},{192,160},{224,192},{256... | collective-permute-start | bytes 1572872 | tf_op jit(solution)/shard_map/ppermute | solution.py:227
  49.0 18.0 %collective-permute-start.4 = (f32[4,16,16,128]{3,2,1,0:T(8,128)S(1)}, f32[4,16,16,128]{3,2,1,0:T(8,128)S(1)}, u32[]{:S(2)}, u32[]{:S(2)}) collective-permute-start(f32[4,16,16,128]{3,2,1,0:T(8,128)S(1)} %shard_map.63.own_ref), channel_id=1, source_target_pairs={{0,1},{1,2},{2,3},{3,4},{4,5},{5,6},{6,7},{7,8},{8,9},{9,10},{10,1... | collective-permute-start | bytes 1572872 | tf_op jit(solution)/shard_map/ppermute | solution.py:223
  50.9 19.1 %collective-permute-start.5 = (f32[4,16,16,128]{3,2,1,0:T(8,128)S(1)}, f32[4,16,16,128]{3,2,1,0:T(8,128)S(1)}, u32[]{:S(2)}, u32[]{:S(2)}) collective-permute-start(f32[4,16,16,128]{3,2,1,0:T(8,128)S(1)} %shard_map.63.own_ref), channel_id=1, source_target_pairs={{1,0},{2,1},{3,2},{4,3},{5,4},{6,5},{7,6},{8,7},{9,8},{10,9},{11,1... | collective-permute-start | bytes 1572872 | tf_op jit(solution)/shard_map/ppermute | solution.py:227
  58.2 22.5 %collective-permute-start.10 = (f32[4,16,16,128]{3,2,1,0:T(8,128)S(1)}, f32[4,16,16,128]{3,2,1,0:T(8,128)S(1)}, u32[]{:S(2)}, u32[]{:S(2)}) collective-permute-start(f32[4,16,16,128]{3,2,1,0:T(8,128)S(1)} %shard_map.66.own_ref), channel_id=1, source_target_pairs={{1,0},{2,1},{3,2},{4,3},{5,4},{6,5},{7,6},{8,7},{9,8},{10,9},{11,1... | collective-permute-start | bytes 1572872 | tf_op jit(solution)/shard_map/ppermute | solution.py:227
  62.2 18.6 %collective-permute-start.9 = (f32[4,16,16,128]{3,2,1,0:T(8,128)S(1)}, f32[4,16,16,128]{3,2,1,0:T(8,128)S(1)}, u32[]{:S(2)}, u32[]{:S(2)}) collective-permute-start(f32[4,16,16,128]{3,2,1,0:T(8,128)S(1)} %shard_map.66.own_ref), channel_id=1, source_target_pairs={{0,1},{1,2},{2,3},{3,4},{4,5},{5,6},{6,7},{7,8},{8,9},{9,10},{10,1... | collective-permute-start | bytes 1572872 | tf_op jit(solution)/shard_map/ppermute | solution.py:223
  70.8 19.3 %collective-permute-start.6 = (f32[16,16,128]{2,1,0:T(8,128)S(1)}, f32[16,16,128]{2,1,0:T(8,128)S(1)}, u32[]{:S(2)}, u32[]{:S(2)}) collective-permute-start(f32[16,16,128]{2,1,0:T(8,128)S(1)} %shard_map.64.own_ref.estimate_ref), channel_id=1, source_target_pairs={{0,1},{1,2},{2,3},{3,4},{4,5},{5,6},{6,7},{7,8},{8,9},{9,10},{10,1... | collective-permute-start | bytes 393224 | tf_op jit(solution)/shard_map/ppermute | solution.py:223
  72.7 17.3 %collective-permute-start.7 = (f32[16,16,128]{2,1,0:T(8,128)S(1)}, f32[16,16,128]{2,1,0:T(8,128)S(1)}, u32[]{:S(2)}, u32[]{:S(2)}) collective-permute-start(f32[16,16,128]{2,1,0:T(8,128)S(1)} %shard_map.64.own_ref.estimate_ref), channel_id=1, source_target_pairs={{1,0},{2,1},{3,2},{4,3},{5,4},{6,5},{7,6},{8,7},{9,8},{10,9},{11,1... | collective-permute-start | bytes 393224 | tf_op jit(solution)/shard_map/ppermute | solution.py:227
  81.6 10.6 %collective-permute-start.11 = (f32[16,16,128]{2,1,0:T(8,128)S(1)}, f32[16,16,128]{2,1,0:T(8,128)S(1)}, u32[]{:S(2)}, u32[]{:S(2)}) collective-permute-start(f32[16,16,128]{2,1,0:T(8,128)S(1)} %shard_map.67.own_ref.estimate_ref), channel_id=1, source_target_pairs={{0,1},{1,2},{2,3},{3,4},{4,5},{5,6},{6,7},{7,8},{8,9},{9,10},{10,1... | collective-permute-start | bytes 393224 | tf_op jit(solution)/shard_map/ppermute | solution.py:223
  83.5 9.0 %collective-permute-start.12 = (f32[16,16,128]{2,1,0:T(8,128)S(1)}, f32[16,16,128]{2,1,0:T(8,128)S(1)}, u32[]{:S(2)}, u32[]{:S(2)}) collective-permute-start(f32[16,16,128]{2,1,0:T(8,128)S(1)} %shard_map.67.own_ref.estimate_ref), channel_id=1, source_target_pairs={{1,0},{2,1},{3,2},{4,3},{5,4},{6,5},{7,6},{8,7},{9,8},{10,9},{11,1... | collective-permute-start | bytes 393224 | tf_op jit(solution)/shard_map/ppermute | solution.py:227
  90.3 8.6 %collective-permute-start.13 = (f32[4,16,16,128]{3,2,1,0:T(8,128)S(1)}, f32[4,16,16,128]{3,2,1,0:T(8,128)S(1)}, u32[]{:S(2)}, u32[]{:S(2)}) collective-permute-start(f32[4,16,16,128]{3,2,1,0:T(8,128)S(1)} %shard_map.65.before_ref.own_ref), channel_id=1, source_target_pairs={{32,0},{64,32},{96,64},{128,96},{160,128},{192,160},{224,192},{256... | collective-permute-start | bytes 1572872 | tf_op jit(solution)/shard_map/ppermute | solution.py:227
  92.8 11.4 %collective-permute-start.15 = (f32[4,16,16,128]{3,2,1,0:T(8,128)S(1)}, f32[4,16,16,128]{3,2,1,0:T(8,128)S(1)}, u32[]{:S(2)}, u32[]{:S(2)}) collective-permute-start(f32[4,16,16,128]{3,2,1,0:T(8,128)S(1)} %shard_map.68.own_ref.after_ref), channel_id=1, source_target_pairs={{0,32},{32,64},{64,96},{96,128},{128,160},{160,192},{192,224},{224... | collective-permute-start | bytes 1572872 | tf_op jit(solution)/shard_map/ppermute | solution.py:223
  99.9 11.0 %collective-permute-start.14 = (f32[4,16,16,128]{3,2,1,0:T(8,128)S(1)}, f32[4,16,16,128]{3,2,1,0:T(8,128)S(1)}, u32[]{:S(2)}, u32[]{:S(2)}) collective-permute-start(f32[4,16,16,128]{3,2,1,0:T(8,128)S(1)} %shard_map.69.after_ref.own_ref), channel_id=1, source_target_pairs={{0,32},{32,64},{64,96},{96,128},{128,160},{160,192},{192,224},{224... | collective-permute-start | bytes 1572872 | tf_op jit(solution)/shard_map/ppermute | solution.py:223
  105.2 14.2 %collective-permute-start.18 = (f32[4,16,16,128]{3,2,1,0:T(8,128)S(1)}, f32[4,16,16,128]{3,2,1,0:T(8,128)S(1)}, u32[]{:S(2)}, u32[]{:S(2)}) collective-permute-start(f32[4,16,16,128]{3,2,1,0:T(8,128)S(1)} %shard_map.70.own_ref.before_ref), channel_id=1, source_target_pairs={{32,0},{64,32},{96,64},{128,96},{160,128},{192,160},{224,192},{256... | collective-permute-start | bytes 1572872 | tf_op jit(solution)/shard_map/ppermute | solution.py:227
  111.5 18.9 %collective-permute-start.16 = (f32[4,16,16,128]{3,2,1,0:T(8,128)S(1)}, f32[4,16,16,128]{3,2,1,0:T(8,128)S(1)}, u32[]{:S(2)}, u32[]{:S(2)}) collective-permute-start(f32[4,16,16,128]{3,2,1,0:T(8,128)S(1)} %shard_map.71.own_ref), channel_id=1, source_target_pairs={{0,1},{1,2},{2,3},{3,4},{4,5},{5,6},{6,7},{7,8},{8,9},{9,10},{10,1... | collective-permute-start | bytes 1572872 | tf_op jit(solution)/shard_map/ppermute | solution.py:223
  113.9 17.9 %collective-permute-start.17 = (f32[4,16,16,128]{3,2,1,0:T(8,128)S(1)}, f32[4,16,16,128]{3,2,1,0:T(8,128)S(1)}, u32[]{:S(2)}, u32[]{:S(2)}) collective-permute-start(f32[4,16,16,128]{3,2,1,0:T(8,128)S(1)} %shard_map.71.own_ref), channel_id=1, source_target_pairs={{1,0},{2,1},{3,2},{4,3},{5,4},{6,5},{7,6},{8,7},{9,8},{10,9},{11,1... | collective-permute-start | bytes 1572872 | tf_op jit(solution)/shard_map/ppermute | solution.py:227
  120.1 19.9 %collective-permute-start.19 = (f32[4,16,16,128]{3,2,1,0:T(8,128)S(1)}, f32[4,16,16,128]{3,2,1,0:T(8,128)S(1)}, u32[]{:S(2)}, u32[]{:S(2)}) collective-permute-start(f32[4,16,16,128]{3,2,1,0:T(8,128)S(1)} %shard_map.73.own_ref), channel_id=1, source_target_pairs={{0,1},{1,2},{2,3},{3,4},{4,5},{5,6},{6,7},{7,8},{8,9},{9,10},{10,1... | collective-permute-start | bytes 1572872 | tf_op jit(solution)/shard_map/ppermute | solution.py:223
  122.0 19.2 %collective-permute-start.20 = (f32[4,16,16,128]{3,2,1,0:T(8,128)S(1)}, f32[4,16,16,128]{3,2,1,0:T(8,128)S(1)}, u32[]{:S(2)}, u32[]{:S(2)}) collective-permute-start(f32[4,16,16,128]{3,2,1,0:T(8,128)S(1)} %shard_map.73.own_ref), channel_id=1, source_target_pairs={{1,0},{2,1},{3,2},{4,3},{5,4},{6,5},{7,6},{8,7},{9,8},{10,9},{11,1... | collective-permute-start | bytes 1572872 | tf_op jit(solution)/shard_map/ppermute | solution.py:227

commit v8 on v7

--- a/solution.py
+++ b/solution.py
@@ -90,9 +90,8 @@
 
 def store_z(matrix, out_ref):
     high, low = split(matrix)
-    for k in (0, LANES):
-        out_ref[k : k + LANES, :LANES] = high
-        out_ref[k : k + LANES, LANES:] = low
+    out_ref[:, :LANES] = high
+    out_ref[:, LANES:] = low
 
 
 def forward_matrices_kernel(packed_ref, x_ref, y_ref, z_ref):
@@ -141,7 +140,8 @@
 
 def blur_z(value, matrix):
     high, low = split(value)
-    product = jnp.dot(jnp.concatenate([high, low], axis=1), matrix, preferred_element_type=jnp.float32)
+    twice = jnp.concatenate([matrix, matrix], axis=0)
+    product = jnp.dot(jnp.concatenate([high, low], axis=1), twice, preferred_element_type=jnp.float32)
     return product[:, :LANES] + product[:, LANES:]
 
 
@@ -249,7 +249,7 @@
     y = ("gy", "view")
     half_shape = ((views, half, width, depth), f32)
     bands_shape = ((views, HALF, 9 * HALF), jnp.bfloat16)
-    matrix_shape = ((views, 2 * LANES, 2 * LANES), jnp.bfloat16)
+    matrix_shape = ((views, LANES, 2 * LANES), jnp.bfloat16)
     part = ((half, width, depth), f32)
 
     own = call(part_kernel, [((rows, width, depth), f32)], [], v_word, estimate)[0]

time: 156 us -> 156 us (level)
  the two profiles are of different devices: /device:TPU:22 before, /device:TPU:18 now
where the time goes in v8:
time: 156 us
  starting transfers between devices  84.5 us (54%)
  waiting for transfers between devices  43 us (28%)
  Pallas kernels  14.6 us (9%)
  blocking collectives  13.2 us (8%)
    ppermute x10, starting transfers between devices, back(): return lax.ppermute(value, axes, shifted(lax.axis_size(axes), -1))  45.2 us
    ppermute x10, starting transfers between devices, onward(): return lax.ppermute(value, axes, shifted(lax.axis_size(axes), 1))  23.1 us
    ppermute x10, waiting for transfers between devices, onward(): return lax.ppermute(value, axes, shifted(lax.axis_size(axes), 1))  19.8 us
    pallas_call x21, Pallas kernels, call(): pl.pallas_call(kernel, out_shape=[jax.ShapeDtypeStruct(s, d) for s, d in...  14.6 us
    all_to_all x1, blocking collectives, exchanged(): return lax.all_to_all(pieces, 'view', 0, 0, tiled=True)  13.2 us
    ppermute x10, waiting for transfers between devices, back(): return lax.ppermute(value, axes, shifted(lax.axis_size(axes), -1))  11.5 us
    ppermute x1, starting transfers between devices, across(): lax.ppermute(value, ('gy', 'view'), pairs + [(b, a) for a, b in pairs])  8.75 us
    all_to_all x1, starting transfers between devices, exchanged(): return lax.all_to_all(pieces, 'view', 0, 0, tiled=True)  7.4 us
  transfers between devices with their start and end apart: 22, of which 13 were waited for; matrix products, arithmetic and copies ran while one was open for 0% of the time, Pallas kernels for 6%

profile of v8, /device:TPU:18, one launch (start us, length us, event | category | flops | bytes accessed | tf_op | source)
XLA Modules:
  0.0 155.7 jit_solution(13481581763700650598)
XLA Ops:
  0.0 2.2 %shard_map.57 = f32[4,520,128]{2,1,0:T(8,128)} custom-call(bf16[32,64,128]{2,1,0:T(8,128)(2,1)} %bitcast.4, f32[1,33]{1,0:T(1,128)} %refs_0_.1, f32[1,33]{1,0:T(1,128)} %refs_1_.1, f32[1,33]{1,0:T(1,128)} %refs_2_.1), custom_call_target="tpu_custom_call" | custom-call | tf_op jit(solution)/shard_map/pallas_call | solution.py:21
  2.2 7.4 %all-to-all-start = ((f32[4,520,128]{2,1,0:T(8,128)}), f32[4,520,128]{2,1,0:T(8,128)S(1)}, u32[]{:S(2)}, u32[]{:S(2)}) async-start(f32[4,520,128]{2,1,0:T(8,128)} %shard_map.57), calls=%async_computation | async-start | bytes 2129920 | tf_op jit(solution)/shard_map/all_to_all | solution.py:237
  9.6 8.8 %collective-permute-start = (f32[32,16,128]{2,1,0:T(8,128)S(1)}, f32[32,16,128]{2,1,0:T(8,128)S(1)}, u32[]{:S(2)}, u32[]{:S(2)}) collective-permute-start(f32[32,16,128]{2,1,0:T(8,128)S(1)} %shard_map.55.estimate_ref), channel_id=1, source_target_pairs={{3,4},{7,8},{11,12},{15,16},{19,20},{23,24},{27,28},{4,3},{8,7},{1... | collective-permute-start | bytes 786440 | tf_op jit(solution)/shard_map/ppermute | solution.py:233
  18.4 5.7 %collective-permute-done.across_ref = f32[32,16,128]{2,1,0:T(8,128)S(1)} collective-permute-done((f32[32,16,128]{2,1,0:T(8,128)S(1)}, f32[32,16,128]{2,1,0:T(8,128)S(1)}, u32[]{:S(2)}, u32[]{:S(2)}) %collective-permute-start) | collective-permute-done | bytes 262176 | tf_op jit(solution)/shard_map/ppermute | solution.py:233
  26.1 3.6 %collective-permute-start.2 = (f32[16,48,128]{2,1,0:T(8,128)S(1)}, f32[16,48,128]{2,1,0:T(8,128)S(1)}, u32[]{:S(2)}, u32[]{:S(2)}) collective-permute-start(f32[16,48,128]{2,1,0:T(8,128)S(1)} %get-tuple-element.18.refs_1_), channel_id=1, source_target_pairs={{32,0},{64,32},{96,64},{128,96},{160,128},{192,160},{224,192},{256... | collective-permute-start | bytes 1179656 | tf_op jit(solution)/shard_map/ppermute | solution.py:227
  29.8 5.9 %all-to-all-done.packed_ref.data_ref = f32[4,520,128]{2,1,0:T(8,128)S(1)} async-done(((f32[4,520,128]{2,1,0:T(8,128)}), f32[4,520,128]{2,1,0:T(8,128)S(1)}, u32[]{:S(2)}, u32[]{:S(2)}) %all-to-all-start) | async-done | bytes 1064992 | tf_op jit(solution)/shard_map/all_to_all | solution.py:237
  37.8 2.4 %collective-permute-start.3 = (f32[4,16,16,128]{3,2,1,0:T(8,128)S(1)}, f32[4,16,16,128]{3,2,1,0:T(8,128)S(1)}, u32[]{:S(2)}, u32[]{:S(2)}) collective-permute-start(f32[4,16,16,128]{3,2,1,0:T(8,128)S(1)} %shard_map.60.after_ref.own_ref), channel_id=1, source_target_pairs={{0,32},{32,64},{64,96},{96,128},{128,160},{160,192},{192,224},{224... | collective-permute-start | bytes 1572872 | tf_op jit(solution)/shard_map/ppermute | solution.py:223
  41.2 3.2 %collective-permute-start.8 = (f32[4,16,16,128]{3,2,1,0:T(8,128)S(1)}, f32[4,16,16,128]{3,2,1,0:T(8,128)S(1)}, u32[]{:S(2)}, u32[]{:S(2)}) collective-permute-start(f32[4,16,16,128]{3,2,1,0:T(8,128)S(1)} %shard_map.61.own_ref.before_ref), channel_id=1, source_target_pairs={{32,0},{64,32},{96,64},{128,96},{160,128},{192,160},{224,192},{256... | collective-permute-start | bytes 1572872 | tf_op jit(solution)/shard_map/ppermute | solution.py:227
  44.8 3.6 %collective-permute-done.3.before_ref = f32[4,16,16,128]{3,2,1,0:T(8,128)S(1)} collective-permute-done((f32[4,16,16,128]{3,2,1,0:T(8,128)S(1)}, f32[4,16,16,128]{3,2,1,0:T(8,128)S(1)}, u32[]{:S(2)}, u32[]{:S(2)}) %collective-permute-start.3) | collective-permute-done | bytes 524320 | tf_op jit(solution)/shard_map/ppermute | solution.py:223
  50.9 6.4 %collective-permute-start.5 = (f32[4,16,16,128]{3,2,1,0:T(8,128)S(1)}, f32[4,16,16,128]{3,2,1,0:T(8,128)S(1)}, u32[]{:S(2)}, u32[]{:S(2)}) collective-permute-start(f32[4,16,16,128]{3,2,1,0:T(8,128)S(1)} %shard_map.63.own_ref), channel_id=1, source_target_pairs={{1,0},{2,1},{3,2},{4,3},{5,4},{6,5},{7,6},{8,7},{9,8},{10,9},{11,1... | collective-permute-start | bytes 1572872 | tf_op jit(solution)/shard_map/ppermute | solution.py:227
  57.9 3.9 %collective-permute-start.10 = (f32[4,16,16,128]{3,2,1,0:T(8,128)S(1)}, f32[4,16,16,128]{3,2,1,0:T(8,128)S(1)}, u32[]{:S(2)}, u32[]{:S(2)}) collective-permute-start(f32[4,16,16,128]{3,2,1,0:T(8,128)S(1)} %shard_map.66.own_ref), channel_id=1, source_target_pairs={{1,0},{2,1},{3,2},{4,3},{5,4},{6,5},{7,6},{8,7},{9,8},{10,9},{11,1... | collective-permute-start | bytes 1572872 | tf_op jit(solution)/shard_map/ppermute | solution.py:227
  63.8 2.8 %collective-permute-done.4.before_ref = f32[4,16,16,128]{3,2,1,0:T(8,128)S(1)} collective-permute-done((f32[4,16,16,128]{3,2,1,0:T(8,128)S(1)}, f32[4,16,16,128]{3,2,1,0:T(8,128)S(1)}, u32[]{:S(2)}, u32[]{:S(2)}) %collective-permute-start.4) | collective-permute-done | bytes 524320 | tf_op jit(solution)/shard_map/ppermute | solution.py:223
  66.7 3.0 %collective-permute-done.5.after_ref = f32[4,16,16,128]{3,2,1,0:T(8,128)S(1)} collective-permute-done((f32[4,16,16,128]{3,2,1,0:T(8,128)S(1)}, f32[4,16,16,128]{3,2,1,0:T(8,128)S(1)}, u32[]{:S(2)}, u32[]{:S(2)}) %collective-permute-start.5) | collective-permute-done | bytes 524320 | tf_op jit(solution)/shard_map/ppermute | solution.py:227
  72.4 6.5 %collective-permute-start.7 = (f32[16,16,128]{2,1,0:T(8,128)S(1)}, f32[16,16,128]{2,1,0:T(8,128)S(1)}, u32[]{:S(2)}, u32[]{:S(2)}) collective-permute-start(f32[16,16,128]{2,1,0:T(8,128)S(1)} %shard_map.64.own_ref.estimate_ref), channel_id=1, source_target_pairs={{1,0},{2,1},{3,2},{4,3},{5,4},{6,5},{7,6},{8,7},{9,8},{10,9},{11,1... | collective-permute-start | bytes 393224 | tf_op jit(solution)/shard_map/ppermute | solution.py:227
  83.2 6.5 %collective-permute-start.12 = (f32[16,16,128]{2,1,0:T(8,128)S(1)}, f32[16,16,128]{2,1,0:T(8,128)S(1)}, u32[]{:S(2)}, u32[]{:S(2)}) collective-permute-start(f32[16,16,128]{2,1,0:T(8,128)S(1)} %shard_map.67.own_ref.estimate_ref), channel_id=1, source_target_pairs={{1,0},{2,1},{3,2},{4,3},{5,4},{6,5},{7,6},{8,7},{9,8},{10,9},{11,1... | collective-permute-start | bytes 393224 | tf_op jit(solution)/shard_map/ppermute | solution.py:227
  94.6 4.0 %collective-permute-done.13.after_ref = f32[4,16,16,128]{3,2,1,0:T(8,128)S(1)} collective-permute-done((f32[4,16,16,128]{3,2,1,0:T(8,128)S(1)}, f32[4,16,16,128]{3,2,1,0:T(8,128)S(1)}, u32[]{:S(2)}, u32[]{:S(2)}) %collective-permute-start.13) | collective-permute-done | bytes 524320 | tf_op jit(solution)/shard_map/ppermute | solution.py:227
  99.6 4.3 %collective-permute-start.14 = (f32[4,16,16,128]{3,2,1,0:T(8,128)S(1)}, f32[4,16,16,128]{3,2,1,0:T(8,128)S(1)}, u32[]{:S(2)}, u32[]{:S(2)}) collective-permute-start(f32[4,16,16,128]{3,2,1,0:T(8,128)S(1)} %shard_map.69.after_ref.own_ref), channel_id=1, source_target_pairs={{0,32},{32,64},{64,96},{96,128},{128,160},{160,192},{192,224},{224... | collective-permute-start | bytes 1572872 | tf_op jit(solution)/shard_map/ppermute | solution.py:223
  106.8 3.7 %collective-permute-done.14.before_ref = f32[4,16,16,128]{3,2,1,0:T(8,128)S(1)} collective-permute-done((f32[4,16,16,128]{3,2,1,0:T(8,128)S(1)}, f32[4,16,16,128]{3,2,1,0:T(8,128)S(1)}, u32[]{:S(2)}, u32[]{:S(2)}) %collective-permute-start.14) | collective-permute-done | bytes 524320 | tf_op jit(solution)/shard_map/ppermute | solution.py:223
  111.2 2.7 %collective-permute-start.16 = (f32[4,16,16,128]{3,2,1,0:T(8,128)S(1)}, f32[4,16,16,128]{3,2,1,0:T(8,128)S(1)}, u32[]{:S(2)}, u32[]{:S(2)}) collective-permute-start(f32[4,16,16,128]{3,2,1,0:T(8,128)S(1)} %shard_map.71.own_ref), channel_id=1, source_target_pairs={{0,1},{1,2},{2,3},{3,4},{4,5},{5,6},{6,7},{7,8},{8,9},{9,10},{10,1... | collective-permute-start | bytes 1572872 | tf_op jit(solution)/shard_map/ppermute | solution.py:223
  113.9 5.2 %collective-permute-start.17 = (f32[4,16,16,128]{3,2,1,0:T(8,128)S(1)}, f32[4,16,16,128]{3,2,1,0:T(8,128)S(1)}, u32[]{:S(2)}, u32[]{:S(2)}) collective-permute-start(f32[4,16,16,128]{3,2,1,0:T(8,128)S(1)} %shard_map.71.own_ref), channel_id=1, source_target_pairs={{1,0},{2,1},{3,2},{4,3},{5,4},{6,5},{7,6},{8,7},{9,8},{10,9},{11,1... | collective-permute-start | bytes 1572872 | tf_op jit(solution)/shard_map/ppermute | solution.py:227
  121.7 6.0 %collective-permute-start.20 = (f32[4,16,16,128]{3,2,1,0:T(8,128)S(1)}, f32[4,16,16,128]{3,2,1,0:T(8,128)S(1)}, u32[]{:S(2)}, u32[]{:S(2)}) collective-permute-start(f32[4,16,16,128]{3,2,1,0:T(8,128)S(1)} %shard_map.73.own_ref), channel_id=1, source_target_pairs={{1,0},{2,1},{3,2},{4,3},{5,4},{6,5},{7,6},{8,7},{9,8},{10,9},{11,1... | collective-permute-start | bytes 1572872 | tf_op jit(solution)/shard_map/ppermute | solution.py:227
  127.8 2.3 %collective-permute-done.16.before_ref = f32[4,16,16,128]{3,2,1,0:T(8,128)S(1)} collective-permute-done((f32[4,16,16,128]{3,2,1,0:T(8,128)S(1)}, f32[4,16,16,128]{3,2,1,0:T(8,128)S(1)}, u32[]{:S(2)}, u32[]{:S(2)}) %collective-permute-start.16) | collective-permute-done | bytes 524320 | tf_op jit(solution)/shard_map/ppermute | solution.py:223
  132.3 7.4 %collective-permute-done.19.before_ref = f32[4,16,16,128]{3,2,1,0:T(8,128)S(1)} collective-permute-done((f32[4,16,16,128]{3,2,1,0:T(8,128)S(1)}, f32[4,16,16,128]{3,2,1,0:T(8,128)S(1)}, u32[]{:S(2)}, u32[]{:S(2)}) %collective-permute-start.19) | collective-permute-done | bytes 524320 | tf_op jit(solution)/shard_map/ppermute | solution.py:223
  141.8 13.2 %all_to_all.10.pieces_ref = f32[4,8,16,128]{3,2,1,0:T(8,128)S(1)} all-to-all(f32[4,8,16,128]{3,2,1,0:T(8,128)S(1)} %bitcast.3), channel_id=1, replica_groups=mesh['gx'=16,'gy'=8,'view'=4] {'view'}, dimensions={0} | all-to-all | bytes 524288 | tf_op jit(solution)/shard_map/all_to_all | solution.py:237
  (45 shorter events, 34.5 us)
Async XLA Ops:
  2.2 7.4 %copy-start = (f32[32,64,128]{2,1,0:T(8,128)S(1)}, f32[32,64,128]{2,1,0:T(8,128)}, u32[]{:S(2)}) copy-start(f32[32,64,128]{2,1,0:T(8,128)} %tile_ref.3) | copy-start | bytes 3145732
  2.2 33.5 %all-to-all-start = ((f32[4,520,128]{2,1,0:T(8,128)}), f32[4,520,128]{2,1,0:T(8,128)S(1)}, u32[]{:S(2)}, u32[]{:S(2)}) async-start(f32[4,520,128]{2,1,0:T(8,128)} %shard_map.57), calls=%async_computation | async-start | bytes 2129920 | tf_op jit(solution)/shard_map/all_to_all | solution.py:237
  9.6 14.5 %collective-permute-start = (f32[32,16,128]{2,1,0:T(8,128)S(1)}, f32[32,16,128]{2,1,0:T(8,128)S(1)}, u32[]{:S(2)}, u32[]{:S(2)}) collective-permute-start(f32[32,16,128]{2,1,0:T(8,128)S(1)} %shard_map.55.estimate_ref), channel_id=1, source_target_pairs={{3,4},{7,8},{11,12},{15,16},{19,20},{23,24},{27,28},{4,3},{8,7},{1... | collective-permute-start | bytes 786440 | tf_op jit(solution)/shard_map/ppermute | solution.py:233
  24.2 12.2 %collective-permute-start.1 = (f32[16,48,128]{2,1,0:T(8,128)S(1)}, f32[16,48,128]{2,1,0:T(8,128)S(1)}, u32[]{:S(2)}, u32[]{:S(2)}) collective-permute-start(f32[16,48,128]{2,1,0:T(8,128)S(1)} %get-tuple-element.17.refs_2_), channel_id=1, source_target_pairs={{0,32},{32,64},{64,96},{96,128},{128,160},{160,192},{192,224},{224... | collective-permute-start | bytes 1179656 | tf_op jit(solution)/shard_map/ppermute | solution.py:223
  26.1 10.3 %collective-permute-start.2 = (f32[16,48,128]{2,1,0:T(8,128)S(1)}, f32[16,48,128]{2,1,0:T(8,128)S(1)}, u32[]{:S(2)}, u32[]{:S(2)}) collective-permute-start(f32[16,48,128]{2,1,0:T(8,128)S(1)} %get-tuple-element.18.refs_1_), channel_id=1, source_target_pairs={{32,0},{64,32},{96,64},{128,96},{160,128},{192,160},{224,192},{256... | collective-permute-start | bytes 1179656 | tf_op jit(solution)/shard_map/ppermute | solution.py:227
  37.8 10.5 %collective-permute-start.3 = (f32[4,16,16,128]{3,2,1,0:T(8,128)S(1)}, f32[4,16,16,128]{3,2,1,0:T(8,128)S(1)}, u32[]{:S(2)}, u32[]{:S(2)}) collective-permute-start(f32[4,16,16,128]{3,2,1,0:T(8,128)S(1)} %shard_map.60.after_ref.own_ref), channel_id=1, source_target_pairs={{0,32},{32,64},{64,96},{96,128},{128,160},{160,192},{192,224},{224... | collective-permute-start | bytes 1572872 | tf_op jit(solution)/shard_map/ppermute | solution.py:223
  41.2 16.1 %collective-permute-start.8 = (f32[4,16,16,128]{3,2,1,0:T(8,128)S(1)}, f32[4,16,16,128]{3,2,1,0:T(8,128)S(1)}, u32[]{:S(2)}, u32[]{:S(2)}) collective-permute-start(f32[4,16,16,128]{3,2,1,0:T(8,128)S(1)} %shard_map.61.own_ref.before_ref), channel_id=1, source_target_pairs={{32,0},{64,32},{96,64},{128,96},{160,128},{192,160},{224,192},{256... | collective-permute-start | bytes 1572872 | tf_op jit(solution)/shard_map/ppermute | solution.py:227
  49.0 17.7 %collective-permute-start.4 = (f32[4,16,16,128]{3,2,1,0:T(8,128)S(1)}, f32[4,16,16,128]{3,2,1,0:T(8,128)S(1)}, u32[]{:S(2)}, u32[]{:S(2)}) collective-permute-start(f32[4,16,16,128]{3,2,1,0:T(8,128)S(1)} %shard_map.63.own_ref), channel_id=1, source_target_pairs={{0,1},{1,2},{2,3},{3,4},{4,5},{5,6},{6,7},{7,8},{8,9},{9,10},{10,1... | collective-permute-start | bytes 1572872 | tf_op jit(solution)/shard_map/ppermute | solution.py:223
  50.9 18.8 %collective-permute-start.5 = (f32[4,16,16,128]{3,2,1,0:T(8,128)S(1)}, f32[4,16,16,128]{3,2,1,0:T(8,128)S(1)}, u32[]{:S(2)}, u32[]{:S(2)}) collective-permute-start(f32[4,16,16,128]{3,2,1,0:T(8,128)S(1)} %shard_map.63.own_ref), channel_id=1, source_target_pairs={{1,0},{2,1},{3,2},{4,3},{5,4},{6,5},{7,6},{8,7},{9,8},{10,9},{11,1... | collective-permute-start | bytes 1572872 | tf_op jit(solution)/shard_map/ppermute | solution.py:227
  57.9 22.5 %collective-permute-start.10 = (f32[4,16,16,128]{3,2,1,0:T(8,128)S(1)}, f32[4,16,16,128]{3,2,1,0:T(8,128)S(1)}, u32[]{:S(2)}, u32[]{:S(2)}) collective-permute-start(f32[4,16,16,128]{3,2,1,0:T(8,128)S(1)} %shard_map.66.own_ref), channel_id=1, source_target_pairs={{1,0},{2,1},{3,2},{4,3},{5,4},{6,5},{7,6},{8,7},{9,8},{10,9},{11,1... | collective-permute-start | bytes 1572872 | tf_op jit(solution)/shard_map/ppermute | solution.py:227
  61.9 18.6 %collective-permute-start.9 = (f32[4,16,16,128]{3,2,1,0:T(8,128)S(1)}, f32[4,16,16,128]{3,2,1,0:T(8,128)S(1)}, u32[]{:S(2)}, u32[]{:S(2)}) collective-permute-start(f32[4,16,16,128]{3,2,1,0:T(8,128)S(1)} %shard_map.66.own_ref), channel_id=1, source_target_pairs={{0,1},{1,2},{2,3},{3,4},{4,5},{5,6},{6,7},{7,8},{8,9},{9,10},{10,1... | collective-permute-start | bytes 1572872 | tf_op jit(solution)/shard_map/ppermute | solution.py:223
  70.5 19.3 %collective-permute-start.6 = (f32[16,16,128]{2,1,0:T(8,128)S(1)}, f32[16,16,128]{2,1,0:T(8,128)S(1)}, u32[]{:S(2)}, u32[]{:S(2)}) collective-permute-start(f32[16,16,128]{2,1,0:T(8,128)S(1)} %shard_map.64.own_ref.estimate_ref), channel_id=1, source_target_pairs={{0,1},{1,2},{2,3},{3,4},{4,5},{5,6},{6,7},{7,8},{8,9},{9,10},{10,1... | collective-permute-start | bytes 393224 | tf_op jit(solution)/shard_map/ppermute | solution.py:223
  72.4 17.3 %collective-permute-start.7 = (f32[16,16,128]{2,1,0:T(8,128)S(1)}, f32[16,16,128]{2,1,0:T(8,128)S(1)}, u32[]{:S(2)}, u32[]{:S(2)}) collective-permute-start(f32[16,16,128]{2,1,0:T(8,128)S(1)} %shard_map.64.own_ref.estimate_ref), channel_id=1, source_target_pairs={{1,0},{2,1},{3,2},{4,3},{5,4},{6,5},{7,6},{8,7},{9,8},{10,9},{11,1... | collective-permute-start | bytes 393224 | tf_op jit(solution)/shard_map/ppermute | solution.py:227
  81.3 10.6 %collective-permute-start.11 = (f32[16,16,128]{2,1,0:T(8,128)S(1)}, f32[16,16,128]{2,1,0:T(8,128)S(1)}, u32[]{:S(2)}, u32[]{:S(2)}) collective-permute-start(f32[16,16,128]{2,1,0:T(8,128)S(1)} %shard_map.67.own_ref.estimate_ref), channel_id=1, source_target_pairs={{0,1},{1,2},{2,3},{3,4},{4,5},{5,6},{6,7},{7,8},{8,9},{9,10},{10,1... | collective-permute-start | bytes 393224 | tf_op jit(solution)/shard_map/ppermute | solution.py:223
  83.2 9.0 %collective-permute-start.12 = (f32[16,16,128]{2,1,0:T(8,128)S(1)}, f32[16,16,128]{2,1,0:T(8,128)S(1)}, u32[]{:S(2)}, u32[]{:S(2)}) collective-permute-start(f32[16,16,128]{2,1,0:T(8,128)S(1)} %shard_map.67.own_ref.estimate_ref), channel_id=1, source_target_pairs={{1,0},{2,1},{3,2},{4,3},{5,4},{6,5},{7,6},{8,7},{9,8},{10,9},{11,1... | collective-permute-start | bytes 393224 | tf_op jit(solution)/shard_map/ppermute | solution.py:227
  90.0 8.6 %collective-permute-start.13 = (f32[4,16,16,128]{3,2,1,0:T(8,128)S(1)}, f32[4,16,16,128]{3,2,1,0:T(8,128)S(1)}, u32[]{:S(2)}, u32[]{:S(2)}) collective-permute-start(f32[4,16,16,128]{3,2,1,0:T(8,128)S(1)} %shard_map.65.before_ref.own_ref), channel_id=1, source_target_pairs={{32,0},{64,32},{96,64},{128,96},{160,128},{192,160},{224,192},{256... | collective-permute-start | bytes 1572872 | tf_op jit(solution)/shard_map/ppermute | solution.py:227
  92.5 11.4 %collective-permute-start.15 = (f32[4,16,16,128]{3,2,1,0:T(8,128)S(1)}, f32[4,16,16,128]{3,2,1,0:T(8,128)S(1)}, u32[]{:S(2)}, u32[]{:S(2)}) collective-permute-start(f32[4,16,16,128]{3,2,1,0:T(8,128)S(1)} %shard_map.68.own_ref.after_ref), channel_id=1, source_target_pairs={{0,32},{32,64},{64,96},{96,128},{128,160},{160,192},{192,224},{224... | collective-permute-start | bytes 1572872 | tf_op jit(solution)/shard_map/ppermute | solution.py:223
  99.6 11.0 %collective-permute-start.14 = (f32[4,16,16,128]{3,2,1,0:T(8,128)S(1)}, f32[4,16,16,128]{3,2,1,0:T(8,128)S(1)}, u32[]{:S(2)}, u32[]{:S(2)}) collective-permute-start(f32[4,16,16,128]{3,2,1,0:T(8,128)S(1)} %shard_map.69.after_ref.own_ref), channel_id=1, source_target_pairs={{0,32},{32,64},{64,96},{96,128},{128,160},{160,192},{192,224},{224... | collective-permute-start | bytes 1572872 | tf_op jit(solution)/shard_map/ppermute | solution.py:223
  104.9 14.3 %collective-permute-start.18 = (f32[4,16,16,128]{3,2,1,0:T(8,128)S(1)}, f32[4,16,16,128]{3,2,1,0:T(8,128)S(1)}, u32[]{:S(2)}, u32[]{:S(2)}) collective-permute-start(f32[4,16,16,128]{3,2,1,0:T(8,128)S(1)} %shard_map.70.own_ref.before_ref), channel_id=1, source_target_pairs={{32,0},{64,32},{96,64},{128,96},{160,128},{192,160},{224,192},{256... | collective-permute-start | bytes 1572872 | tf_op jit(solution)/shard_map/ppermute | solution.py:227
  111.2 18.9 %collective-permute-start.16 = (f32[4,16,16,128]{3,2,1,0:T(8,128)S(1)}, f32[4,16,16,128]{3,2,1,0:T(8,128)S(1)}, u32[]{:S(2)}, u32[]{:S(2)}) collective-permute-start(f32[4,16,16,128]{3,2,1,0:T(8,128)S(1)} %shard_map.71.own_ref), channel_id=1, source_target_pairs={{0,1},{1,2},{2,3},{3,4},{4,5},{5,6},{6,7},{7,8},{8,9},{9,10},{10,1... | collective-permute-start | bytes 1572872 | tf_op jit(solution)/shard_map/ppermute | solution.py:223
  113.9 17.6 %collective-permute-start.17 = (f32[4,16,16,128]{3,2,1,0:T(8,128)S(1)}, f32[4,16,16,128]{3,2,1,0:T(8,128)S(1)}, u32[]{:S(2)}, u32[]{:S(2)}) collective-permute-start(f32[4,16,16,128]{3,2,1,0:T(8,128)S(1)} %shard_map.71.own_ref), channel_id=1, source_target_pairs={{1,0},{2,1},{3,2},{4,3},{5,4},{6,5},{7,6},{8,7},{9,8},{10,9},{11,1... | collective-permute-start | bytes 1572872 | tf_op jit(solution)/shard_map/ppermute | solution.py:227
  119.8 19.9 %collective-permute-start.19 = (f32[4,16,16,128]{3,2,1,0:T(8,128)S(1)}, f32[4,16,16,128]{3,2,1,0:T(8,128)S(1)}, u32[]{:S(2)}, u32[]{:S(2)}) collective-permute-start(f32[4,16,16,128]{3,2,1,0:T(8,128)S(1)} %shard_map.73.own_ref), channel_id=1, source_target_pairs={{0,1},{1,2},{2,3},{3,4},{4,5},{5,6},{6,7},{7,8},{8,9},{9,10},{10,1... | collective-permute-start | bytes 1572872 | tf_op jit(solution)/shard_map/ppermute | solution.py:223
  121.7 19.2 %collective-permute-start.20 = (f32[4,16,16,128]{3,2,1,0:T(8,128)S(1)}, f32[4,16,16,128]{3,2,1,0:T(8,128)S(1)}, u32[]{:S(2)}, u32[]{:S(2)}) collective-permute-start(f32[4,16,16,128]{3,2,1,0:T(8,128)S(1)} %shard_map.73.own_ref), channel_id=1, source_target_pairs={{1,0},{2,1},{3,2},{4,3},{5,4},{6,5},{7,6},{8,7},{9,8},{10,9},{11,1... | collective-permute-start | bytes 1572872 | tf_op jit(solution)/shard_map/ppermute | solution.py:227

commit v9 on v8

--- a/solution.py
+++ b/solution.py
@@ -201,11 +201,11 @@
 
 def update_kernel(first, before_ref, own_ref, after_ref, bands_ref, matrix_ref, estimate_ref, out_ref):
     views, rows, width, _ = own_ref.shape
-    total = None
+    backs = []
     for view in range(views):
         blurred = banded(bands_ref[view], [beside(ref.at[view], rows) for ref in (before_ref, own_ref, after_ref)])
-        terms = jnp.log(blur_z(stacked(blurred), matrix_ref[view]))
-        total = terms if total is None else total + terms
+        backs.append(blur_z(stacked(blurred), matrix_ref[view]))
+    total = sum(jnp.log(backs[n] * backs[n + 1]) for n in range(0, views, 2))
     out_ref[...] = estimate_ref[pl.ds(first, rows)] * jnp.exp(total / views).reshape(rows, width, LANES)
 
 

time: 156 us -> 156 us (level)
  the two profiles are of different devices: /device:TPU:18 before, /device:TPU:16 now
where the time goes in v9:
time: 156 us
  waiting for transfers between devices  68.8 us (44%)
  starting transfers between devices  58.4 us (37%)
  Pallas kernels  14.6 us (9%)
  blocking collectives  13.5 us (9%)
    ppermute x10, starting transfers between devices, onward(): return lax.ppermute(value, axes, shifted(lax.axis_size(axes), 1))  31.4 us
    ppermute x10, waiting for transfers between devices, back(): return lax.ppermute(value, axes, shifted(lax.axis_size(axes), -1))  26 us
    ppermute x10, waiting for transfers between devices, onward(): return lax.ppermute(value, axes, shifted(lax.axis_size(axes), 1))  23.1 us
    all_to_all x1, waiting for transfers between devices, exchanged(): return lax.all_to_all(pieces, 'view', 0, 0, tiled=True)  19.7 us
    ppermute x10, starting transfers between devices, back(): return lax.ppermute(value, axes, shifted(lax.axis_size(axes), -1))  18.9 us
    pallas_call x21, Pallas kernels, call(): pl.pallas_call(kernel, out_shape=[jax.ShapeDtypeStruct(s, d) for s, d in...  14.6 us
    all_to_all x1, blocking collectives, exchanged(): return lax.all_to_all(pieces, 'view', 0, 0, tiled=True)  13.5 us
    all_to_all x1, starting transfers between devices, exchanged(): return lax.all_to_all(pieces, 'view', 0, 0, tiled=True)  7.4 us
  transfers between devices with their start and end apart: 22, of which 12 were waited for; matrix products, arithmetic and copies ran while one was open for 0% of the time, Pallas kernels for 6%

profile of v9, /device:TPU:16, one launch (start us, length us, event | category | flops | bytes accessed | tf_op | source)
XLA Modules:
  0.0 155.7 jit_solution(5400808289929133018)
XLA Ops:
  0.0 2.2 %shard_map.57 = f32[4,520,128]{2,1,0:T(8,128)} custom-call(bf16[32,64,128]{2,1,0:T(8,128)(2,1)} %bitcast.4, f32[1,33]{1,0:T(1,128)} %refs_0_.1, f32[1,33]{1,0:T(1,128)} %refs_1_.1, f32[1,33]{1,0:T(1,128)} %refs_2_.1), custom_call_target="tpu_custom_call" | custom-call | tf_op jit(solution)/shard_map/pallas_call | solution.py:21
  2.2 7.4 %all-to-all-start = ((f32[4,520,128]{2,1,0:T(8,128)}), f32[4,520,128]{2,1,0:T(8,128)S(1)}, u32[]{:S(2)}, u32[]{:S(2)}) async-start(f32[4,520,128]{2,1,0:T(8,128)} %shard_map.57), calls=%async_computation | async-start | bytes 2129920 | tf_op jit(solution)/shard_map/all_to_all | solution.py:237
  12.3 3.6 %collective-permute-start.2 = (f32[16,48,128]{2,1,0:T(8,128)S(1)}, f32[16,48,128]{2,1,0:T(8,128)S(1)}, u32[]{:S(2)}, u32[]{:S(2)}) collective-permute-start(f32[16,48,128]{2,1,0:T(8,128)S(1)} %get-tuple-element.18.refs_1_), channel_id=1, source_target_pairs={{32,0},{64,32},{96,64},{128,96},{160,128},{192,160},{224,192},{256... | collective-permute-start | bytes 1179656 | tf_op jit(solution)/shard_map/ppermute | solution.py:227
  16.0 19.7 %all-to-all-done.packed_ref.data_ref = f32[4,520,128]{2,1,0:T(8,128)S(1)} async-done(((f32[4,520,128]{2,1,0:T(8,128)}), f32[4,520,128]{2,1,0:T(8,128)S(1)}, u32[]{:S(2)}, u32[]{:S(2)}) %all-to-all-start) | async-done | bytes 1064992 | tf_op jit(solution)/shard_map/all_to_all | solution.py:237
  40.7 3.6 %collective-permute-start.8 = (f32[4,16,16,128]{3,2,1,0:T(8,128)S(1)}, f32[4,16,16,128]{3,2,1,0:T(8,128)S(1)}, u32[]{:S(2)}, u32[]{:S(2)}) collective-permute-start(f32[4,16,16,128]{3,2,1,0:T(8,128)S(1)} %shard_map.61.own_ref.before_ref), channel_id=1, source_target_pairs={{32,0},{64,32},{96,64},{128,96},{160,128},{192,160},{224,192},{256... | collective-permute-start | bytes 1572872 | tf_op jit(solution)/shard_map/ppermute | solution.py:227
  44.7 3.6 %collective-permute-done.3.before_ref = f32[4,16,16,128]{3,2,1,0:T(8,128)S(1)} collective-permute-done((f32[4,16,16,128]{3,2,1,0:T(8,128)S(1)}, f32[4,16,16,128]{3,2,1,0:T(8,128)S(1)}, u32[]{:S(2)}, u32[]{:S(2)}) %collective-permute-start.3) | collective-permute-done | bytes 524320 | tf_op jit(solution)/shard_map/ppermute | solution.py:223
  53.5 5.2 %collective-permute-start.9 = (f32[4,16,16,128]{3,2,1,0:T(8,128)S(1)}, f32[4,16,16,128]{3,2,1,0:T(8,128)S(1)}, u32[]{:S(2)}, u32[]{:S(2)}) collective-permute-start(f32[4,16,16,128]{3,2,1,0:T(8,128)S(1)} %shard_map.66.own_ref), channel_id=1, source_target_pairs={{0,1},{1,2},{2,3},{3,4},{4,5},{5,6},{6,7},{7,8},{8,9},{9,10},{10,1... | collective-permute-start | bytes 1572872 | tf_op jit(solution)/shard_map/ppermute | solution.py:223
  58.8 3.8 %collective-permute-done.4.before_ref = f32[4,16,16,128]{3,2,1,0:T(8,128)S(1)} collective-permute-done((f32[4,16,16,128]{3,2,1,0:T(8,128)S(1)}, f32[4,16,16,128]{3,2,1,0:T(8,128)S(1)}, u32[]{:S(2)}, u32[]{:S(2)}) %collective-permute-start.4) | collective-permute-done | bytes 524320 | tf_op jit(solution)/shard_map/ppermute | solution.py:223
  62.6 4.4 %collective-permute-done.5.after_ref = f32[4,16,16,128]{3,2,1,0:T(8,128)S(1)} collective-permute-done((f32[4,16,16,128]{3,2,1,0:T(8,128)S(1)}, f32[4,16,16,128]{3,2,1,0:T(8,128)S(1)}, u32[]{:S(2)}, u32[]{:S(2)}) %collective-permute-start.5) | collective-permute-done | bytes 524320 | tf_op jit(solution)/shard_map/ppermute | solution.py:227
  67.9 3.1 %collective-permute-start.6 = (f32[16,16,128]{2,1,0:T(8,128)S(1)}, f32[16,16,128]{2,1,0:T(8,128)S(1)}, u32[]{:S(2)}, u32[]{:S(2)}) collective-permute-start(f32[16,16,128]{2,1,0:T(8,128)S(1)} %shard_map.64.own_ref.estimate_ref), channel_id=1, source_target_pairs={{0,1},{1,2},{2,3},{3,4},{4,5},{5,6},{6,7},{7,8},{8,9},{9,10},{10,1... | collective-permute-start | bytes 393224 | tf_op jit(solution)/shard_map/ppermute | solution.py:223
  72.3 5.3 %collective-permute-done.10.after_ref = f32[4,16,16,128]{3,2,1,0:T(8,128)S(1)} collective-permute-done((f32[4,16,16,128]{3,2,1,0:T(8,128)S(1)}, f32[4,16,16,128]{3,2,1,0:T(8,128)S(1)}, u32[]{:S(2)}, u32[]{:S(2)}) %collective-permute-start.10) | collective-permute-done | bytes 524320 | tf_op jit(solution)/shard_map/ppermute | solution.py:227
  78.4 2.7 %collective-permute-start.11 = (f32[16,16,128]{2,1,0:T(8,128)S(1)}, f32[16,16,128]{2,1,0:T(8,128)S(1)}, u32[]{:S(2)}, u32[]{:S(2)}) collective-permute-start(f32[16,16,128]{2,1,0:T(8,128)S(1)} %shard_map.67.own_ref.estimate_ref), channel_id=1, source_target_pairs={{0,1},{1,2},{2,3},{3,4},{4,5},{5,6},{6,7},{7,8},{8,9},{9,10},{10,1... | collective-permute-start | bytes 393224 | tf_op jit(solution)/shard_map/ppermute | solution.py:223
  84.6 7.5 %collective-permute-done.12.after_ref = f32[16,16,128]{2,1,0:T(8,128)S(1)} collective-permute-done((f32[16,16,128]{2,1,0:T(8,128)S(1)}, f32[16,16,128]{2,1,0:T(8,128)S(1)}, u32[]{:S(2)}, u32[]{:S(2)}) %collective-permute-start.12) | collective-permute-done | bytes 131104 | tf_op jit(solution)/shard_map/ppermute | solution.py:227
  95.2 3.9 %collective-permute-start.14 = (f32[4,16,16,128]{3,2,1,0:T(8,128)S(1)}, f32[4,16,16,128]{3,2,1,0:T(8,128)S(1)}, u32[]{:S(2)}, u32[]{:S(2)}) collective-permute-start(f32[4,16,16,128]{3,2,1,0:T(8,128)S(1)} %shard_map.69.after_ref.own_ref), channel_id=1, source_target_pairs={{0,32},{32,64},{64,96},{96,128},{128,160},{160,192},{192,224},{224... | collective-permute-start | bytes 1572872 | tf_op jit(solution)/shard_map/ppermute | solution.py:223
  99.1 3.7 %collective-permute-done.15.before_ref = f32[4,16,16,128]{3,2,1,0:T(8,128)S(1)} collective-permute-done((f32[4,16,16,128]{3,2,1,0:T(8,128)S(1)}, f32[4,16,16,128]{3,2,1,0:T(8,128)S(1)}, u32[]{:S(2)}, u32[]{:S(2)}) %collective-permute-start.15) | collective-permute-done | bytes 524320 | tf_op jit(solution)/shard_map/ppermute | solution.py:223
  103.7 1.9 %collective-permute-start.18 = (f32[4,16,16,128]{3,2,1,0:T(8,128)S(1)}, f32[4,16,16,128]{3,2,1,0:T(8,128)S(1)}, u32[]{:S(2)}, u32[]{:S(2)}) collective-permute-start(f32[4,16,16,128]{3,2,1,0:T(8,128)S(1)} %shard_map.70.own_ref.before_ref), channel_id=1, source_target_pairs={{32,0},{64,32},{96,64},{128,96},{160,128},{192,160},{224,192},{256... | collective-permute-start | bytes 1572872 | tf_op jit(solution)/shard_map/ppermute | solution.py:227
  105.7 2.7 %collective-permute-done.14.before_ref = f32[4,16,16,128]{3,2,1,0:T(8,128)S(1)} collective-permute-done((f32[4,16,16,128]{3,2,1,0:T(8,128)S(1)}, f32[4,16,16,128]{3,2,1,0:T(8,128)S(1)}, u32[]{:S(2)}, u32[]{:S(2)}) %collective-permute-start.14) | collective-permute-done | bytes 524320 | tf_op jit(solution)/shard_map/ppermute | solution.py:223
  109.0 4.9 %collective-permute-start.16 = (f32[4,16,16,128]{3,2,1,0:T(8,128)S(1)}, f32[4,16,16,128]{3,2,1,0:T(8,128)S(1)}, u32[]{:S(2)}, u32[]{:S(2)}) collective-permute-start(f32[4,16,16,128]{3,2,1,0:T(8,128)S(1)} %shard_map.71.own_ref), channel_id=1, source_target_pairs={{0,1},{1,2},{2,3},{3,4},{4,5},{5,6},{6,7},{7,8},{8,9},{9,10},{10,1... | collective-permute-start | bytes 1572872 | tf_op jit(solution)/shard_map/ppermute | solution.py:223
  115.9 4.6 %collective-permute-start.19 = (f32[4,16,16,128]{3,2,1,0:T(8,128)S(1)}, f32[4,16,16,128]{3,2,1,0:T(8,128)S(1)}, u32[]{:S(2)}, u32[]{:S(2)}) collective-permute-start(f32[4,16,16,128]{3,2,1,0:T(8,128)S(1)} %shard_map.73.own_ref), channel_id=1, source_target_pairs={{0,1},{1,2},{2,3},{3,4},{4,5},{5,6},{6,7},{7,8},{8,9},{9,10},{10,1... | collective-permute-start | bytes 1572872 | tf_op jit(solution)/shard_map/ppermute | solution.py:223
  121.8 4.4 %collective-permute-done.16.before_ref = f32[4,16,16,128]{3,2,1,0:T(8,128)S(1)} collective-permute-done((f32[4,16,16,128]{3,2,1,0:T(8,128)S(1)}, f32[4,16,16,128]{3,2,1,0:T(8,128)S(1)}, u32[]{:S(2)}, u32[]{:S(2)}) %collective-permute-start.16) | collective-permute-done | bytes 524320 | tf_op jit(solution)/shard_map/ppermute | solution.py:223
  126.2 4.4 %collective-permute-done.17.after_ref = f32[4,16,16,128]{3,2,1,0:T(8,128)S(1)} collective-permute-done((f32[4,16,16,128]{3,2,1,0:T(8,128)S(1)}, f32[4,16,16,128]{3,2,1,0:T(8,128)S(1)}, u32[]{:S(2)}, u32[]{:S(2)}) %collective-permute-start.17) | collective-permute-done | bytes 524320 | tf_op jit(solution)/shard_map/ppermute | solution.py:227
  131.5 4.8 %collective-permute-done.19.before_ref = f32[4,16,16,128]{3,2,1,0:T(8,128)S(1)} collective-permute-done((f32[4,16,16,128]{3,2,1,0:T(8,128)S(1)}, f32[4,16,16,128]{3,2,1,0:T(8,128)S(1)}, u32[]{:S(2)}, u32[]{:S(2)}) %collective-permute-start.19) | collective-permute-done | bytes 524320 | tf_op jit(solution)/shard_map/ppermute | solution.py:223
  136.3 4.4 %collective-permute-done.20.after_ref = f32[4,16,16,128]{3,2,1,0:T(8,128)S(1)} collective-permute-done((f32[4,16,16,128]{3,2,1,0:T(8,128)S(1)}, f32[4,16,16,128]{3,2,1,0:T(8,128)S(1)}, u32[]{:S(2)}, u32[]{:S(2)}) %collective-permute-start.20) | collective-permute-done | bytes 524320 | tf_op jit(solution)/shard_map/ppermute | solution.py:227
  141.5 13.5 %all_to_all.10.pieces_ref = f32[4,8,16,128]{3,2,1,0:T(8,128)S(1)} all-to-all(f32[4,8,16,128]{3,2,1,0:T(8,128)S(1)} %bitcast.3), channel_id=1, replica_groups=mesh['gx'=16,'gy'=8,'view'=4] {'view'}, dimensions={0} | all-to-all | bytes 524288 | tf_op jit(solution)/shard_map/all_to_all | solution.py:237
  (45 shorter events, 30.0 us)
Async XLA Ops:
  2.2 7.4 %copy-start = (f32[32,64,128]{2,1,0:T(8,128)S(1)}, f32[32,64,128]{2,1,0:T(8,128)}, u32[]{:S(2)}) copy-start(f32[32,64,128]{2,1,0:T(8,128)} %tile_ref.3) | copy-start | bytes 3145732
  2.2 33.5 %all-to-all-start = ((f32[4,520,128]{2,1,0:T(8,128)}), f32[4,520,128]{2,1,0:T(8,128)S(1)}, u32[]{:S(2)}, u32[]{:S(2)}) async-start(f32[4,520,128]{2,1,0:T(8,128)} %shard_map.57), calls=%async_computation | async-start | bytes 2129920 | tf_op jit(solution)/shard_map/all_to_all | solution.py:237
  9.6 0.7 collective-permute-start
  10.4 26.0 %collective-permute-start.1 = (f32[16,48,128]{2,1,0:T(8,128)S(1)}, f32[16,48,128]{2,1,0:T(8,128)S(1)}, u32[]{:S(2)}, u32[]{:S(2)}) collective-permute-start(f32[16,48,128]{2,1,0:T(8,128)S(1)} %get-tuple-element.17.refs_2_), channel_id=1, source_target_pairs={{0,32},{32,64},{64,96},{96,128},{128,160},{160,192},{192,224},{224... | collective-permute-start | bytes 1179656 | tf_op jit(solution)/shard_map/ppermute | solution.py:223
  12.3 24.1 %collective-permute-start.2 = (f32[16,48,128]{2,1,0:T(8,128)S(1)}, f32[16,48,128]{2,1,0:T(8,128)S(1)}, u32[]{:S(2)}, u32[]{:S(2)}) collective-permute-start(f32[16,48,128]{2,1,0:T(8,128)S(1)} %get-tuple-element.18.refs_1_), channel_id=1, source_target_pairs={{32,0},{64,32},{96,64},{128,96},{160,128},{192,160},{224,192},{256... | collective-permute-start | bytes 1179656 | tf_op jit(solution)/shard_map/ppermute | solution.py:227
  37.8 10.5 %collective-permute-start.3 = (f32[4,16,16,128]{3,2,1,0:T(8,128)S(1)}, f32[4,16,16,128]{3,2,1,0:T(8,128)S(1)}, u32[]{:S(2)}, u32[]{:S(2)}) collective-permute-start(f32[4,16,16,128]{3,2,1,0:T(8,128)S(1)} %shard_map.60.after_ref.own_ref), channel_id=1, source_target_pairs={{0,32},{32,64},{64,96},{96,128},{128,160},{160,192},{192,224},{224... | collective-permute-start | bytes 1572872 | tf_op jit(solution)/shard_map/ppermute | solution.py:223
  40.7 10.9 %collective-permute-start.8 = (f32[4,16,16,128]{3,2,1,0:T(8,128)S(1)}, f32[4,16,16,128]{3,2,1,0:T(8,128)S(1)}, u32[]{:S(2)}, u32[]{:S(2)}) collective-permute-start(f32[4,16,16,128]{3,2,1,0:T(8,128)S(1)} %shard_map.61.own_ref.before_ref), channel_id=1, source_target_pairs={{32,0},{64,32},{96,64},{128,96},{160,128},{192,160},{224,192},{256... | collective-permute-start | bytes 1572872 | tf_op jit(solution)/shard_map/ppermute | solution.py:227
  49.0 13.7 %collective-permute-start.4 = (f32[4,16,16,128]{3,2,1,0:T(8,128)S(1)}, f32[4,16,16,128]{3,2,1,0:T(8,128)S(1)}, u32[]{:S(2)}, u32[]{:S(2)}) collective-permute-start(f32[4,16,16,128]{3,2,1,0:T(8,128)S(1)} %shard_map.63.own_ref), channel_id=1, source_target_pairs={{0,1},{1,2},{2,3},{3,4},{4,5},{5,6},{6,7},{7,8},{8,9},{9,10},{10,1... | collective-permute-start | bytes 1572872 | tf_op jit(solution)/shard_map/ppermute | solution.py:223
  50.3 16.8 %collective-permute-start.5 = (f32[4,16,16,128]{3,2,1,0:T(8,128)S(1)}, f32[4,16,16,128]{3,2,1,0:T(8,128)S(1)}, u32[]{:S(2)}, u32[]{:S(2)}) collective-permute-start(f32[4,16,16,128]{3,2,1,0:T(8,128)S(1)} %shard_map.63.own_ref), channel_id=1, source_target_pairs={{1,0},{2,1},{3,2},{4,3},{5,4},{6,5},{7,6},{8,7},{9,8},{10,9},{11,1... | collective-permute-start | bytes 1572872 | tf_op jit(solution)/shard_map/ppermute | solution.py:227
  52.2 25.3 %collective-permute-start.10 = (f32[4,16,16,128]{3,2,1,0:T(8,128)S(1)}, f32[4,16,16,128]{3,2,1,0:T(8,128)S(1)}, u32[]{:S(2)}, u32[]{:S(2)}) collective-permute-start(f32[4,16,16,128]{3,2,1,0:T(8,128)S(1)} %shard_map.66.own_ref), channel_id=1, source_target_pairs={{1,0},{2,1},{3,2},{4,3},{5,4},{6,5},{7,6},{8,7},{9,8},{10,9},{11,1... | collective-permute-start | bytes 1572872 | tf_op jit(solution)/shard_map/ppermute | solution.py:227
  53.5 24.0 %collective-permute-start.9 = (f32[4,16,16,128]{3,2,1,0:T(8,128)S(1)}, f32[4,16,16,128]{3,2,1,0:T(8,128)S(1)}, u32[]{:S(2)}, u32[]{:S(2)}) collective-permute-start(f32[4,16,16,128]{3,2,1,0:T(8,128)S(1)} %shard_map.66.own_ref), channel_id=1, source_target_pairs={{0,1},{1,2},{2,3},{3,4},{4,5},{5,6},{6,7},{7,8},{8,9},{9,10},{10,1... | collective-permute-start | bytes 1572872 | tf_op jit(solution)/shard_map/ppermute | solution.py:223
  67.9 14.5 %collective-permute-start.6 = (f32[16,16,128]{2,1,0:T(8,128)S(1)}, f32[16,16,128]{2,1,0:T(8,128)S(1)}, u32[]{:S(2)}, u32[]{:S(2)}) collective-permute-start(f32[16,16,128]{2,1,0:T(8,128)S(1)} %shard_map.64.own_ref.estimate_ref), channel_id=1, source_target_pairs={{0,1},{1,2},{2,3},{3,4},{4,5},{5,6},{6,7},{7,8},{8,9},{9,10},{10,1... | collective-permute-start | bytes 393224 | tf_op jit(solution)/shard_map/ppermute | solution.py:223
  71.0 11.4 %collective-permute-start.7 = (f32[16,16,128]{2,1,0:T(8,128)S(1)}, f32[16,16,128]{2,1,0:T(8,128)S(1)}, u32[]{:S(2)}, u32[]{:S(2)}) collective-permute-start(f32[16,16,128]{2,1,0:T(8,128)S(1)} %shard_map.64.own_ref.estimate_ref), channel_id=1, source_target_pairs={{1,0},{2,1},{3,2},{4,3},{5,4},{6,5},{7,6},{8,7},{9,8},{10,9},{11,1... | collective-permute-start | bytes 393224 | tf_op jit(solution)/shard_map/ppermute | solution.py:227
  78.4 6.2 %collective-permute-start.11 = (f32[16,16,128]{2,1,0:T(8,128)S(1)}, f32[16,16,128]{2,1,0:T(8,128)S(1)}, u32[]{:S(2)}, u32[]{:S(2)}) collective-permute-start(f32[16,16,128]{2,1,0:T(8,128)S(1)} %shard_map.67.own_ref.estimate_ref), channel_id=1, source_target_pairs={{0,1},{1,2},{2,3},{3,4},{4,5},{5,6},{6,7},{7,8},{8,9},{9,10},{10,1... | collective-permute-start | bytes 393224 | tf_op jit(solution)/shard_map/ppermute | solution.py:223
  81.1 11.0 %collective-permute-start.12 = (f32[16,16,128]{2,1,0:T(8,128)S(1)}, f32[16,16,128]{2,1,0:T(8,128)S(1)}, u32[]{:S(2)}, u32[]{:S(2)}) collective-permute-start(f32[16,16,128]{2,1,0:T(8,128)S(1)} %shard_map.67.own_ref.estimate_ref), channel_id=1, source_target_pairs={{1,0},{2,1},{3,2},{4,3},{5,4},{6,5},{7,6},{8,7},{9,8},{10,9},{11,1... | collective-permute-start | bytes 393224 | tf_op jit(solution)/shard_map/ppermute | solution.py:227
  82.6 11.6 %collective-permute-start.13 = (f32[4,16,16,128]{3,2,1,0:T(8,128)S(1)}, f32[4,16,16,128]{3,2,1,0:T(8,128)S(1)}, u32[]{:S(2)}, u32[]{:S(2)}) collective-permute-start(f32[4,16,16,128]{3,2,1,0:T(8,128)S(1)} %shard_map.65.before_ref.own_ref), channel_id=1, source_target_pairs={{32,0},{64,32},{96,64},{128,96},{160,128},{192,160},{224,192},{256... | collective-permute-start | bytes 1572872 | tf_op jit(solution)/shard_map/ppermute | solution.py:227
  92.3 10.5 %collective-permute-start.15 = (f32[4,16,16,128]{3,2,1,0:T(8,128)S(1)}, f32[4,16,16,128]{3,2,1,0:T(8,128)S(1)}, u32[]{:S(2)}, u32[]{:S(2)}) collective-permute-start(f32[4,16,16,128]{3,2,1,0:T(8,128)S(1)} %shard_map.68.own_ref.after_ref), channel_id=1, source_target_pairs={{0,32},{32,64},{64,96},{96,128},{128,160},{160,192},{192,224},{224... | collective-permute-start | bytes 1572872 | tf_op jit(solution)/shard_map/ppermute | solution.py:223
  95.2 13.2 %collective-permute-start.14 = (f32[4,16,16,128]{3,2,1,0:T(8,128)S(1)}, f32[4,16,16,128]{3,2,1,0:T(8,128)S(1)}, u32[]{:S(2)}, u32[]{:S(2)}) collective-permute-start(f32[4,16,16,128]{3,2,1,0:T(8,128)S(1)} %shard_map.69.after_ref.own_ref), channel_id=1, source_target_pairs={{0,32},{32,64},{64,96},{96,128},{128,160},{160,192},{192,224},{224... | collective-permute-start | bytes 1572872 | tf_op jit(solution)/shard_map/ppermute | solution.py:223
  103.7 11.5 %collective-permute-start.18 = (f32[4,16,16,128]{3,2,1,0:T(8,128)S(1)}, f32[4,16,16,128]{3,2,1,0:T(8,128)S(1)}, u32[]{:S(2)}, u32[]{:S(2)}) collective-permute-start(f32[4,16,16,128]{3,2,1,0:T(8,128)S(1)} %shard_map.70.own_ref.before_ref), channel_id=1, source_target_pairs={{32,0},{64,32},{96,64},{128,96},{160,128},{192,160},{224,192},{256... | collective-permute-start | bytes 1572872 | tf_op jit(solution)/shard_map/ppermute | solution.py:227
  109.0 17.2 %collective-permute-start.16 = (f32[4,16,16,128]{3,2,1,0:T(8,128)S(1)}, f32[4,16,16,128]{3,2,1,0:T(8,128)S(1)}, u32[]{:S(2)}, u32[]{:S(2)}) collective-permute-start(f32[4,16,16,128]{3,2,1,0:T(8,128)S(1)} %shard_map.71.own_ref), channel_id=1, source_target_pairs={{0,1},{1,2},{2,3},{3,4},{4,5},{5,6},{6,7},{7,8},{8,9},{9,10},{10,1... | collective-permute-start | bytes 1572872 | tf_op jit(solution)/shard_map/ppermute | solution.py:223
  113.9 16.7 %collective-permute-start.17 = (f32[4,16,16,128]{3,2,1,0:T(8,128)S(1)}, f32[4,16,16,128]{3,2,1,0:T(8,128)S(1)}, u32[]{:S(2)}, u32[]{:S(2)}) collective-permute-start(f32[4,16,16,128]{3,2,1,0:T(8,128)S(1)} %shard_map.71.own_ref), channel_id=1, source_target_pairs={{1,0},{2,1},{3,2},{4,3},{5,4},{6,5},{7,6},{8,7},{9,8},{10,9},{11,1... | collective-permute-start | bytes 1572872 | tf_op jit(solution)/shard_map/ppermute | solution.py:227
  115.9 20.4 %collective-permute-start.19 = (f32[4,16,16,128]{3,2,1,0:T(8,128)S(1)}, f32[4,16,16,128]{3,2,1,0:T(8,128)S(1)}, u32[]{:S(2)}, u32[]{:S(2)}) collective-permute-start(f32[4,16,16,128]{3,2,1,0:T(8,128)S(1)} %shard_map.73.own_ref), channel_id=1, source_target_pairs={{0,1},{1,2},{2,3},{3,4},{4,5},{5,6},{6,7},{7,8},{8,9},{9,10},{10,1... | collective-permute-start | bytes 1572872 | tf_op jit(solution)/shard_map/ppermute | solution.py:223
  120.5 20.2 %collective-permute-start.20 = (f32[4,16,16,128]{3,2,1,0:T(8,128)S(1)}, f32[4,16,16,128]{3,2,1,0:T(8,128)S(1)}, u32[]{:S(2)}, u32[]{:S(2)}) collective-permute-start(f32[4,16,16,128]{3,2,1,0:T(8,128)S(1)} %shard_map.73.own_ref), channel_id=1, source_target_pairs={{1,0},{2,1},{3,2},{4,3},{5,4},{6,5},{7,6},{8,7},{9,8},{10,9},{11,1... | collective-permute-start | bytes 1572872 | tf_op jit(solution)/shard_map/ppermute | solution.py:227
